TPU v7x, 32 devices: a whole 2x2x4 slice. The times are simulated.
32 devices in a mesh: rows: 8 (over z, y), ch: 4 (over x, core).
Axes of the slice: x: 2, y: 2, z: 4, core: 2. Of those that a mesh axis runs over, the one named last changes fastest.
Arguments:
- pixels: bfloat16 [2, 16, 128, 768], P(None, 'rows', None, 'ch'), may hold values from -6 to 6
- row_starts: int32 [2, 16], replicated, may hold values from 0 to 1, as said below
- col_starts: int32 [2, 128], replicated, may hold values from 0 to 1
- log_step: float32 [2, 2, 768], P(None, None, 'ch'), may hold values from -6.9 to -2.3
- log_decay: float32 [2, 2, 768, 64], P(None, None, 'ch'), may hold values from -1 to 1
- frequency: float32 [2, 2, 768, 64], P(None, None, 'ch'), may hold values from 0 to 100
- coef_real: float32 [2, 2, 768, 64], P(None, None, 'ch'), may hold values from -12 to 12
- coef_imag: float32 [2, 2, 768, 64], P(None, None, 'ch'), may hold values from -12 to 12
- skip_gain: float32 [2, 768], P(None, 'ch'), may hold values from -4 to 4
- norm_gain: float32 [2, 768], P(None, 'ch'), may hold values from 0.5 to 1.5
- norm_shift: float32 [2, 768], P(None, 'ch'), may hold values from -3 to 3
- weight_in: bfloat16 [2, 768, 3072], P(None, None, 'ch'), may hold values from -0.21875 to 0.21875
- bias_in: float32 [2, 3072], P(None, 'ch'), may hold values from -3 to 3
- weight_out: bfloat16 [2, 3072, 768], P(None, 'ch'), may hold values from -0.109375 to 0.109375
- bias_out: float32 [2, 768], P(None, 'ch'), may hold values from -3 to 3
- layer_scale: float32 [2, 768], P(None, 'ch'), may hold values from 0.5 to 1.5
- cotangent: bfloat16 [2, 16, 128, 768], P(None, 'rows', None, 'ch'), may hold values from -6 to 6
Outputs:
- activations: bfloat16 [2, 16, 128, 768], P(None, 'rows', None, 'ch')
- pixels_grad: bfloat16 [2, 16, 128, 768], P(None, 'rows', None, 'ch')
- log_step_grad: float32 [2, 2, 768], P(None, None, 'ch')
- log_decay_grad: float32 [2, 2, 768, 64], P(None, None, 'ch')
- frequency_grad: float32 [2, 2, 768, 64], P(None, None, 'ch')
- coef_real_grad: float32 [2, 2, 768, 64], P(None, None, 'ch')
- coef_imag_grad: float32 [2, 2, 768, 64], P(None, None, 'ch')
- skip_gain_grad: float32 [2, 768], P(None, 'ch')
- norm_gain_grad: float32 [2, 768], P(None, 'ch')
- norm_shift_grad: float32 [2, 768], P(None, 'ch')
- weight_in_grad: float32 [2, 768, 3072], P(None, None, 'ch')
- bias_in_grad: float32 [2, 3072], P(None, 'ch')
- weight_out_grad: float32 [2, 3072, 768], P(None, 'ch')
- bias_out_grad: float32 [2, 768], P(None, 'ch')
- layer_scale_grad: float32 [2, 768], P(None, 'ch')
Inputs may be any that keep to these rules, and one draw needn't show every extreme that they name: `row_starts`: entry 0 of every canvas is 1; in one canvas, drawn from the seed, no other entry is 1; every other canvas has at least one more 1.
All inputs are finite; a program needn't handle non-finite values.
Results may differ from a plain program's by a relative error of at most 0.02.
Values may be sent and summed in bfloat16 or wider, within the bound.
No kernel may reach another device: no remote copies, remote signals or barrier semaphores. Data moves between devices by JAX's collectives and lax.ppermute only.
A program may use at most 256 MiB of HBM per device.

v0:
```python
from functools import partial

import jax
import jax.numpy as jnp
from jax import lax
from jax.sharding import PartitionSpec as P

epsilon = 1e-06
group_width = 32
width_forms = ("cij,rjc->ric", "cij,ric->rjc", "bric,brjc->bcij")
height_forms = ("cij,jwc->iwc", "cij,iwc->jwc", "biwc,bjwc->bcij")


def s4_kernel(log_step, log_decay, frequency, coef_real, coef_imag, length):
    step_size = jnp.exp(log_step)[:, None, None]
    places = jnp.arange(length).astype(jnp.float32)[None, None, :]
    fading = jnp.exp(-step_size * jnp.exp(log_decay)[:, :, None] * places)
    turning = step_size * frequency[:, :, None] * places
    waving = coef_real[:, :, None] * jnp.cos(turning) - coef_imag[:, :, None] * jnp.sin(turning)
    return step_size[:, :, 0] * jnp.sum(fading * waving, axis=1)


def toeplitz(kernel):
    channels, length = kernel.shape
    widened = jnp.concatenate(
        [kernel[:, :1], jnp.zeros((channels, length), kernel.dtype), kernel[:, 1:][:, ::-1]], axis=1
    )
    repeated = jnp.tile(widened, (1, length))[:, : length * (2 * length - 1)]
    return repeated.reshape(channels, length, 2 * length - 1)[:, :, :length]


def diagonal_sums(products):
    channels, length = (products.shape[0], products.shape[1])
    turned = products[:, :, ::-1]
    padded = jnp.concatenate(
        [turned, jnp.zeros((channels, length, length), products.dtype)], axis=2
    )
    skewed = padded.reshape(channels, 2 * length * length)[:, : length * (2 * length - 1)]
    skewed = skewed.reshape(channels, length, 2 * length - 1)
    return jnp.sum(skewed[:, :, length - 1 :], axis=1)


def crop_mask(starts):
    labels = jnp.cumsum(starts, axis=1)
    return (labels[:, :, None] == labels[:, None, :]).astype(jnp.float32)


def forward_conv(inputs, kernel, crop_masks, patterns):
    channels = kernel.shape[0]
    stride = min(group_width, channels)
    pieces = []
    for offset in range(0, channels, stride):
        matrix = toeplitz(kernel[offset : offset + stride])
        outputs = []
        for canvas in range(inputs.shape[0]):
            masked = matrix * crop_masks[canvas][None]
            outputs.append(
                jnp.einsum(
                    patterns[0],
                    masked,
                    inputs[canvas, :, :, offset : offset + stride],
                    preferred_element_type=jnp.float32,
                )
            )
        pieces.append(jnp.stack(outputs))
    return jnp.concatenate(pieces, axis=3)


def backward_conv(inputs, upstream, kernel, crop_masks, patterns):
    channels = kernel.shape[0]
    stride = min(group_width, channels)
    masks_float = crop_masks.astype(jnp.float32)[:, None]
    input_pieces = []
    kernel_pieces = []
    for offset in range(0, channels, stride):
        matrix = toeplitz(kernel[offset : offset + stride])
        upstream_part = upstream[:, :, :, offset : offset + stride]
        outputs = []
        for canvas in range(inputs.shape[0]):
            masked = matrix * crop_masks[canvas][None]
            outputs.append(
                jnp.einsum(
                    patterns[1], masked, upstream_part[canvas], preferred_element_type=jnp.float32
                )
            )
        products = jnp.einsum(
            patterns[2],
            upstream_part,
            inputs[:, :, :, offset : offset + stride],
            preferred_element_type=jnp.float32,
        )
        summed = jnp.sum(products * masks_float, axis=0)
        input_pieces.append(jnp.stack(outputs))
        kernel_pieces.append(diagonal_sums(summed))
    return (jnp.concatenate(input_pieces, axis=3), jnp.concatenate(kernel_pieces, axis=0))


def kernel_pullback(log_step, log_decay, frequency, coef_real, coef_imag, length, kernel_grad):
    unused, pullback = jax.vjp(
        partial(s4_kernel, length=length), log_step, log_decay, frequency, coef_real, coef_imag
    )
    return pullback(kernel_grad)


def block_forward(stream, params, row_masks, col_masks, canvas_height, canvas_width):
    (
        log_step,
        log_decay,
        frequency,
        coef_real,
        coef_imag,
        skip_gain,
        norm_gain,
        norm_shift,
        weight_in,
        bias_in,
        weight_out,
        bias_out,
        layer_scale,
    ) = params
    channels = weight_in.shape[0]
    tall_kernel = s4_kernel(
        log_step[0], log_decay[0], frequency[0], coef_real[0], coef_imag[0], canvas_height
    ).astype(jnp.bfloat16)
    wide_kernel = s4_kernel(
        log_step[1], log_decay[1], frequency[1], coef_real[1], coef_imag[1], canvas_width
    ).astype(jnp.bfloat16)
    stream_low = stream.astype(jnp.bfloat16)
    across = forward_conv(stream_low, wide_kernel, col_masks, width_forms).astype(jnp.bfloat16)
    columns = lax.all_to_all(across, "rows", split_axis=2, concat_axis=1, tiled=True)
    mixer_cols = forward_conv(columns, tall_kernel, row_masks, height_forms).astype(jnp.bfloat16)
    mixer_rows = lax.all_to_all(mixer_cols, "rows", split_axis=1, concat_axis=2, tiled=True).astype(
        jnp.float32
    )
    mixed_rows = mixer_rows + skip_gain * stream
    total_sum, square_sum = lax.psum(
        (jnp.sum(mixed_rows, axis=3), jnp.sum(mixed_rows * mixed_rows, axis=3)), "ch"
    )
    average = (total_sum / channels)[..., None]
    inverse = lax.rsqrt(square_sum[..., None] / channels - average * average + epsilon)
    centred = (mixed_rows - average) * inverse
    normed = (centred * norm_gain + norm_shift).astype(jnp.bfloat16)
    local_rows = normed.reshape(-1, normed.shape[3])
    gathered = lax.all_gather(local_rows, "ch", axis=1, tiled=True)
    before = jnp.dot(gathered, weight_in, preferred_element_type=jnp.float32) + bias_in
    hidden = jax.nn.gelu(before).astype(jnp.bfloat16)
    partial_out = jnp.dot(hidden, weight_out, preferred_element_type=jnp.float32)
    branch = (
        lax.psum_scatter(partial_out, "ch", scatter_dimension=1, tiled=True) + bias_out
    ).reshape(stream.shape)
    output = stream + layer_scale * branch
    stored = (
        stream,
        stream_low,
        columns,
        centred,
        inverse,
        gathered,
        before,
        hidden,
        branch,
        tall_kernel,
        wide_kernel,
    )
    return (output, stored)


def block_backward(upstream, params, stored, row_masks, col_masks, canvas_height, canvas_width):
    (
        log_step,
        log_decay,
        frequency,
        coef_real,
        coef_imag,
        skip_gain,
        norm_gain,
        norm_shift,
        weight_in,
        bias_in,
        weight_out,
        bias_out,
        layer_scale,
    ) = params
    (
        stream,
        stream_low,
        kept_columns,
        centred,
        inverse,
        gathered,
        before,
        hidden,
        branch,
        tall_kernel,
        wide_kernel,
    ) = stored
    channels = weight_in.shape[0]
    sum_axes = (0, 1, 2)
    scale_grad = jnp.sum(upstream * branch, axis=sum_axes)
    branch_grad = upstream * layer_scale
    bias_out_grad = jnp.sum(branch_grad, axis=sum_axes)
    branch_low = branch_grad.astype(jnp.bfloat16).reshape(-1, branch_grad.shape[3])
    grad_full = lax.all_gather(branch_low, "ch", axis=1, tiled=True)
    hidden_grad = lax.dot_general(
        grad_full, weight_out, (((1,), (1,)), ((), ())), preferred_element_type=jnp.float32
    )
    weight_out_grad = lax.dot_general(
        hidden, grad_full, (((0,), (0,)), ((), ())), preferred_element_type=jnp.float32
    )
    unused, gelu_pull = jax.vjp(jax.nn.gelu, before)
    before_grad = gelu_pull(hidden_grad)[0].astype(jnp.bfloat16)
    bias_in_grad = jnp.sum(before_grad.astype(jnp.float32), axis=0)
    weight_in_grad = lax.dot_general(
        gathered, before_grad, (((0,), (0,)), ((), ())), preferred_element_type=jnp.float32
    )
    normed_part = lax.dot_general(
        before_grad, weight_in, (((1,), (1,)), ((), ())), preferred_element_type=jnp.float32
    )
    normed_grad = lax.psum_scatter(normed_part, "ch", scatter_dimension=1, tiled=True).reshape(
        stream.shape
    )
    gain_grad = jnp.sum(normed_grad * centred, axis=sum_axes)
    shift_grad = jnp.sum(normed_grad, axis=sum_axes)
    scaled = normed_grad * norm_gain
    scaled_sum, paired_sum = lax.psum(
        (jnp.sum(scaled, axis=3), jnp.sum(scaled * centred, axis=3)), "ch"
    )
    mixed_grad = inverse * (
        scaled - scaled_sum[..., None] / channels - centred * paired_sum[..., None] / channels
    )
    skip_grad = jnp.sum(mixed_grad * stream, axis=sum_axes)
    mixer_low = mixed_grad.astype(jnp.bfloat16)
    mixer_cols_grad = lax.all_to_all(mixer_low, "rows", split_axis=2, concat_axis=1, tiled=True)
    across_cols_grad, tall_grad = backward_conv(
        kept_columns, mixer_cols_grad, tall_kernel, row_masks, height_forms
    )
    across_grad = lax.all_to_all(
        across_cols_grad.astype(jnp.bfloat16), "rows", split_axis=1, concat_axis=2, tiled=True
    )
    input_part, wide_grad = backward_conv(
        stream_low, across_grad, wide_kernel, col_masks, width_forms
    )
    stream_grad = upstream + skip_gain * mixed_grad + input_part
    tall_params = kernel_pullback(
        log_step[0],
        log_decay[0],
        frequency[0],
        coef_real[0],
        coef_imag[0],
        canvas_height,
        tall_grad,
    )
    wide_params = kernel_pullback(
        log_step[1], log_decay[1], frequency[1], coef_real[1], coef_imag[1], canvas_width, wide_grad
    )
    state_grads = jnp.stack(
        [
            jnp.stack([tall_params[1], wide_params[1]]),
            jnp.stack([tall_params[2], wide_params[2]]),
            jnp.stack([tall_params[3], wide_params[3]]),
            jnp.stack([tall_params[4], wide_params[4]]),
        ]
    )
    channel_grads = jnp.stack(
        [
            tall_params[0],
            wide_params[0],
            skip_grad,
            gain_grad,
            shift_grad,
            bias_out_grad,
            scale_grad,
        ]
    )
    return (
        stream_grad,
        (state_grads, channel_grads, weight_in_grad, bias_in_grad, weight_out_grad),
    )


def on_device(
    pixels,
    row_starts,
    col_starts,
    log_step,
    log_decay,
    frequency,
    coef_real,
    coef_imag,
    skip_gain,
    norm_gain,
    norm_shift,
    weight_in,
    bias_in,
    weight_out,
    bias_out,
    layer_scale,
    cotangent,
):
    canvas_height = row_starts.shape[1]
    canvas_width = col_starts.shape[1]
    row_masks = crop_mask(row_starts).astype(jnp.bfloat16)
    col_masks = crop_mask(col_starts).astype(jnp.bfloat16)
    weights = (
        log_step,
        log_decay,
        frequency,
        coef_real,
        coef_imag,
        skip_gain,
        norm_gain,
        norm_shift,
        weight_in,
        bias_in,
        weight_out,
        bias_out,
        layer_scale,
    )
    stream = pixels.astype(jnp.float32)
    stored_all = []
    for section_index in range(2):
        params = tuple((member[section_index] for member in weights))
        stream, stored = block_forward(
            stream, params, row_masks, col_masks, canvas_height, canvas_width
        )
        stored_all.append(stored)
    activations = stream.astype(jnp.bfloat16)
    upstream = cotangent.astype(jnp.float32)
    block_grads = [None, None]
    for section_index in (1, 0):
        params = tuple((member[section_index] for member in weights))
        upstream, gradients = block_backward(
            upstream,
            params,
            stored_all[section_index],
            row_masks,
            col_masks,
            canvas_height,
            canvas_width,
        )
        block_grads[section_index] = gradients
    lower_block = block_grads[0]
    upper_block = block_grads[1]
    totals = lax.psum(
        (
            lower_block[0],
            lower_block[1],
            lower_block[2],
            lower_block[3],
            lower_block[4],
            upper_block[0],
            upper_block[1],
            upper_block[2],
            upper_block[3],
            upper_block[4],
        ),
        "rows",
    )
    lower_block = totals[0:5]
    upper_block = totals[5:10]
    state_all = jnp.stack([lower_block[0], upper_block[0]])
    channel_all = jnp.stack([lower_block[1], upper_block[1]])
    return (
        activations,
        upstream.astype(jnp.bfloat16),
        channel_all[:, 0:2],
        state_all[:, 0],
        state_all[:, 1],
        state_all[:, 2],
        state_all[:, 3],
        channel_all[:, 2],
        channel_all[:, 3],
        channel_all[:, 4],
        jnp.stack([lower_block[2], upper_block[2]]),
        jnp.stack([lower_block[3], upper_block[3]]),
        jnp.stack([lower_block[4], upper_block[4]]),
        channel_all[:, 5],
        channel_all[:, 6],
    )


def solution(mesh):
    in_specs = (
        P(None, "rows", None, "ch"),
        P(),
        P(),
        P(None, None, "ch"),
        P(None, None, "ch", None),
        P(None, None, "ch", None),
        P(None, None, "ch", None),
        P(None, None, "ch", None),
        P(None, "ch"),
        P(None, "ch"),
        P(None, "ch"),
        P(None, None, "ch"),
        P(None, "ch"),
        P(None, "ch", None),
        P(None, "ch"),
        P(None, "ch"),
        P(None, "rows", None, "ch"),
    )
    out_specs = (
        P(None, "rows", None, "ch"),
        P(None, "rows", None, "ch"),
        P(None, None, "ch"),
        P(None, None, "ch", None),
        P(None, None, "ch", None),
        P(None, None, "ch", None),
        P(None, None, "ch", None),
        P(None, "ch"),
        P(None, "ch"),
        P(None, "ch"),
        P(None, None, "ch"),
        P(None, "ch"),
        P(None, "ch", None),
        P(None, "ch"),
        P(None, "ch"),
    )
    return jax.shard_map(
        on_device, mesh=mesh, in_specs=in_specs, out_specs=out_specs, check_vma=False
    )
```

profile of v0, /device:TPU:0, one launch (start us, length us, event | category | flops | bytes accessed | tf_op | source)
XLA Modules:
  0.0 1403.7 jit_solution(15828878527991495895)
XLA Ops:
  12.2 49.1 %fusion.19 = (f32[192,128]{1,0:T(8,128)S(1)}, f32[192,128]{1,0:T(8,128)S(1)}) fusion(f32[192,64]{1,0:T(8,128)S(1)} %copy.1249, f32[192,64]{1,0:T(8,128)S(1)} %bitcast_multiply_fusion.3, f32[192,64]{1,0:T(8,128)S(1)} %copy.1247, f32[128]{0:T(128)S(1)} %iota_convert_fusion.1, f32[192,64]{1,0:T(8,128)S(1)} %copy.1246, f32[192,64]{1,0:T(8,128)S(1)} %copy.1298, ...), kind=kLoop, calls=%fused_computation.23 | loop fusion | flops 21970944 | bytes 590336 | tf_op jit(solution)/shard_map/reduce_sum | solution.py:20
  64.7 7.8 reshape.1376
  75.4 8.0 reshape.1377
  90.1 7.8 reshape.1378
  103.1 7.8 reshape.1379
  116.2 8.2 reshape.1380
  129.6 7.8 reshape.1381
  142.4 7.6 all-to-all-start
  150.1 8.3 fusion.186
  196.7 8.8 all_gather.12
  212.9 8.0 reshape.1393
  222.4 7.8 reshape.1392
  231.7 7.8 reshape.1391
  241.0 8.2 reshape.1390
  250.7 7.8 reshape.1394
  260.0 7.9 reshape.1395
  325.9 9.7 all_gather.14
  347.8 8.2 all_gather.13
  415.1 9.0 reduce-scatter.7.cloned.1.call-done
  492.4 7.9 all_gather.15
  509.9 15.2 %rev.213 = f32[32,128,128]{2,1,0:T(8,128)S(1)} reverse(f32[32,128,128]{2,1,0:T(8,128)} %multiply_reduce_fusion.2), dimensions={2} | reverse | bytes 4194304 | tf_op jit(solution)/shard_map/rev | solution.py:34
  530.3 9.4 reshape.1451
  542.0 14.9 %rev.212 = f32[32,128,128]{2,1,0:T(8,128)S(1)} reverse(f32[32,128,128]{2,1,0:T(8,128)} %multiply_reduce_fusion.3), dimensions={2} | reverse | bytes 4194304 | tf_op jit(solution)/shard_map/rev | solution.py:34
  562.1 9.8 reshape.1449
  574.2 14.9 %rev.211 = f32[32,128,128]{2,1,0:T(8,128)S(1)} reverse(f32[32,128,128]{2,1,0:T(8,128)} %multiply_reduce_fusion.4), dimensions={2} | reverse | bytes 4194304 | tf_op jit(solution)/shard_map/rev | solution.py:34
  594.4 9.4 reshape.1447
  606.1 14.9 %rev.210 = f32[32,128,128]{2,1,0:T(8,128)S(1)} reverse(f32[32,128,128]{2,1,0:T(8,128)} %multiply_reduce_fusion.5), dimensions={2} | reverse | bytes 4194304 | tf_op jit(solution)/shard_map/rev | solution.py:34
  626.2 9.6 reshape.1445
  638.1 14.9 %rev.214 = f32[32,128,128]{2,1,0:T(8,128)S(1)} reverse(f32[32,128,128]{2,1,0:T(8,128)} %multiply_reduce_fusion.1), dimensions={2} | reverse | bytes 4194304 | tf_op jit(solution)/shard_map/rev | solution.py:34
  658.2 9.4 reshape.1453
  669.9 15.1 %rev.215 = f32[32,128,128]{2,1,0:T(8,128)S(1)} reverse(f32[32,128,128]{2,1,0:T(8,128)} %multiply_reduce_fusion), dimensions={2} | reverse | bytes 4194304 | tf_op jit(solution)/shard_map/rev | solution.py:34
  690.2 9.4 reshape.1455
  762.4 12.0 fusion.182
  778.2 14.9 %rev.198 = f32[32,128,128]{2,1,0:T(8,128)S(1)} reverse(f32[32,128,128]{2,1,0:T(8,128)} %multiply_reduce_fusion.11), dimensions={2} | reverse | bytes 4194304 | tf_op jit(solution)/shard_map/rev | solution.py:34
  798.4 9.4 reshape.1421
  812.9 15.1 %rev.199 = f32[32,128,128]{2,1,0:T(8,128)S(1)} reverse(f32[32,128,128]{2,1,0:T(8,128)} %multiply_reduce_fusion.10), dimensions={2} | reverse | bytes 4194304 | tf_op jit(solution)/shard_map/rev | solution.py:34
  833.2 9.4 reshape.1423
  847.7 14.9 %rev.200 = f32[32,128,128]{2,1,0:T(8,128)S(1)} reverse(f32[32,128,128]{2,1,0:T(8,128)} %multiply_reduce_fusion.9), dimensions={2} | reverse | bytes 4194304 | tf_op jit(solution)/shard_map/rev | solution.py:34
  867.9 9.8 reshape.1425
  882.7 14.9 %rev.201 = f32[32,128,128]{2,1,0:T(8,128)S(1)} reverse(f32[32,128,128]{2,1,0:T(8,128)} %multiply_reduce_fusion.8), dimensions={2} | reverse | bytes 4194304 | tf_op jit(solution)/shard_map/rev | solution.py:34
  902.9 9.4 reshape.1427
  917.4 15.1 %rev.202 = f32[32,128,128]{2,1,0:T(8,128)S(1)} reverse(f32[32,128,128]{2,1,0:T(8,128)} %multiply_reduce_fusion.7), dimensions={2} | reverse | bytes 4194304 | tf_op jit(solution)/shard_map/rev | solution.py:34
  937.7 9.4 reshape.1429
  952.2 14.9 %rev.203 = f32[32,128,128]{2,1,0:T(8,128)S(1)} reverse(f32[32,128,128]{2,1,0:T(8,128)} %multiply_reduce_fusion.6), dimensions={2} | reverse | bytes 4194304 | tf_op jit(solution)/shard_map/rev | solution.py:34
  972.3 9.6 reshape.1431
  985.5 65.8 %fusion.26 = (f32[192,64]{1,0:T(8,128)S(1)}, f32[192,64]{1,0:T(8,128)S(1)}, f32[192,64]{1,0:T(8,128)S(1)}, f32[192,64]{1,0:T(8,128)S(1)}, f32[192,64]{1,0:T(8,12...) fusion(f32[192,128]{1,0:T(8,128)S(1)} %get-tuple-element.371, ...), kind=kLoop, calls=%fused_computation.30 | loop fusion | flops 72253440 | bytes 983552 | tf_op jit(solution)/shard_map/transpose(jvp())/reduce_sum | solution.py:18
  1058.7 39.9 %all-reduce.24 = (f32[1,7,192]{2,0,1:T(1,128)S(1)}, f32[1,7,192]{2,0,1:T(1,128)S(1)}, f32[1,768]{1,0:T(1,128)S(1)}, f32[1,768]{1,0:T(1,128)S(1)}) all-reduce(f32[1,7,192]{2,0,1:T(1,128)S(1)} %stack.861, f32[1,7,192]{2,0,1:T(1,128)S(1)} %stack.868, f32[1,768]{1,0:T(1,128)S(1)} %stack.903, ...), channel_id=1, replica_groups=mesh['rows'=8,'ch'=4] {'rows'}, use_global_device_ids=true, to_apply=%region_65.66 | all-reduce | flops 4224 | bytes 33792 | tf_op jit(solution)/shard_map/psum | solution.py:344
  1109.4 277.2 %all-reduce.32.cloned.1.call-done = (f32[1,4,2,192,64]{3,4,2,1,0:T(8,128)}, f32[1,4,2,192,64]{3,4,2,1,0:T(8,128)}, f32[1,768,768]{2,1,0:T(8,128)}, f32[1,768,768...) async-done(((f32[1,4,2,192,64]{3,4,2,1,0:T(8,128)}, f32[1,4,2,192,64]{3,4,2,1,0:T(8,128)}, f32[1,768,768]{2,1,0:T(8,128)}, f32[1,768,768]{2,1,0:T(8,128)}, ...) | async-done | bytes 10223632 | tf_op jit(solution)/shard_map/psum | solution.py:344
  (1182 shorter events, 491.8 us)
Async XLA Ops:
  7.2 54.1 %copy-start.200 = (f32[128]{0:T(128)}, f32[128]{0:T(128)S(1)}, u32[]{:S(2)}) copy-start(f32[128]{0:T(128)S(1)} %iota_convert_fusion.1) | copy-start | bytes 1540
  8.0 53.5 %copy-start.137 = (f32[1,1,192]{2,1,0:T(1,128)}, f32[1,1,192]{2,1,0:T(1,128)S(1)}, u32[]{:S(2)}) copy-start(f32[1,1,192]{2,1,0:T(1,128)S(1)} %get-tuple-element.440) | copy-start | bytes 2308
  8.0 53.7 %copy-start.139 = (f32[1,1,192]{2,1,0:T(1,128)}, f32[1,1,192]{2,1,0:T(1,128)S(1)}, u32[]{:S(2)}) copy-start(f32[1,1,192]{2,1,0:T(1,128)S(1)} %get-tuple-element.442) | copy-start | bytes 2308
  8.0 150.5 %copy-start.141 = (f32[1,1,192]{2,1,0:T(1,128)}, f32[1,1,192]{2,1,0:T(1,128)S(1)}, u32[]{:S(2)}) copy-start(f32[1,1,192]{2,1,0:T(1,128)S(1)} %get-tuple-element.439) | copy-start | bytes 2308
  8.0 150.7 %copy-start.143 = (f32[1,1,192]{2,1,0:T(1,128)}, f32[1,1,192]{2,1,0:T(1,128)S(1)}, u32[]{:S(2)}) copy-start(f32[1,1,192]{2,1,0:T(1,128)S(1)} %get-tuple-element.441) | copy-start | bytes 2308
  8.0 53.2 %copy-start.169 = (f32[192]{0:T(256)}, f32[192]{0:T(256)S(1)}, u32[]{:S(2)}) copy-start(f32[192]{0:T(256)S(1)} %neg.116) | copy-start | bytes 2308
  8.1 53.2 %copy-start.171 = (f32[192]{0:T(256)}, f32[192]{0:T(256)S(1)}, u32[]{:S(2)}) copy-start(f32[192]{0:T(256)S(1)} %neg.117) | copy-start | bytes 2308
  8.1 53.2 %copy-start.173 = (f32[192]{0:T(256)}, f32[192]{0:T(256)S(1)}, u32[]{:S(2)}) copy-start(f32[192]{0:T(256)S(1)} %neg.118) | copy-start | bytes 2308
  8.1 53.2 %copy-start.175 = (f32[192]{0:T(256)}, f32[192]{0:T(256)S(1)}, u32[]{:S(2)}) copy-start(f32[192]{0:T(256)S(1)} %neg.119) | copy-start | bytes 2308
  9.1 141.0 %copy-start.125 = (f32[192,64]{0,1:T(8,128)}, f32[192,64]{0,1:T(8,128)S(1)}, u32[]{:S(2)}) copy-start(f32[192,64]{0,1:T(8,128)S(1)} %get-tuple-element.318) | copy-start | bytes 147460
  9.1 141.0 %copy-start.127 = (f32[192,64]{0,1:T(8,128)}, f32[192,64]{0,1:T(8,128)S(1)}, u32[]{:S(2)}) copy-start(f32[192,64]{0,1:T(8,128)S(1)} %get-tuple-element.320) | copy-start | bytes 147460
  9.2 52.1 %copy-start.96 = (f32[192,64]{1,0:T(8,128)}, f32[192,64]{1,0:T(8,128)S(1)}, u32[]{:S(2)}) copy-start(f32[192,64]{1,0:T(8,128)S(1)} %copy.1246) | copy-start | bytes 147460
  9.3 52.0 %copy-start.98 = (f32[192,64]{1,0:T(8,128)}, f32[192,64]{1,0:T(8,128)S(1)}, u32[]{:S(2)}) copy-start(f32[192,64]{1,0:T(8,128)S(1)} %copy.1295) | copy-start | bytes 147460
  10.4 51.0 %copy-start.54 = (f32[1,1,192,64]{3,2,1,0:T(8,128)}, f32[1,1,192,64]{3,2,1,0:T(8,128)S(1)}, u32[]{:S(2)}) copy-start(f32[1,1,192,64]{3,2,1,0:T(8,128)S(1)} %copy.1534) | copy-start | bytes 147460
  10.5 50.9 %copy-start.100 = (f32[192,64]{1,0:T(8,128)}, f32[192,64]{1,0:T(8,128)S(1)}, u32[]{:S(2)}) copy-start(f32[192,64]{1,0:T(8,128)S(1)} %bitcast_multiply_fusion.1) | copy-start | bytes 147460
  10.6 50.8 %copy-start.56 = (f32[1,1,192,64]{3,2,1,0:T(8,128)}, f32[1,1,192,64]{3,2,1,0:T(8,128)S(1)}, u32[]{:S(2)}) copy-start(f32[1,1,192,64]{3,2,1,0:T(8,128)S(1)} %copy.1509) | copy-start | bytes 147460
  10.7 50.7 %copy-start.102 = (f32[192,64]{1,0:T(8,128)}, f32[192,64]{1,0:T(8,128)S(1)}, u32[]{:S(2)}) copy-start(f32[192,64]{1,0:T(8,128)S(1)} %bitcast_multiply_fusion.3) | copy-start | bytes 147460
  11.7 138.4 %copy-start.129 = (f32[192,64]{0,1:T(8,128)}, f32[192,64]{0,1:T(8,128)S(1)}, u32[]{:S(2)}) copy-start(f32[192,64]{0,1:T(8,128)S(1)} %get-tuple-element.322) | copy-start | bytes 147460
  11.7 138.4 %copy-start.131 = (f32[192,64]{0,1:T(8,128)}, f32[192,64]{0,1:T(8,128)S(1)}, u32[]{:S(2)}) copy-start(f32[192,64]{0,1:T(8,128)S(1)} %get-tuple-element.324) | copy-start | bytes 147460
  11.8 49.6 %copy-start.104 = (f32[192,64]{1,0:T(8,128)}, f32[192,64]{1,0:T(8,128)S(1)}, u32[]{:S(2)}) copy-start(f32[192,64]{1,0:T(8,128)S(1)} %copy.1247) | copy-start | bytes 147460
  11.8 138.3 %copy-start.133 = (f32[192,64]{0,1:T(8,128)}, f32[192,64]{0,1:T(8,128)S(1)}, u32[]{:S(2)}) copy-start(f32[192,64]{0,1:T(8,128)S(1)} %get-tuple-element.328) | copy-start | bytes 147460
  11.9 138.3 %copy-start.135 = (f32[192,64]{0,1:T(8,128)}, f32[192,64]{0,1:T(8,128)S(1)}, u32[]{:S(2)}) copy-start(f32[192,64]{0,1:T(8,128)S(1)} %get-tuple-element.330) | copy-start | bytes 147460
  12.0 49.4 %copy-start.106 = (f32[192,64]{1,0:T(8,128)}, f32[192,64]{1,0:T(8,128)S(1)}, u32[]{:S(2)}) copy-start(f32[192,64]{1,0:T(8,128)S(1)} %copy.1249) | copy-start | bytes 147460
  72.9 64.4 %copy-start.159 = (bf16[128,128]{1,0:T(8,128)(2,1)}, bf16[128,128]{1,0:T(8,128)(2,1)S(1)}, u32[]{:S(2)}) copy-start(bf16[128,128]{1,0:T(8,128)(2,1)S(1)} %get-tuple-element.374) | copy-start | bytes 98308
  72.9 66.3 %copy-start.155 = (bf16[128,128]{1,0:T(8,128)(2,1)}, bf16[128,128]{1,0:T(8,128)(2,1)S(1)}, u32[]{:S(2)}) copy-start(bf16[128,128]{1,0:T(8,128)(2,1)S(1)} %get-tuple-element.375) | copy-start | bytes 98308
  142.4 24.0 %all-to-all-start = ((bf16[2,2,128,192]{3,1,0,2:T(2,128)(2,1)}), bf16[2,2,128,192]{3,1,0,2:T(2,128)(2,1)S(1)}, u32[]{:S(2)}, u32[]{:S(2)}) async-start(bf16[2,2,128,192]{3,1,0,2:T(2,128)(2,1)} %copy.1262), calls=%async_computation | async-start | bytes 524288 | tf_op jit(solution)/shard_map/all_to_all | solution.py:130
  175.6 14.5 %all-to-all-start.1 = ((bf16[2,16,16,192]{3,2,0,1:T(8,128)(2,1)}), bf16[2,16,16,192]{3,2,0,1:T(8,128)(2,1)S(1)}, u32[]{:S(2)}, u32[]{:S(2)}) async-start(bf16[2,16,16,192]{3,2,0,1:T(8,128)(2,1)} %copy.1289), calls=%async_computation.1 | async-start | bytes 524288 | tf_op jit(solution)/shard_map/all_to_all | solution.py:132
  181.6 86.9 %reduce-scatter.5.cloned.1.call-start = ((), (), s32[]{:S(2)}) async-start(), calls=%async_computation.12 | async-start | bytes 1966080 | tf_op jit(solution)/shard_map/reduce_scatter | solution.py:149
  268.5 56.3 %copy-start.179 = (f32[1,192]{1,0:T(1,128)}, f32[1,192]{1,0:T(1,128)S(1)}, u32[]{:S(2)}) copy-start(f32[1,192]{1,0:T(1,128)S(1)} %get-tuple-element.443) | copy-start | bytes 2308
  268.5 68.2 %copy-start.166 = (f32[1,192]{1,0:T(1,128)}, f32[1,192]{1,0:T(1,128)S(1)}, u32[]{:S(2)}) copy-start(f32[1,192]{1,0:T(1,128)S(1)} %get-tuple-element.444) | copy-start | bytes 2308
  282.0 13.1 all-to-all-start.2
  321.2 14.4 %all-to-all-start.3 = ((bf16[2,16,16,192]{3,2,0,1:T(8,128)(2,1)}), bf16[2,16,16,192]{3,2,0,1:T(8,128)(2,1)S(1)}, u32[]{:S(2)}, u32[]{:S(2)}) async-start(bf16[2,16,16,192]{3,2,0,1:T(8,128)(2,1)} %copy.1338), calls=%async_computation.4 | async-start | bytes 524288 | tf_op jit(solution)/shard_map/all_to_all | solution.py:132
  324.8 68.6 %reduce-scatter.9.cloned.1.call-start = ((), (), s32[]{:S(2)}) async-start(), calls=%async_computation.14 | async-start | bytes 1966080 | tf_op jit(solution)/shard_map/reduce_scatter | solution.py:219
  364.2 59.8 %reduce-scatter.7.cloned.1.call-start = ((), (), s32[]{:S(2)}) async-start(), calls=%async_computation.13 | async-start | bytes 1966080 | tf_op jit(solution)/shard_map/reduce_scatter | solution.py:149
  403.7 87.5 %copy-start.7 = (f32[2,2,128,192]{2,3,1,0:T(8,128)}, f32[2,2,128,192]{2,3,1,0:T(8,128)S(1)}, u32[]{:S(2)}) copy-start(f32[2,2,128,192]{2,3,1,0:T(8,128)S(1)} %get-tuple-element.196) | copy-start | bytes 1179652
  405.7 20.5 %all-to-all-start.4 = ((bf16[2,2,128,192]{3,1,0,2:T(2,128)(2,1)}), bf16[2,2,128,192]{3,1,0,2:T(2,128)(2,1)S(1)}, u32[]{:S(2)}, u32[]{:S(2)}) async-start(bf16[2,2,128,192]{3,1,0,2:T(2,128)(2,1)} %copy.1346), calls=%async_computation.7 | async-start | bytes 524288 | tf_op jit(solution)/shard_map/all_to_all | solution.py:233
  455.0 15.3 %all-to-all-start.5 = ((bf16[2,16,16,192]{3,2,0,1:T(8,128)(2,1)}), bf16[2,16,16,192]{3,2,0,1:T(8,128)(2,1)S(1)}, u32[]{:S(2)}, u32[]{:S(2)}) async-start(bf16[2,16,16,192]{3,2,0,1:T(8,128)(2,1)} %copy.1361), calls=%async_computation.8 | async-start | bytes 524288 | tf_op jit(solution)/shard_map/all_to_all | solution.py:237
  460.6 254.4 %reduce-scatter.11.cloned.1.call-start = ((), (), s32[]{:S(2)}) async-start(), calls=%async_computation.15 | async-start | bytes 1966080 | tf_op jit(solution)/shard_map/reduce_scatter | solution.py:219
  728.3 14.5 %all-to-all-start.6 = ((bf16[2,2,128,192]{3,1,0,2:T(2,128)(2,1)}), bf16[2,2,128,192]{3,1,0,2:T(2,128)(2,1)S(1)}, u32[]{:S(2)}, u32[]{:S(2)}) async-start(bf16[2,2,128,192]{3,1,0,2:T(2,128)(2,1)} %copy.1390), calls=%async_computation.10 | async-start | bytes 524288 | tf_op jit(solution)/shard_map/all_to_all | solution.py:233
  758.7 17.1 %all-to-all-start.7 = ((bf16[2,16,16,192]{3,2,0,1:T(8,128)(2,1)}), bf16[2,16,16,192]{3,2,0,1:T(8,128)(2,1)S(1)}, u32[]{:S(2)}, u32[]{:S(2)}) async-start(bf16[2,16,16,192]{3,2,0,1:T(8,128)(2,1)} %copy.1405), calls=%async_computation.11 | async-start | bytes 524288 | tf_op jit(solution)/shard_map/all_to_all | solution.py:237
  762.1 624.5 %all-reduce.32.cloned.1.call-start = ((), (), s32[]{:S(2)}) async-start(), calls=%async_computation.16 | async-start | bytes 20971520 | tf_op jit(solution)/shard_map/psum | solution.py:344
  985.4 66.7 %copy-start.24 = (f32[2,2,192,64]{2,3,1,0:T(8,128)S(1)}, f32[2,2,192,64]{2,3,1,0:T(8,128)}, u32[]{:S(2)}) copy-start(f32[2,2,192,64]{2,3,1,0:T(8,128)} %param.21) | copy-start | bytes 589828
  985.4 66.6 %copy-start.81 = (f32[192,64]{0,1:T(8,128)S(1)}, f32[192,64]{0,1:T(8,128)}, u32[]{:S(2)}) copy-start(f32[192,64]{0,1:T(8,128)} %get-tuple-element.144) | copy-start | bytes 147460
  985.4 66.6 %copy-start.82 = (f32[192,64]{0,1:T(8,128)S(1)}, f32[192,64]{0,1:T(8,128)}, u32[]{:S(2)}) copy-start(f32[192,64]{0,1:T(8,128)} %get-tuple-element.168) | copy-start | bytes 147460
  985.5 66.6 %copy-start.170 = (f32[192]{0:T(256)S(1)}, f32[192]{0:T(256)}, u32[]{:S(2)}) copy-start(f32[192]{0:T(256)} %copy-done.169) | copy-start | bytes 2308
  985.5 66.6 %copy-start.172 = (f32[192]{0:T(256)S(1)}, f32[192]{0:T(256)}, u32[]{:S(2)}) copy-start(f32[192]{0:T(256)} %copy-done.171) | copy-start | bytes 2308
  985.5 66.6 %copy-start.174 = (f32[192]{0:T(256)S(1)}, f32[192]{0:T(256)}, u32[]{:S(2)}) copy-start(f32[192]{0:T(256)} %copy-done.173) | copy-start | bytes 2308
  985.5 66.6 %copy-start.176 = (f32[192]{0:T(256)S(1)}, f32[192]{0:T(256)}, u32[]{:S(2)}) copy-start(f32[192]{0:T(256)} %copy-done.175) | copy-start | bytes 2308
  (171 other events, 1096.9 us)
Sparse Core Ops, SparseCore 0:
  211.6 26.4 reduce-scatter.4
  364.4 28.9 reduce-scatter.8
  395.9 28.1 reduce-scatter.6
  506.7 29.3 reduce-scatter.10
  1054.3 332.2 all-reduce.31
where the time goes:
time: 1430 us; the launch traced here: 1400 us
  local copies, waits for them, and re-layouts  583 us (41%)
  waiting for transfers between devices  305 us (21%)
  other arithmetic  215 us (15%)
  matrix products  138 us (10%)
  blocking collectives  100 us (7%)
  starting transfers between devices  42.1 us (3%)
  between operations  19.8 us (1%)
    psum x1, waiting for transfers between devices, on_device(): lax.psum((lower_block[0], lower_block[1], lower_block[2], lower_block[3],...  277 us
    rev x24, local copies, waits for them, and re-layouts, diagonal_sums(): turned = products[:, :, ::-1]  181 us
    reshape x24, local copies, waits for them, and re-layouts, diagonal_sums(): skewed = skewed.reshape(channels, length, 2 * length - 1)  116 us
    unnamed x558, local copies, waits for them, and re-layouts  98.2 us
    reshape x24, local copies, waits for them, and re-layouts, toeplitz(): return repeated.reshape(channels, length, 2 * length - 1)[:, :, :length]  97 us
    reduce_sum x5, other arithmetic, s4_kernel(): turning = step_size * frequency[:, :, None] * places  78.9 us
    reduce_sum x4, other arithmetic, s4_kernel(): return step_size[:, :, 0] * jnp.sum(fading * waving, axis=1)  57.7 us
    dot_general x48, matrix products, forward_conv(): jnp.einsum(patterns[0], masked, inputs[canvas, :, :, offset:offset + stri...  40.4 us
  transfers between devices with their start and end apart: 13, of which 6 were waited for; matrix products, arithmetic and copies ran while one was open for 26% of the time, Pallas kernels for 0%

commit v1 on v0

v1 whole, which is shorter than its diff:
```python
from functools import partial

import jax
import jax.numpy as jnp
from jax import lax
from jax.experimental import pallas as pl
from jax.experimental.pallas import tpu as pltpu
from jax.sharding import PartitionSpec as P


epsilon = 1e-06
bf16 = jnp.bfloat16
f32 = jnp.float32
vmem_bytes = 56 * 1024 * 1024
ahead = 8
band = 16
lane = 128


def dot(a, b, ca, cb):
    return lax.dot_general(a, b, (((ca,), (cb,)), ((), ())), preferred_element_type=f32)


def vmem_spec():
    return pl.BlockSpec(memory_space=pltpu.VMEM)


def smem_spec():
    return pl.BlockSpec(memory_space=pltpu.SMEM)


def struct(shape, dtype):
    return jax.ShapeDtypeStruct(shape, dtype)


def params(flops=0, moved=0):
    return dict(
        compiler_params=pltpu.CompilerParams(vmem_limit_bytes=vmem_bytes),
        cost_estimate=pl.CostEstimate(flops=flops, bytes_accessed=moved, transcendentals=0),
    )


def transposed(value):
    rows, cols = value.shape
    return jnp.transpose(value)


def state_powers(step, decay, frequency):
    size = jnp.exp(-step * decay)
    turn = step * frequency
    z = (size * jnp.cos(turn), size * jnp.sin(turn))

    def times(p, q):
        return (p[0] * q[0] - p[1] * q[1], p[0] * q[1] + p[1] * q[0])

    z2 = times(z, z)
    z3 = times(z2, z)
    z4 = times(z2, z2)
    return [None, z, z2, z3, z4, times(z4, z), times(z4, z2), times(z4, z3)], times(z4, z4), times


def s4_body(lengths, step_ref, decay_ref, freq_ref, real_ref, imag_ref, tall_ref, wide_ref,
            qr_ref, qi_ref, pr_ref, pi_ref, out_ref):
    channels = step_ref.shape[2]
    for direction, length in enumerate(lengths):
        step = jnp.exp(step_ref[0, direction:direction + 1, :])
        decay = jnp.exp(decay_ref[0, direction])
        powers, z8, times = state_powers(step, decay, freq_ref[0, direction])
        powers[0] = (jnp.ones_like(decay), jnp.zeros_like(decay))
        for a in range(ahead):
            qr_ref[a] = powers[a][0]
            qi_ref[a] = powers[a][1]
        pr_ref[0] = real_ref[0, direction]
        pi_ref[0] = imag_ref[0, direction]
        turns = length // ahead
        qr_ref[ahead] = z8[0]
        qi_ref[ahead] = z8[1]

        def block(b, carry):
            pr, pi = pr_ref[0], pi_ref[0]
            rows = []
            for a in range(ahead):
                rows.append(jnp.sum(pr * qr_ref[a] - pi * qi_ref[a], axis=0, keepdims=True))
            out_ref[pl.ds(pl.multiple_of(b * ahead, ahead), ahead), 0:channels] = (
                step * jnp.concatenate(rows, axis=0)
            ).astype(bf16).astype(f32)
            zr, zi = qr_ref[ahead], qi_ref[ahead]
            pr_ref[0] = pr * zr - pi * zi
            pi_ref[0] = pr * zi + pi * zr
            return carry

        lax.fori_loop(0, turns, block, 0)
        flipped = jnp.transpose(out_ref[...])[0:channels, :]
        if direction == 0:
            tall_ref[...] = flipped
        else:
            copies = wide_ref.shape[1] // channels
            wide_ref[...] = jnp.transpose(jnp.concatenate([flipped] * copies, axis=0))


def s4_kernels(section, lengths, log_step, log_decay, frequency, coef_real, coef_imag, copies):
    states, channels = log_decay.shape[2], log_decay.shape[3]
    whole = pl.BlockSpec((1, 2, states, channels), lambda i: (section, 0, 0, 0))
    wide_lanes = -(-channels // lane) * lane
    return pl.pallas_call(
        partial(s4_body, lengths),
        grid=(1,),
        in_specs=[pl.BlockSpec((1, 2, channels), lambda i: (section, 0, 0)), whole, whole, whole, whole],
        out_specs=[
            pl.BlockSpec((channels, lane), lambda i: (0, 0)),
            pl.BlockSpec((lane, copies * channels), lambda i: (0, 0)),
        ],
        out_shape=[struct((channels, lane), f32), struct((lane, copies * channels), f32)],
        scratch_shapes=[
            pltpu.VMEM((ahead + 1, states, channels), f32),
            pltpu.VMEM((ahead + 1, states, channels), f32),
            pltpu.VMEM((1, states, channels), f32),
            pltpu.VMEM((1, states, channels), f32),
            pltpu.VMEM((lane, wide_lanes), f32),
        ],
        name="s4_kernels",
        **params(10_000_000, 1_000_000),
    )(log_step, log_decay, frequency, coef_real, coef_imag)


def pull_body(lengths, tall_ref, wide_ref, step_ref, decay_ref, freq_ref, real_ref, imag_ref,
              dstep_ref, ddecay_ref, dfreq_ref, dreal_ref, dimag_ref, turn_ref, grad_ref, q_ref, s_ref):
    channels = step_ref.shape[2]
    states = decay_ref.shape[2]
    for direction, length in enumerate(lengths):
        step = jnp.exp(step_ref[0, direction:direction + 1, :])
        decay = jnp.exp(decay_ref[0, direction])
        freq = freq_ref[0, direction]
        powers, z8, times = state_powers(step, decay, freq)
        for a in range(1, ahead):
            q_ref[2 * a] = powers[a][0]
            q_ref[2 * a + 1] = powers[a][1]
        q_ref[0] = z8[0]
        q_ref[1] = z8[1]
        turn_ref[0:channels, :] = (tall_ref if direction == 0 else wide_ref)[0]
        flat = jnp.transpose(turn_ref[...])
        for place in range(length):
            grad_ref[place] = jnp.broadcast_to(flat[place:place + 1, 0:channels], (8, channels))
        turns = length // ahead

        def group(n, carry):
            off = pl.multiple_of(n * 8, 8)
            part = pl.ds(off, 8)
            q = [(q_ref[2 * a, part, :], q_ref[2 * a + 1, part, :]) for a in range(ahead)]
            zr, zi = q[0]

            def block(index, sums):
                s0r, s0i, s1r, s1i = sums
                b = turns - 1 - index
                g = grad_ref[b * ahead]
                t0r, t0i = g, jnp.zeros_like(g)
                t1r, t1i = jnp.zeros_like(g), jnp.zeros_like(g)
                for a in range(1, ahead):
                    g = grad_ref[b * ahead + a]
                    x, y = g * q[a][0], g * q[a][1]
                    t0r, t0i = t0r + x, t0i + y
                    t1r, t1i = t1r + a * x, t1i + a * y
                base = (b * ahead).astype(f32)
                v1r, v1i = t1r + base * t0r, t1i + base * t0i
                return (
                    s0r * zr - s0i * zi + t0r,
                    s0r * zi + s0i * zr + t0i,
                    s1r * zr - s1i * zi + v1r,
                    s1r * zi + s1i * zr + v1i,
                )

            zero = jnp.zeros((8, channels), f32)
            sums = lax.fori_loop(0, turns, block, (zero, zero, zero, zero))
            for k in range(4):
                s_ref[k, part, :] = sums[k]
            return carry

        lax.fori_loop(0, states // 8, group, 0)
        real, imag = real_ref[0, direction], imag_ref[0, direction]
        s0r, s0i, s1r, s1i = s_ref[0], s_ref[1], s_ref[2], s_ref[3]
        dreal = step * s0r
        dimag = -step * s0i
        ddecay = -step * step * decay * (real * s1r - imag * s1i)
        dfreq = -step * step * (real * s1i + imag * s1r)
        dreal_ref[0, direction] = dreal
        dimag_ref[0, direction] = dimag
        ddecay_ref[0, direction] = ddecay
        dfreq_ref[0, direction] = dfreq
        dstep_ref[0, direction:direction + 1, :] = jnp.sum(
            real * dreal + imag * dimag + ddecay + freq * dfreq, axis=0, keepdims=True
        )


def s4_pullback(lengths, tall_grads, wide_grads, log_step, log_decay, frequency, coef_real, coef_imag):
    states, channels = log_decay.shape[2], log_decay.shape[3]
    whole = pl.BlockSpec((1, 2, states, channels), lambda i: (i, 0, 0, 0))
    row = pl.BlockSpec((1, 2, channels), lambda i: (i, 0, 0))
    grad = pl.BlockSpec((1, channels, lane), lambda i: (i, 0, 0))
    wide_lanes = -(-channels // lane) * lane
    return pl.pallas_call(
        partial(pull_body, lengths),
        grid=(2,),
        in_specs=[grad, grad, row, whole, whole, whole, whole],
        out_specs=[row, whole, whole, whole, whole],
        out_shape=[struct(log_step.shape, f32)] + [struct(log_decay.shape, f32)] * 4,
        scratch_shapes=[
            pltpu.VMEM((wide_lanes, lane), f32),
            pltpu.VMEM((lane, 8, channels), f32),
            pltpu.VMEM((2 * ahead, states, channels), f32),
            pltpu.VMEM((4, states, channels), f32),
        ],
        name="s4_pullback",
        **params(100_000_000, 2_000_000),
    )(tall_grads, wide_grads, log_step, log_decay, frequency, coef_real, coef_imag)


def spread_kernel(wide_ref, spread_ref):
    for place in range(wide_ref.shape[0]):
        spread_ref[place] = jnp.broadcast_to(wide_ref[place:place + 1, :], (8, wide_ref.shape[1]))


def shift_copies(value, shifted_ref, sign):
    for s in range(ahead):
        shifted_ref[s] = value if s == 0 else pltpu.roll(value, (sign * s) % value.shape[0], 0)


def width_conv(canvas, sign, shifted_ref, spread_ref, age_ref, reach_ref, out_ref):
    width = out_ref.shape[0]
    groups = width // 8
    tiles = out_ref.shape[1] // lane
    per = band // 8
    for index in range(width // band):
        ages = [age_ref[canvas, pl.ds((index * per + k) * 8, 8), :] for k in range(per)]

        def body(q, sums):
            sums = list(sums)
            places = [
                pl.multiple_of(jnp.clip(index * per + k - sign * q, 0, groups - 1) * 8, 8) for k in range(per)
            ]
            for s in range(ahead):
                lag = q * ahead + s
                for k in range(per):
                    seen = ages[k] >= lag
                    for t in range(tiles):
                        cut = slice(t * lane, (t + 1) * lane)
                        x = shifted_ref[s, pl.ds(places[k], 8), cut]
                        sums[k * tiles + t] += spread_ref[lag, :, cut] * jnp.where(seen, x, 0.0)
            return tuple(sums)

        zero = jnp.zeros((8, lane), f32)
        sums = lax.fori_loop(0, reach_ref[canvas, index], body, (zero,) * (per * tiles))
        for k in range(per):
            for t in range(tiles):
                out_ref[pl.ds((index * per + k) * 8, 8), t * lane:(t + 1) * lane] = sums[k * tiles + t]


def width_products(canvas, shifted_ref, grad_ref, age_ref, reach_ref, total_ref):
    width = grad_ref.shape[0]
    groups = width // 8
    tiles = grad_ref.shape[1] // lane
    per = band // 8
    for index in range(width // band):
        ages = [age_ref[canvas, pl.ds((index * per + k) * 8, 8), :] for k in range(per)]
        grads = [
            [grad_ref[pl.ds((index * per + k) * 8, 8), t * lane:(t + 1) * lane] for t in range(tiles)]
            for k in range(per)
        ]

        def body(q, carry):
            places = [
                pl.multiple_of(jnp.clip(index * per + k - q, 0, groups - 1) * 8, 8) for k in range(per)
            ]
            for s in range(ahead):
                lag = q * ahead + s
                seen = [ages[k] >= lag for k in range(per)]
                for t in range(tiles):
                    cut = slice(t * lane, (t + 1) * lane)
                    total = total_ref[lag, :, cut]
                    for k in range(per):
                        x = shifted_ref[s, pl.ds(places[k], 8), cut]
                        total += grads[k][t] * jnp.where(seen[k], x, 0.0)
                    total_ref[lag, :, cut] = total
            return carry

        lax.fori_loop(0, reach_ref[canvas, index], body, 0)


def stacked_rows(ref, canvas):
    picture = ref[canvas].astype(f32)
    return jnp.transpose(picture.reshape(-1, picture.shape[2]))


def unstacked(value, rows):
    flat = jnp.transpose(value)
    return flat.reshape(rows, flat.shape[0] // rows, flat.shape[1])


def width_scratch(rows, channels):
    lanes = rows * channels
    return [
        pltpu.VMEM((ahead, lane, lanes), f32),
        pltpu.VMEM((lane, 8, lanes), f32),
        pltpu.VMEM((lane, lanes), f32),
    ]


def wide_forward_body(picture_ref, wide_ref, age_ref, reach_ref, out_ref, shifted_ref, spread_ref, sum_ref):
    rows = picture_ref.shape[1]
    spread_kernel(wide_ref, spread_ref)
    for canvas in range(picture_ref.shape[0]):
        shift_copies(stacked_rows(picture_ref, canvas), shifted_ref, 1)
        width_conv(canvas, 1, shifted_ref, spread_ref, age_ref, reach_ref, sum_ref)
        out_ref[canvas] = unstacked(sum_ref[...], rows).astype(bf16)


def wide_forward(picture, wide, age, reach):
    return pl.pallas_call(
        wide_forward_body,
        in_specs=[vmem_spec(), vmem_spec(), vmem_spec(), smem_spec()],
        out_specs=vmem_spec(),
        out_shape=struct(picture.shape, bf16),
        scratch_shapes=width_scratch(picture.shape[1], picture.shape[2]),
        name="wide_forward",
        **params(30_000_000, 2_000_000),
    )(picture, wide, age, reach)


def wide_mixed_body(tall_ref, stream_ref, wide_ref, age_ref, reach_ref, pack_ref, out_ref,
                    shifted_ref, spread_ref, sum_ref):
    rows = tall_ref.shape[1]
    skip = pack_ref[:, 0:1]
    spread_kernel(wide_ref, spread_ref)
    for canvas in range(tall_ref.shape[0]):
        shift_copies(stacked_rows(tall_ref, canvas), shifted_ref, 1)
        width_conv(canvas, 1, shifted_ref, spread_ref, age_ref, reach_ref, sum_ref)
        mixer = unstacked(sum_ref[...], rows)
        for row in range(rows):
            at = (canvas * rows + row) * lane
            out_ref[:, at:at + lane] = (
                mixer[row] + skip * stream_ref[canvas, row].astype(f32)
            ).astype(bf16)


def wide_mixed(tall, stream, wide, age, reach, pack):
    pixels = tall.shape[0] * tall.shape[1] * lane
    return pl.pallas_call(
        wide_mixed_body,
        in_specs=[vmem_spec()] * 4 + [smem_spec(), vmem_spec()],
        out_specs=vmem_spec(),
        out_shape=struct((tall.shape[2], pixels), bf16),
        scratch_shapes=width_scratch(tall.shape[1], tall.shape[2]),
        name="wide_mixed",
        **params(30_000_000, 2_000_000),
    )(tall, stream, wide, age, reach, pack)


def norm_backward(grads, mixed_ref, stats_ref, pack_ref, channels_all):
    channels = mixed_ref.shape[0]
    keep, near, far = grads
    total = keep[...].astype(f32) + near[...].astype(f32) + far[...].astype(f32)
    normed_grad = total[0:channels]
    scaled_mean = total[channels:channels + 1] / channels_all
    paired_mean = total[channels + 1:channels + 2] / channels_all
    average, inverse = stats_ref[0:1, :], stats_ref[1:2, :]
    centred = (mixed_ref[...].astype(f32) - average) * inverse
    gain = pack_ref[:, 1:2]
    mixed_grad = inverse * (normed_grad * gain - scaled_mean - centred * paired_mean)
    return (
        mixed_grad,
        jnp.sum(normed_grad * centred, axis=1, keepdims=True),
        jnp.sum(normed_grad, axis=1, keepdims=True),
    )


def put_columns(ref, columns):
    places = lax.broadcasted_iota(jnp.int32, ref.shape, 1)
    value = jnp.zeros(ref.shape, f32)
    for index, column in enumerate(columns):
        value = jnp.where(places == index, column, value)
    ref[...] = value


def wide_norm_back_body(channels_all, keep_ref, near_ref, far_ref, mixed_ref, stats_ref, pack_ref, stream_ref,
                        cotangent_ref, wide_ref, fore_ref, reach_ref, conv_ref, rest_ref, grad_ref, sums_ref,
                        shifted_ref, spread_ref, sum_ref):
    canvases, rows = conv_ref.shape[0], conv_ref.shape[1]
    mixed_grad, gain_grad, shift_grad = norm_backward(
        (keep_ref, near_ref, far_ref), mixed_ref, stats_ref, pack_ref, channels_all
    )
    skip = pack_ref[:, 0:1]
    skip_grad = jnp.zeros_like(gain_grad)
    spread_kernel(wide_ref, spread_ref)
    for canvas in range(canvases):
        for row in range(rows):
            at = (canvas * rows + row) * lane
            part = mixed_grad[:, at:at + lane]
            grad_ref[canvas, row] = part.astype(bf16)
            skip_grad += jnp.sum(part * stream_ref[canvas, row].astype(f32), axis=1, keepdims=True)
            rest_ref[canvas, row] = (cotangent_ref[canvas, row].astype(f32) + skip * part).astype(bf16)
        shift_copies(stacked_rows(grad_ref, canvas), shifted_ref, -1)
        width_conv(canvas, -1, shifted_ref, spread_ref, fore_ref, reach_ref, sum_ref)
        conv_ref[canvas] = unstacked(sum_ref[...], rows).astype(bf16)
    put_columns(sums_ref, [skip_grad, gain_grad, shift_grad])


def wide_norm_back(channels_all, grads, mixed, stats, pack, stream, cotangent, wide, fore, reach):
    return pl.pallas_call(
        partial(wide_norm_back_body, channels_all),
        in_specs=[vmem_spec()] * 10 + [smem_spec()],
        out_specs=[vmem_spec()] * 4,
        out_shape=[struct(stream.shape, bf16)] * 3 + [struct((stream.shape[2], lane), f32)],
        scratch_shapes=width_scratch(stream.shape[1], stream.shape[2]),
        name="wide_norm_back",
        **params(30_000_000, 2_000_000),
    )(*grads, mixed, stats, pack, stream, cotangent, wide, fore, reach)


def wide_back_body(grad_ref, rest_ref, wide_ref, fore_ref, reach_ref, out_ref, shifted_ref, spread_ref, sum_ref):
    rows = grad_ref.shape[1]
    spread_kernel(wide_ref, spread_ref)
    for canvas in range(grad_ref.shape[0]):
        shift_copies(stacked_rows(grad_ref, canvas), shifted_ref, -1)
        width_conv(canvas, -1, shifted_ref, spread_ref, fore_ref, reach_ref, sum_ref)
        out_ref[canvas] = (unstacked(sum_ref[...], rows) + rest_ref[canvas].astype(f32)).astype(bf16)


def wide_back(grad, rest, wide, fore, reach):
    return pl.pallas_call(
        wide_back_body,
        in_specs=[vmem_spec()] * 4 + [smem_spec()],
        out_specs=vmem_spec(),
        out_shape=struct(grad.shape, bf16),
        scratch_shapes=width_scratch(grad.shape[1], grad.shape[2]),
        name="wide_back",
        **params(30_000_000, 2_000_000),
    )(grad, rest, wide, fore, reach)


def wide_kernel_grad_body(grad_ref, input_ref, age_ref, reach_ref, out_ref, shifted_ref, total_ref, flat_ref, sum_ref):
    channels = grad_ref.shape[2]
    rows = grad_ref.shape[1]
    total_ref[...] = jnp.zeros(total_ref.shape, f32)
    for canvas in range(grad_ref.shape[0]):
        shift_copies(stacked_rows(input_ref, canvas), shifted_ref, 1)
        flat_ref[...] = stacked_rows(grad_ref, canvas)
        width_products(canvas, shifted_ref, flat_ref, age_ref, reach_ref, total_ref)

    def reduce(index, carry):
        at = pl.multiple_of(index * 8, 8)
        sum_ref[pl.ds(at, 8), :] = jnp.sum(total_ref[pl.ds(at, 8)], axis=1)
        return carry

    lax.fori_loop(0, total_ref.shape[0] // 8, reduce, 0)
    flat = jnp.transpose(sum_ref[...])
    out_ref[...] = sum(flat[row * channels:(row + 1) * channels] for row in range(rows))


def wide_kernel_grad(grad, inputs, age, reach):
    lanes = grad.shape[1] * grad.shape[2]
    return pl.pallas_call(
        wide_kernel_grad_body,
        in_specs=[vmem_spec()] * 3 + [smem_spec()],
        out_specs=vmem_spec(),
        out_shape=struct((grad.shape[2], lane), f32),
        scratch_shapes=width_scratch(grad.shape[1], grad.shape[2]) + [pltpu.VMEM((lane, lanes), f32)],
        name="wide_kernel_grad",
        **params(30_000_000, 2_000_000),
    )(grad, inputs, age, reach)


def height_loop(count, body, carry):
    if count <= 16:
        for lag in range(count):
            carry = body(lag, carry)
        return carry
    return lax.fori_loop(0, count, body, carry)


def tap(tall_ref, lag):
    if isinstance(lag, int):
        return tall_ref[:, lag:lag + 1]
    places = lax.broadcasted_iota(jnp.int32, tall_ref.shape, 1)
    return jnp.sum(jnp.where(places == lag, tall_ref[...], 0.0), axis=1, keepdims=True)


def height_conv(value, tall_ref, age, sign, height):
    columns = value.shape[1] // height

    def body(lag, total):
        moved = pltpu.roll(value, (sign * lag * columns) % value.shape[1], 1) if not isinstance(lag, int) or lag else value
        return total + tap(tall_ref, lag) * jnp.where(age >= lag, moved, 0.0)

    return height_loop(height, body, jnp.zeros_like(value))


def height_products(grad, value, age, height, start):
    columns = value.shape[1] // height
    places = lax.broadcasted_iota(jnp.int32, start.shape, 1)

    def body(lag, total):
        moved = pltpu.roll(value, (lag * columns) % value.shape[1], 1) if not isinstance(lag, int) or lag else value
        summed = jnp.sum(grad * jnp.where(age >= lag, moved, 0.0), axis=1, keepdims=True)
        return total + jnp.where(places == lag, summed, 0.0)

    return height_loop(height, body, start)


def canvas_cut(ref, canvas, canvases):
    each = ref.shape[1] // canvases
    return slice(canvas * each, (canvas + 1) * each)


def tall_mixed_body(height, across_ref, stream_ref, tall_ref, age_ref, pack_ref, out_ref):
    canvases = age_ref.shape[0]
    skip = pack_ref[:, 0:1]
    for canvas in range(canvases):
        cut = canvas_cut(across_ref, canvas, canvases)
        mixer = height_conv(across_ref[:, cut].astype(f32), tall_ref, age_ref[canvas], 1, height)
        out_ref[:, cut] = (mixer + skip * stream_ref[:, cut].astype(f32)).astype(bf16)


def tall_mixed(height, across, stream, tall, age, pack):
    return pl.pallas_call(
        partial(tall_mixed_body, height),
        in_specs=[vmem_spec()] * 5,
        out_specs=vmem_spec(),
        out_shape=struct(across.shape, bf16),
        name="tall_mixed",
        **params(10_000_000, 1_000_000),
    )(across, stream, tall, age, pack)


def tall_next_body(height, keep_ref, near_ref, far_ref, stream_ref, pack_ref, tall_ref, age_ref,
                   next_ref, branch_ref, out_ref):
    canvases = age_ref.shape[0]
    bias, scale = pack_ref[:, 3:4], pack_ref[:, 4:5]
    for canvas in range(canvases):
        cut = canvas_cut(stream_ref, canvas, canvases)
        branch = keep_ref[:, cut].astype(f32) + near_ref[:, cut].astype(f32) + far_ref[:, cut].astype(f32) + bias
        branch_ref[:, cut] = branch
        low = (stream_ref[:, cut].astype(f32) + scale * branch).astype(bf16)
        next_ref[:, cut] = low
        out_ref[:, cut] = height_conv(low.astype(f32), tall_ref, age_ref[canvas], 1, height).astype(bf16)


def tall_next(height, branches, stream, pack, tall, age):
    return pl.pallas_call(
        partial(tall_next_body, height),
        in_specs=[vmem_spec()] * 7,
        out_specs=[vmem_spec()] * 3,
        out_shape=[struct(stream.shape, bf16), struct(stream.shape, f32), struct(stream.shape, bf16)],
        name="tall_next",
        **params(10_000_000, 1_000_000),
    )(*branches, stream, pack, tall, age)


def tall_back_body(height, conv_ref, rest_ref, tall_ref, fore_ref, pack_ref, branch_ref,
                   grad_ref, low_ref, sums_ref):
    canvases = fore_ref.shape[0]
    scale = pack_ref[:, 4:5]
    scale_grad = jnp.zeros((conv_ref.shape[0], 1), f32)
    bias_grad = jnp.zeros((conv_ref.shape[0], 1), f32)
    for canvas in range(canvases):
        cut = canvas_cut(conv_ref, canvas, canvases)
        grad = rest_ref[:, cut].astype(f32) + height_conv(
            conv_ref[:, cut].astype(f32), tall_ref, fore_ref[canvas], -1, height
        )
        grad_ref[:, cut] = grad
        scaled = grad * scale
        low_ref[:, cut] = scaled.astype(bf16)
        scale_grad += jnp.sum(grad * branch_ref[:, cut], axis=1, keepdims=True)
        bias_grad += jnp.sum(scaled, axis=1, keepdims=True)
    put_columns(sums_ref, [scale_grad, bias_grad])


def tall_back(height, conv, rest, tall, fore, pack, branch):
    return pl.pallas_call(
        partial(tall_back_body, height),
        in_specs=[vmem_spec()] * 6,
        out_specs=[vmem_spec()] * 3,
        out_shape=[struct(conv.shape, f32), struct(conv.shape, bf16), struct((conv.shape[0], lane), f32)],
        name="tall_back",
        **params(10_000_000, 1_000_000),
    )(conv, rest, tall, fore, pack, branch)


def tall_norm_back_body(height, channels_all, keep_ref, near_ref, far_ref, mixed_ref, stats_ref, pack_ref, stream_ref,
                        grad_ref, tall_ref, fore_ref, conv_ref, rest_ref, low_ref, sums_ref):
    canvases = fore_ref.shape[0]
    mixed_grad, gain_grad, shift_grad = norm_backward(
        (keep_ref, near_ref, far_ref), mixed_ref, stats_ref, pack_ref, channels_all
    )
    skip = pack_ref[:, 0:1]
    low_ref[...] = mixed_grad.astype(bf16)
    rest_ref[...] = (grad_ref[...] + skip * mixed_grad).astype(bf16)
    skip_grad = jnp.sum(mixed_grad * stream_ref[...].astype(f32), axis=1, keepdims=True)
    for canvas in range(canvases):
        cut = canvas_cut(conv_ref, canvas, canvases)
        conv_ref[:, cut] = height_conv(
            low_ref[:, cut].astype(f32), tall_ref, fore_ref[canvas], -1, height
        ).astype(bf16)
    put_columns(sums_ref, [skip_grad, gain_grad, shift_grad])


def tall_norm_back(height, channels_all, grads, mixed, stats, pack, stream, grad, tall, fore):
    return pl.pallas_call(
        partial(tall_norm_back_body, height, channels_all),
        in_specs=[vmem_spec()] * 10,
        out_specs=[vmem_spec()] * 4,
        out_shape=[struct(mixed.shape, bf16)] * 3 + [struct((mixed.shape[0], lane), f32)],
        name="tall_norm_back",
        **params(10_000_000, 1_000_000),
    )(*grads, mixed, stats, pack, stream, grad, tall, fore)


def tall_kernel_grad_body(height, grad_ref, input_ref, age_ref, out_ref):
    canvases = age_ref.shape[0]
    total = jnp.zeros(out_ref.shape, f32)
    for canvas in range(canvases):
        cut = canvas_cut(grad_ref, canvas, canvases)
        total = height_products(
            grad_ref[:, cut].astype(f32), input_ref[:, cut].astype(f32), age_ref[canvas], height, total
        )
    out_ref[...] = total


def tall_kernel_grad(height, grad, inputs, age):
    return pl.pallas_call(
        partial(tall_kernel_grad_body, height),
        in_specs=[vmem_spec()] * 3,
        out_specs=vmem_spec(),
        out_shape=struct((grad.shape[0], lane), f32),
        name="tall_kernel_grad",
        **params(10_000_000, 1_000_000),
    )(grad, inputs, age)


root = 0.7978845608028654
cubic = 0.044715


def gather_into(me_ref, parts, whole_ref):
    me = me_ref[0]
    for flip, part in enumerate(parts):
        whole_ref[me ^ flip] = part[...]


def scatter_out(me_ref, whole_ref, outs):
    me = me_ref[0]
    for flip, out in zip((3, 1, 2, 0), outs, strict=True):
        out[...] = whole_ref[me ^ flip]


def mlp_forward(me_ref, parts, full_ref, shape_ref, weight_in_ref, bias_ref, normed_ref, hidden_ref, slope_ref, stats_ref):
    gather_into(me_ref, parts, full_ref)
    mixed = full_ref[...].astype(f32).reshape(-1, full_ref.shape[2])
    average = jnp.mean(mixed, axis=0, keepdims=True)
    moved = mixed - average
    inverse = lax.rsqrt(jnp.mean(moved * moved, axis=0, keepdims=True) + epsilon)
    centred = moved * inverse
    stats_ref[0:1, :] = average
    stats_ref[1:2, :] = inverse
    normed = (centred * shape_ref[:, 0:1] + shape_ref[:, 1:2]).astype(bf16)
    normed_ref[...] = normed
    before = dot(weight_in_ref[0], normed, 0, 0) + bias_ref[...]
    square = before * before
    bend = jnp.tanh(root * before * (1.0 + cubic * square))
    half = 0.5 * (1.0 + bend)
    hidden_ref[...] = (before * half).astype(bf16)
    slope_ref[...] = (half + 0.5 * before * (1.0 - bend * bend) * root * (1.0 + 3.0 * cubic * square)).astype(slope_ref.dtype)
    return centred


def mlp_first_body(me_ref, own, near, far, cross, shape_ref, weight_in_ref, bias_ref, weight_out_ref,
                   send_far, send_own, keep_far, keep_own, normed_ref, hidden_ref, slope_ref, stats_ref, full_ref, sum_ref):
    mlp_forward(me_ref, (own, near, far, cross), full_ref, shape_ref, weight_in_ref, bias_ref,
                normed_ref, hidden_ref, slope_ref, stats_ref)
    partial_out = dot(weight_out_ref[0], hidden_ref[...], 0, 0)
    sum_ref[...] = partial_out.astype(bf16).reshape(sum_ref.shape)
    scatter_out(me_ref, sum_ref, (send_far, send_own, keep_far, keep_own))


def mlp_backward(me_ref, parts, full_ref, weight_out_ref, weight_in_ref, normed_ref, hidden_ref, slope, shape_ref, centred,
                 sum_ref, outs, in_grad_ref, out_grad_ref, bias_grad_ref, in_total, out_total):
    step, last = pl.program_id(0), pl.num_programs(0) - 1
    gather_into(me_ref, parts, full_ref)
    grad = full_ref[...].reshape(-1, full_ref.shape[2])
    before_grad = (dot(weight_out_ref[0], grad, 1, 0) * slope).astype(bf16)
    normed_part = dot(weight_in_ref[0], before_grad, 1, 0)
    channels = sum_ref.shape[1] - 16
    scaled = normed_part * shape_ref[:, 0:1]
    scaled_sum = jnp.sum(scaled, axis=0, keepdims=True)
    paired_sum = jnp.sum(scaled * centred, axis=0, keepdims=True)
    places = lax.broadcasted_iota(jnp.int32, (16, grad.shape[1]), 0)
    tail = jnp.where(places == 0, scaled_sum, jnp.where(places == 1, paired_sum, 0.0)).astype(bf16)
    for index in range(sum_ref.shape[0]):
        sum_ref[index, 0:channels, :] = normed_part[index * channels:(index + 1) * channels].astype(bf16)
        sum_ref[index, channels:, :] = tail
    scatter_out(me_ref, sum_ref, outs)
    bias = jnp.sum(before_grad.astype(f32), axis=1, keepdims=True)
    in_part = dot(normed_ref[...], before_grad, 1, 1)
    out_part = dot(hidden_ref[...], grad, 1, 1)

    @pl.when(step == 0)
    def _():
        bias_grad_ref[...] = jnp.broadcast_to(bias, bias_grad_ref.shape)
        in_total[...] = in_part
        out_total[...] = out_part

    @pl.when(step > 0)
    def _():
        bias_grad_ref[...] += jnp.broadcast_to(bias, bias_grad_ref.shape)
        in_total[...] += in_part
        out_total[...] += out_part

    @pl.when(step == last)
    def _():
        in_grad_ref[...] = in_total[...].astype(bf16)
        out_grad_ref[...] = out_total[...].astype(bf16)


def mlp_both_body(me_ref, own, near, far, cross, grad_own, grad_near, grad_far, grad_cross, shape_ref, weight_in_ref,
                  bias_ref, weight_out_ref,
                  out_sf, out_so, out_kf, out_ko, back_sf, back_so, back_kf, back_ko, stats_ref,
                  in_grad_ref, out_grad_ref, bias_grad_ref,
                  full_ref, sum_ref, back_ref, normed_ref, hidden_ref, slope_ref, in_total, out_total):
    centred = mlp_forward(me_ref, (own, near, far, cross), full_ref, shape_ref, weight_in_ref, bias_ref,
                          normed_ref, hidden_ref, slope_ref, stats_ref)
    sum_ref[...] = dot(weight_out_ref[0], hidden_ref[...], 0, 0).astype(bf16).reshape(sum_ref.shape)
    scatter_out(me_ref, sum_ref, (out_sf, out_so, out_kf, out_ko))
    mlp_backward(me_ref, (grad_own, grad_near, grad_far, grad_cross), full_ref, weight_out_ref, weight_in_ref,
                 normed_ref, hidden_ref, slope_ref[...], shape_ref, centred, back_ref,
                 (back_sf, back_so, back_kf, back_ko), in_grad_ref, out_grad_ref, bias_grad_ref, in_total, out_total)


def mlp_back_body(me_ref, own, near, far, cross, grad_own, grad_near, grad_far, grad_cross, shape_ref, weight_in_ref,
                  weight_out_ref, normed_ref, hidden_ref, slope_ref, stats_ref,
                  back_sf, back_so, back_kf, back_ko, in_grad_ref, out_grad_ref, bias_grad_ref,
                  full_ref, back_ref, in_total, out_total):
    gather_into(me_ref, (own, near, far, cross), full_ref)
    centred = (full_ref[...].astype(f32).reshape(-1, full_ref.shape[2]) - stats_ref[0:1, :]) * stats_ref[1:2, :]
    mlp_backward(me_ref, (grad_own, grad_near, grad_far, grad_cross), full_ref, weight_out_ref, weight_in_ref,
                 normed_ref, hidden_ref, slope_ref[...], shape_ref, centred, back_ref,
                 (back_sf, back_so, back_kf, back_ko), in_grad_ref, out_grad_ref, bias_grad_ref, in_total, out_total)


tile = 256


def pixel_block(rows):
    return pl.BlockSpec((rows, tile), lambda i: (0, i))


def fixed_block(shape):
    return pl.BlockSpec(shape, lambda i: (0,) * len(shape))


def section_block(section, shape):
    return pl.BlockSpec((1,) + shape, lambda i: (section, 0, 0))


def mlp_first(section, me, parts, shaping, weight_in, bias, weight_out):
    own = parts[0]
    channels, pixels = own.shape
    wide, units = weight_in.shape[1], weight_in.shape[2]
    piece = pixel_block(channels)
    return pl.pallas_call(
        mlp_first_body,
        grid=(pixels // tile,),
        in_specs=[smem_spec()] + [piece] * 4 + [
            fixed_block(shaping.shape), section_block(section, (wide, units)), fixed_block(bias.shape),
            section_block(section, (units, wide)),
        ],
        out_specs=[piece] * 4 + [pixel_block(wide), pixel_block(units), pixel_block(units), pixel_block(8)],
        out_shape=[struct(own.shape, bf16)] * 4 + [
            struct((wide, pixels), bf16), struct((units, pixels), bf16), struct((units, pixels), f32), struct((8, pixels), f32),
        ],
        scratch_shapes=[pltpu.VMEM((4, channels, tile), bf16), pltpu.VMEM((4, channels, tile), bf16)],
        name="mlp_first",
        **params(1_300_000_000, 6_000_000),
    )(me, *parts, shaping, weight_in, bias, weight_out)


def mlp_both(section, me, parts, grads, shaping, weight_in, bias, weight_out):
    own = parts[0]
    channels, pixels = own.shape
    wide, units = weight_in.shape[1], weight_in.shape[2]
    piece, back = pixel_block(channels), pixel_block(channels + 16)
    return pl.pallas_call(
        mlp_both_body,
        grid=(pixels // tile,),
        in_specs=[smem_spec()] + [piece] * 8 + [
            fixed_block(shaping.shape), section_block(section, (wide, units)), fixed_block(bias.shape),
            section_block(section, (units, wide)),
        ],
        out_specs=[piece] * 4 + [back] * 4 + [
            pixel_block(8), fixed_block((wide, units)), fixed_block((units, wide)), fixed_block((units, lane)),
        ],
        out_shape=[struct(own.shape, bf16)] * 4 + [struct((channels + 16, pixels), bf16)] * 4 + [
            struct((8, pixels), f32), struct((wide, units), bf16), struct((units, wide), bf16), struct((units, lane), f32),
        ],
        scratch_shapes=[
            pltpu.VMEM((4, channels, tile), bf16), pltpu.VMEM((4, channels, tile), bf16),
            pltpu.VMEM((4, channels + 16, tile), bf16), pltpu.VMEM((wide, tile), bf16),
            pltpu.VMEM((units, tile), bf16), pltpu.VMEM((units, tile), f32),
            pltpu.VMEM((wide, units), f32), pltpu.VMEM((units, wide), f32),
        ],
        name="mlp_both",
        **params(3_600_000_000, 9_000_000),
    )(me, *parts, *grads, shaping, weight_in, bias, weight_out)


def mlp_back(section, me, parts, grads, shaping, weight_in, weight_out, normed, hidden, slope, stats):
    own = parts[0]
    channels, pixels = own.shape
    wide, units = weight_in.shape[1], weight_in.shape[2]
    piece, back = pixel_block(channels), pixel_block(channels + 16)
    return pl.pallas_call(
        mlp_back_body,
        grid=(pixels // tile,),
        in_specs=[smem_spec()] + [piece] * 8 + [
            fixed_block(shaping.shape), section_block(section, (wide, units)), section_block(section, (units, wide)),
            pixel_block(wide), pixel_block(units), pixel_block(units), pixel_block(8),
        ],
        out_specs=[back] * 4 + [fixed_block((wide, units)), fixed_block((units, wide)), fixed_block((units, lane))],
        out_shape=[struct((channels + 16, pixels), bf16)] * 4 + [
            struct((wide, units), bf16), struct((units, wide), bf16), struct((units, lane), f32),
        ],
        scratch_shapes=[
            pltpu.VMEM((4, channels, tile), bf16), pltpu.VMEM((4, channels + 16, tile), bf16),
            pltpu.VMEM((wide, units), f32), pltpu.VMEM((units, wide), f32),
        ],
        name="mlp_back",
        **params(2_400_000_000, 9_000_000),
    )(me, *parts, *grads, shaping, weight_in, weight_out, normed, hidden, slope, stats)


core_pairs = [(i, i ^ 1) for i in range(4)]
chip_pairs = [(i, i ^ 2) for i in range(4)]


def gather_channels(own):
    far = lax.ppermute(own, "ch", chip_pairs)
    near = lax.ppermute(own, "ch", core_pairs)
    cross = lax.ppermute(far, "ch", core_pairs)
    return (own, near, far, cross)


def scatter_channels(send_far, send_own, keep_far, keep_own):
    near_far = lax.ppermute(send_far, "ch", core_pairs)
    near_own = lax.ppermute(send_own, "ch", core_pairs)
    onward = (keep_far.astype(f32) + near_far.astype(f32)).astype(bf16)
    far = lax.ppermute(onward, "ch", chip_pairs)
    return (keep_own, near_own, far)


def rows_to_cols(parts, count):
    pieces = []
    for part in parts:
        canvases, rows, channels, width = part.shape
        cut = part.reshape(canvases, rows, channels, count, width // count)
        pieces.append(cut.transpose(3, 2, 0, 1, 4).reshape(count, channels, -1))
    moved = lax.all_to_all(jnp.stack(pieces, axis=1), "rows", split_axis=0, concat_axis=0, tiled=True)
    moved = moved.reshape(count, len(parts), channels, canvases, rows, width // count)
    return [moved[:, k].transpose(1, 2, 0, 3, 4).reshape(channels, -1) for k in range(len(parts))]


def cols_to_rows(parts, count, canvases, rows, width):
    channels = parts[0].shape[0]
    pieces = []
    for part in parts:
        cut = part.reshape(channels, canvases, count, rows, width // count)
        pieces.append(cut.transpose(2, 0, 1, 3, 4).reshape(count, channels, -1))
    moved = lax.all_to_all(jnp.stack(pieces, axis=1), "rows", split_axis=0, concat_axis=0, tiled=True)
    moved = moved.reshape(count, len(parts), channels, canvases, rows, width // count)
    return [moved[:, k].transpose(2, 3, 1, 0, 4).reshape(canvases, rows, channels, width) for k in range(len(parts))]


def crop_reach(starts):
    count = starts.shape[1]
    places = jnp.arange(count, dtype=jnp.int32)[None, :]
    first = lax.cummax(jnp.where(starts > 0, places, 0), axis=1)
    following = lax.cummin(jnp.where(starts > 0, places, count), axis=1, reverse=True)
    following = jnp.concatenate([following[:, 1:], jnp.full((starts.shape[0], 1), count, jnp.int32)], axis=1)
    return places - first, following - 1 - places


def band_turns(age):
    return jnp.max(age.reshape(age.shape[0], -1, band), axis=2) // ahead + 1


def on_device(
    count,
    pixels,
    row_starts,
    col_starts,
    log_step,
    log_decay,
    frequency,
    coef_real,
    coef_imag,
    skip_gain,
    norm_gain,
    norm_shift,
    weight_in,
    bias_in,
    weight_out,
    bias_out,
    layer_scale,
    cotangent,
):
    canvases, rows, width, channels = pixels.shape
    height = row_starts.shape[1]
    channels_all = weight_in.shape[1]
    lengths = (height, width)
    me = lax.axis_index("ch").astype(jnp.int32).reshape(1)

    stream = jnp.swapaxes(pixels, 2, 3)
    upstream = jnp.swapaxes(cotangent, 2, 3)
    states = [jnp.swapaxes(value, 2, 3) for value in (log_decay, frequency, coef_real, coef_imag)]

    age, fore = crop_reach(col_starts)
    age_reach, fore_reach = band_turns(age), band_turns(fore)
    age = jnp.broadcast_to(age[:, :, None], (canvases, width, lane))
    fore = jnp.broadcast_to(fore[:, :, None], (canvases, width, lane))
    row_age, row_fore = crop_reach(row_starts)
    row_age = jnp.repeat(row_age, width // count, axis=1)[:, None, :]
    row_fore = jnp.repeat(row_fore, width // count, axis=1)[:, None, :]

    packs = [
        jnp.stack([skip_gain[k], norm_gain[k], norm_shift[k], bias_out[k], layer_scale[k]], axis=1) for k in range(2)
    ]
    shaping_all = lax.all_gather(jnp.stack([norm_gain, norm_shift], axis=2), "ch", axis=1, tiled=True)
    bias_columns = [bias_in[k][:, None] for k in range(2)]

    top_scaled = upstream.astype(f32) * packs[1][:, 4:5]
    top_low = top_scaled.astype(bf16).transpose(2, 0, 1, 3).reshape(channels, -1)
    top_parts = gather_channels(top_low)
    top_bias_grad = jnp.sum(top_scaled, axis=(0, 1, 3))

    tall, wide = zip(
        *[s4_kernels(k, lengths, log_step, *states, rows) for k in range(2)], strict=True
    )

    across = wide_forward(stream, wide[0], age, age_reach)
    across_cols, stream_cols = rows_to_cols([across, stream], count)
    mixed_low = tall_mixed(height, across_cols, stream_cols, tall[0], row_age, packs[0])
    low_parts = gather_channels(mixed_low)
    first = mlp_first(0, me, low_parts, shaping_all[0], weight_in, bias_columns[0], weight_out)
    normed_low, hidden_low, slope_low, stats_low = first[4:]
    branches = scatter_channels(*first[:4])

    next_cols, branch_cols, tall_cols = tall_next(height, branches, stream_cols, packs[0], tall[1], row_age)
    tall_rows, next_rows = cols_to_rows([tall_cols, next_cols], count, canvases, rows, width)
    mixed_top = wide_mixed(tall_rows, next_rows, wide[1], age, age_reach, packs[1])
    top_mixed_parts = gather_channels(mixed_top)
    both = mlp_both(1, me, top_mixed_parts, top_parts, shaping_all[1], weight_in, bias_columns[1], weight_out)
    stats_top, top_in_grad, top_out_grad, top_bias_in = both[8:]
    top_grads = scatter_channels(*both[4:8])
    top_weights = lax.psum((top_in_grad, top_out_grad), "rows")

    conv_rows, rest_rows, grad_rows, top_sums = wide_norm_back(
        channels_all, top_grads, mixed_top, stats_top, packs[1], next_rows, upstream, wide[1], fore, fore_reach
    )
    conv_cols, rest_cols = rows_to_cols([conv_rows, rest_rows], count)
    grad_cols, grad_low, low_branch_sums = tall_back(height, conv_cols, rest_cols, tall[1], row_fore, packs[0], branch_cols)

    grad_parts = gather_channels(grad_low)
    back = mlp_back(
        0, me, low_parts, grad_parts, shaping_all[0], weight_in, weight_out, normed_low, hidden_low, slope_low, stats_low
    )
    low_in_grad, low_out_grad, low_bias_in = back[4:]
    low_grads = scatter_channels(*back[:4])
    low_conv_cols, low_rest_cols, low_grad_cols, low_sums = tall_norm_back(
        height, channels_all, low_grads, mixed_low, stats_low, packs[0], stream_cols, grad_cols, tall[0], row_fore
    )
    low_weights = lax.psum((low_in_grad, low_out_grad), "rows")
    low_conv_rows, low_rest_rows = cols_to_rows([low_conv_cols, low_rest_cols], count, canvases, rows, width)
    pixels_grad = wide_back(low_conv_rows, low_rest_rows, wide[0], fore, fore_reach)

    top_branches = scatter_channels(*both[:4])
    branch_top = sum(part.astype(f32) for part in top_branches) + packs[1][:, 3:4]
    branch_top = branch_top.reshape(channels, canvases, rows, width).transpose(1, 2, 0, 3)
    activations = (next_rows.astype(f32) + packs[1][:, 4:5] * branch_top).astype(bf16)
    top_scale_grad = jnp.sum(upstream.astype(f32) * branch_top, axis=(0, 1, 3))

    top_tall = tall_kernel_grad(height, conv_cols, next_cols, row_age)
    top_wide = wide_kernel_grad(grad_rows, tall_rows, age, age_reach)
    low_tall = tall_kernel_grad(height, low_grad_cols, across_cols, row_age)
    low_wide = wide_kernel_grad(low_conv_rows, stream, age, age_reach)
    tall_grads = jnp.stack([low_tall, top_tall])
    wide_grads = jnp.stack([low_wide, top_wide])
    columns = jnp.stack(
        [
            jnp.concatenate([low_sums[:, 0:3], low_branch_sums[:, 1:2], low_branch_sums[:, 0:1]], axis=1),
            jnp.concatenate([top_sums[:, 0:3], top_bias_grad[:, None], top_scale_grad[:, None]], axis=1),
        ]
    )
    bias_grads = jnp.stack([low_bias_in[:, 0], top_bias_in[:, 0]])
    tall_grads, wide_grads, columns, bias_grads = lax.psum((tall_grads, wide_grads, columns, bias_grads), "rows")
    step_grad, decay_grad, freq_grad, real_grad, imag_grad = s4_pullback(
        lengths, tall_grads, wide_grads, log_step, *states
    )
    return (
        jnp.swapaxes(activations, 2, 3),
        jnp.swapaxes(pixels_grad, 2, 3),
        step_grad,
        jnp.swapaxes(decay_grad, 2, 3),
        jnp.swapaxes(freq_grad, 2, 3),
        jnp.swapaxes(real_grad, 2, 3),
        jnp.swapaxes(imag_grad, 2, 3),
        columns[:, :, 0],
        columns[:, :, 1],
        columns[:, :, 2],
        jnp.stack([low_weights[0], top_weights[0]]).astype(f32),
        bias_grads,
        jnp.stack([low_weights[1], top_weights[1]]).astype(f32),
        columns[:, :, 3],
        columns[:, :, 4],
    )


def solution(mesh):
    picture = P(None, "rows", None, "ch")
    state = P(None, None, "ch", None)
    step = P(None, None, "ch")
    vector = P(None, "ch")
    into = P(None, None, "ch")
    out = P(None, "ch", None)
    in_specs = (
        picture, P(), P(), step, state, state, state, state, vector, vector, vector, into, vector, out, vector, vector, picture,
    )
    out_specs = (
        picture, picture, step, state, state, state, state, vector, vector, vector, into, vector, out, vector, vector,
    )
    return jax.shard_map(
        partial(on_device, mesh.shape["rows"]), mesh=mesh, in_specs=in_specs, out_specs=out_specs, check_vma=False
    )
```

time: 1430 us -> 512 us (0.36); the launches traced: 1400 us -> 502 us
  local copies, waits for them, and re-layouts: 583 us -> 32.5 us
  other arithmetic: 215 us -> 19.8 us
  matrix products: 138 us -> 0 us
  Pallas kernels: 0 us -> 102 us
  waiting for transfers between devices: 305 us -> 249 us
  blocking collectives: 100 us -> 46.2 us
    reshape x68 -> x11, local copies, waits for them, and re-layouts: 221 us -> 6.9 us  [the longest x4 3.28 us: cols_to_rows(): moved[:, k].transpose(2, 3, 1, 0, 4)]
    rev x60 -> x0, local copies, waits for them, and re-layouts: 184 us -> none  [the longest x24 181 us: diagonal_sums(): turned = products[:, :, ::-1]]
    reduce_sum x41 -> x1, other arithmetic: 177 us -> 0.85 us  [on_device(): top_bias_grad = jnp.sum(top_scaled, axis=(0, 1, 3))]
    dot_general x132 -> x0, matrix products: 138 us -> none  [the longest x48 40.4 us: forward_conv(): jnp.einsum(patterns[0], masked, inputs[canvas, :, :, offset:offset + stri...]
    pallas_call x0 -> x18, Pallas kernels: none -> 102 us  [the longest x1 11.3 us: mlp_both(): pl.pallas_call(mlp_both_body, grid=(pixels // tile,), in_specs=[smem_spec...]
    psum x1 -> x2, waiting for transfers between devices: 277 us -> 181 us  [the longest x1 164 us: on_device(): top_weights = lax.psum((top_in_grad, top_out_grad), 'rows')]
    unnamed x558 -> x84, local copies, waits for them, and re-layouts: 98.2 us -> 3.84 us
    slice x66 -> x10, local copies, waits for them, and re-layouts: 42.7 us -> 0.9 us  [the longest x2 0.35 us: on_device(): bias_grads = jnp.stack([low_bias_in[:, 0], top_bias_in[:, 0]])]
  transfers between devices with their start and end apart: 13 -> 30, of which waited for: 6 -> 17; matrix products, arithmetic and copies ran while one was open for 26% -> 4% of each run, Pallas kernels for 0% -> 8%
where the time goes in v1:
time: 512 us; the launch traced here: 502 us
  waiting for transfers between devices  249 us (49%)
  Pallas kernels  102 us (20%)
  blocking collectives  46.2 us (9%)
  starting transfers between devices  37 us (7%)
  local copies, waits for them, and re-layouts  32.5 us (6%)
  other arithmetic  19.8 us (4%)
  between operations  15.3 us (3%)
    psum x1, waiting for transfers between devices, on_device(): top_weights = lax.psum((top_in_grad, top_out_grad), 'rows')  164 us
    psum x1, blocking collectives, on_device(): lax.psum((tall_grads, wide_grads, columns, bias_grads), 'rows')  38.1 us
    all_to_all x2, waiting for transfers between devices, rows_to_cols(): lax.all_to_all(jnp.stack(pieces, axis=1), 'rows', split_axis=0, concat_ax...  25.7 us
    ppermute x4, waiting for transfers between devices, scatter_channels(): far = lax.ppermute(onward, 'ch', chip_pairs)  17.1 us
    psum x1, waiting for transfers between devices, on_device(): lax.psum((tall_grads, wide_grads, columns, bias_grads), 'rows')  17.1 us
    all_to_all x2, starting transfers between devices, rows_to_cols(): lax.all_to_all(jnp.stack(pieces, axis=1), 'rows', split_axis=0, concat_ax...  12.1 us
    all_to_all x2, waiting for transfers between devices, cols_to_rows(): lax.all_to_all(jnp.stack(pieces, axis=1), 'rows', split_axis=0, concat_ax...  11.4 us
    pallas_call x1, Pallas kernels, mlp_both(): pl.pallas_call(mlp_both_body, grid=(pixels // tile,), in_specs=[smem_spec...  11.3 us
  transfers between devices with their start and end apart: 30, of which 17 were waited for; matrix products, arithmetic and copies ran while one was open for 4% of the time, Pallas kernels for 8%

profile of v1, /device:TPU:0, one launch (start us, length us, event | category | flops | bytes accessed | tf_op | source)
XLA Modules:
  0.0 502.5 jit_solution(13781595017933111047)
XLA Ops:
  10.1 4.8 s4_kernels.2
  15.6 4.6 wide_forward.1
  22.3 7.3 %all-to-all-start = ((bf16[8,2,192,64]{2,3,1,0:T(8,128)(2,1)}), bf16[8,2,192,64]{2,3,1,0:T(8,128)(2,1)S(1)}, u32[]{:S(2)}, u32[]{:S(2)}) async-start(bf16[8,2,192,64]{2,3,1,0:T(8,128)(2,1)} %copy.162), calls=%async_computation | async-start | bytes 1048576 | tf_op jit(solution)/shard_map/all_to_all | solution.py:863
  31.4 12.7 %all-to-all-done = bf16[8,2,192,64]{2,3,1,0:T(8,128)(2,1)S(1)} async-done(((bf16[8,2,192,64]{2,3,1,0:T(8,128)(2,1)}), bf16[8,2,192,64]{2,3,1,0:T(8,128)(2,1)S(1)}, u32[]{:S(2)}, u32[]{:S(2)}) %all-to-all-start) | async-done | bytes 393248 | tf_op jit(solution)/shard_map/all_to_all | solution.py:863
  45.8 3.5 tall_mixed.1.own.mixed_ref
  49.3 1.5 collective-permute-start.1
  52.2 8.1 %all_gather.3 = f32[2,768,2]{2,1,0:T(8,128)S(1)} all-gather(f32[2,192,2]{2,1,0:T(8,128)S(1)} %pad_maximum_fusion.4), channel_id=1, replica_groups=mesh['rows'=8,'ch'=4] {'ch'}, dimensions={1}, use_global_device_ids=true | all-gather | bytes 15360 | tf_op jit(solution)/shard_map/all_gather | solution.py:933
  62.8 6.7 %mlp_first.1 = (bf16[192,512]{1,0:T(8,128)(2,1)}, bf16[192,512]{1,0:T(8,128)(2,1)}, bf16[192,512]{1,0:T(8,128)(2,1)}, bf16[192,512]{1,0:T(8,128)(2,1)}, bf16[768...) custom-call(s32[1]{0:T(128)} %bitcast.me_ref, ...), custom_call_target="tpu_custom_call" | custom-call | flops 1300000000 | bytes 6000000 | tf_op jit(solution)/shard_map/mlp_first/pallas_call | solution.py:767
  72.2 1.6 collective-permute-start.5
  73.8 4.8 s4_kernels.3
  80.0 3.7 tall_next.1
  86.9 4.9 all-to-all-start.1
  92.3 1.6 collective-permute-start.10
  94.7 11.4 %all-to-all-done.1 = bf16[8,2,192,64]{2,3,1,0:T(8,128)(2,1)S(1)} async-done(((bf16[8,2,192,64]{2,3,1,0:T(8,128)(2,1)}), bf16[8,2,192,64]{2,3,1,0:T(8,128)(2,1)S(1)}, u32[]{:S(2)}, u32[]{:S(2)}) %all-to-all-start.1) | async-done | bytes 393248 | tf_op jit(solution)/shard_map/all_to_all | solution.py:874
  107.8 4.8 wide_mixed.1.own.mixed_ref
  112.6 1.5 collective-permute-start.7
  114.7 3.8 collective-permute-done.7.far
  120.6 11.3 %mlp_both.1 = (bf16[192,512]{1,0:T(8,128)(2,1)}, bf16[192,512]{1,0:T(8,128)(2,1)}, bf16[192,512]{1,0:T(8,128)(2,1)}, bf16[192,512]{1,0:T(8,128)(2,1)}, bf16[208,...) custom-call(s32[1]{0:T(128)} %bitcast.me_ref, ...), custom_call_target="tpu_custom_call" | custom-call | flops 3600000000 | bytes 9000000 | tf_op jit(solution)/shard_map/mlp_both/pallas_call | solution.py:789
  132.2 2.3 reduce_window_min.20
  136.2 1.5 collective-permute-start.17
  138.3 5.3 %collective-permute-done.17.far_ref = bf16[208,512]{1,0:T(8,128)(2,1)S(1)} collective-permute-done((bf16[208,512]{1,0:T(8,128)(2,1)S(1)}, bf16[208,512]{1,0:T(8,128)(2,1)S(1)}, u32[]{:S(2)}, u32[]{:S(2)}) %collective-permute-start.17) | collective-permute-done | bytes 213024 | tf_op jit(solution)/shard_map/ppermute | solution.py:853
  144.4 5.7 %wide_norm_back.1 = (bf16[2,2,192,128]{3,2,1,0:T(8,128)(2,1)}, bf16[2,2,192,128]{3,2,1,0:T(8,128)(2,1)}, bf16[2,2,192,128]{3,2,1,0:T(8,128)(2,1)}, f32[192,128]{1,0:T(8,128)}) custom-call(bf16[208,512]{1,0:T(8,128)(2,1)} %get-tuple-element.79.keep_ref, bf16[208,512]{1,0:T(8,128)(2,1)} %copy-done.15, bf16[208,512]{1,0:T(8,128)(2,1)} %copy-done.16, ...), custom_call_target="tpu_custom_call" | custom-call | flops 30000000 | bytes 2000000 | tf_op jit(solution)/shard_map/wide_norm_back/pallas_call | solution.py:407
  153.2 4.8 all-to-all-start.2
  159.0 13.0 %all-to-all-done.2 = bf16[8,2,192,64]{2,3,1,0:T(8,128)(2,1)S(1)} async-done(((bf16[8,2,192,64]{2,3,1,0:T(8,128)(2,1)}), bf16[8,2,192,64]{2,3,1,0:T(8,128)(2,1)S(1)}, u32[]{:S(2)}, u32[]{:S(2)}) %all-to-all-start.2) | async-done | bytes 393248 | tf_op jit(solution)/shard_map/all_to_all | solution.py:863
  173.7 3.9 tall_back.1
  177.6 1.5 collective-permute-start.19
  179.1 4.4 collective-permute-done.19.grad_far
  183.5 1.4 collective-permute-done.20.grad_cross
  185.7 9.8 %mlp_back.1 = (bf16[208,512]{1,0:T(8,128)(2,1)}, bf16[208,512]{1,0:T(8,128)(2,1)}, bf16[208,512]{1,0:T(8,128)(2,1)}, bf16[208,512]{1,0:T(8,128)(2,1)}, bf16[768,...) custom-call(s32[1]{0:T(128)} %bitcast.me_ref, bf16[192,512]{1,0:T(8,128)(2,1)} %tall_mixed.1.own.mixed_ref, ...), custom_call_target="tpu_custom_call" | custom-call | flops 2400000000 | bytes 9000000 | tf_op jit(solution)/shard_map/mlp_back/pallas_call | solution.py:818
  198.2 1.6 collective-permute-start.23
  199.8 5.8 %collective-permute-done.23.far_ref = bf16[208,512]{1,0:T(8,128)(2,1)S(1)} collective-permute-done((bf16[208,512]{1,0:T(8,128)(2,1)S(1)}, bf16[208,512]{1,0:T(8,128)(2,1)S(1)}, u32[]{:S(2)}, u32[]{:S(2)}) %collective-permute-start.23) | collective-permute-done | bytes 213024 | tf_op jit(solution)/shard_map/ppermute | solution.py:853
  206.3 4.1 tall_norm_back.1
  213.5 4.4 all-to-all-start.3
  218.0 5.3 %wide_kernel_grad.3 = f32[192,128]{1,0:T(8,128)} custom-call(bf16[2,2,192,128]{3,2,1,0:T(8,128)(2,1)} %get-tuple-element.100.grad_ref, bf16[2,2,192,128]{3,2,1,0:T(8,128)(2,1)} %copy.181.tall_ref.input_ref, s32[2,128,128]{2,1,0:T(8,128)} %broadcast_in_dim.54.age_ref, s32[2,8]{1,0:T(2,128)} %fusion.7.reach_ref), custom_call_target="tpu_custom_call" | custom-call | flops 30000000 | bytes 2000000 | tf_op jit(solution)/shard_map/wide_kernel_grad/pallas_call | solution.py:460
  223.3 4.0 tall_kernel_grad.3
  227.3 4.0 tall_kernel_grad.2
  231.3 1.7 pad_maximum_fusion.5
  233.9 5.0 %wide_kernel_grad.2 = f32[192,128]{1,0:T(8,128)} custom-call(bf16[2,2,192,128]{3,2,1,0:T(8,128)(2,1)} %copy.208.grad_ref, bf16[2,2,192,128]{3,2,1,0:T(8,128)(2,1)} %bitcast.179, s32[2,128,128]{2,1,0:T(8,128)} %broadcast_in_dim.54.age_ref, s32[2,8]{1,0:T(2,128)} %fusion.7.reach_ref), custom_call_target="tpu_custom_call" | custom-call | flops 30000000 | bytes 2000000 | tf_op jit(solution)/shard_map/wide_kernel_grad/pallas_call | solution.py:460
  238.9 1.6 pad_maximum_fusion.6
  243.0 1.6 collective-permute-start.14
  244.8 5.2 %collective-permute-done.14 = bf16[192,512]{1,0:T(8,128)(2,1)S(1)} collective-permute-done((bf16[192,512]{1,0:T(8,128)(2,1)S(1)}, bf16[192,512]{1,0:T(8,128)(2,1)S(1)}, u32[]{:S(2)}, u32[]{:S(2)}) %collective-permute-start.14) | collective-permute-done | bytes 196640 | tf_op jit(solution)/shard_map/ppermute | solution.py:853
  252.0 38.1 %all-reduce.2 = (f32[2,192,5]{1,0,2:T(2,128)S(1)}, f32[2,768]{1,0:T(2,128)}) all-reduce(f32[2,192,5]{1,0,2:T(2,128)S(1)} %pad_maximum_fusion.7, f32[2,768]{1,0:T(2,128)S(1)} %pad_maximum_fusion.8), channel_id=1, replica_groups=mesh['rows'=8,'ch'=4] {'rows'}, use_global_device_ids=true, to_apply=%region_10.11 | all-reduce | flops 3456 | bytes 27648 | tf_op jit(solution)/shard_map/psum | solution.py:1000
  291.6 4.9 wide_back.1
  296.4 17.1 %all-reduce.8.cloned.1.call-done = (f32[2,192,128]{2,1,0:T(8,128)}, f32[2,192,128]{2,1,0:T(8,128)}) async-done(((f32[2,192,128]{2,1,0:T(8,128)}, f32[2,192,128]{2,1,0:T(8,128)}), (f32[2,192,128]{2,1,0:T(8,128)}, f32[2,192,128]{2,1,0:T(8,128)})) %all-reduce.8.cloned.1.call-update) | async-done | bytes 393232 | tf_op jit(solution)/shard_map/psum | solution.py:1000
  313.5 11.0 %s4_pullback.1 = (f32[2,2,192]{2,1,0:T(2,128)}, f32[2,2,64,192]{3,2,1,0:T(8,128)}, f32[2,2,64,192]{3,2,1,0:T(8,128)}, f32[2,2,64,192]{3,2,1,0:T(8,128)}, f32[2,2,64,192]{3,2,1,0:T(8,128)}) custom-call(f32[2,192,128]{2,1,0:T(8,128)} %get-tuple-element.119.tall_ref, f32[2,192,128]{2,1,0:T(8,128)} %get-tuple-element.120.wide_ref, f32[2,2,192]{2,1,0:T(2,128)} %step_ref.5, ...), custom_call_target="tpu_custom_call" | custom-call | flops 100000000 | bytes 2000000 | tf_op jit(solution)/shard_map/s4_pullback/pallas_call | solution.py:200
  324.6 163.8 %all-reduce.10.cloned.1.call-done = (bf16[1,768,768]{2,1,0:T(8,128)(2,1)}, bf16[1,768,768]{2,1,0:T(8,128)(2,1)}, bf16[1,768,768]{2,1,0:T(8,128)(2,1)}, bf16[1,768,768]{2,1,0:T(8,128)(2,1)}) async-done(((bf16[1,768,768]{2,1,0:T(8,128)(2,1)}, bf16[1,768,768]{2,1,0:T(8,128)(2,1)}, bf16[1,768,768]{2,1,0:T(8,128)(2,1)}, bf16[1,768,768]{2,1,0:T(8,128)(2,1)}), (bf16[1,768,768]{2,1,0:T(8,128)(2,1)}, ...) | async-done | bytes 4718608 | tf_op jit(solution)/shard_map/psum | solution.py:960
  488.4 4.3 maximum_convert_fusion
  492.7 2.5 maximum_convert_fusion.1
  (231 shorter events, 48.8 us)
Async XLA Ops:
  21.3 8.3 %copy-start.33 = (s32[2,16]{1,0:T(2,128)S(1)}, s32[2,16]{1,0:T(2,128)}, u32[]{:S(2)}) copy-start(s32[2,16]{1,0:T(2,128)} %param.18) | copy-start | bytes 388
  21.3 9.2 %copy-start.30 = (f32[2,192]{1,0:T(2,128)S(1)}, f32[2,192]{1,0:T(2,128)}, u32[]{:S(2)}) copy-start(f32[2,192]{1,0:T(2,128)} %param.32) | copy-start | bytes 4612
  21.4 9.2 %copy-start.27 = (f32[2,192]{1,0:T(2,128)S(1)}, f32[2,192]{1,0:T(2,128)}, u32[]{:S(2)}) copy-start(f32[2,192]{1,0:T(2,128)} %param.27) | copy-start | bytes 4612
  21.4 9.2 %copy-start.28 = (f32[2,192]{1,0:T(2,128)S(1)}, f32[2,192]{1,0:T(2,128)}, u32[]{:S(2)}) copy-start(f32[2,192]{1,0:T(2,128)} %param.26) | copy-start | bytes 4612
  21.4 9.2 %copy-start.31 = (f32[2,192]{1,0:T(2,128)S(1)}, f32[2,192]{1,0:T(2,128)}, u32[]{:S(2)}) copy-start(f32[2,192]{1,0:T(2,128)} %param.25) | copy-start | bytes 4612
  21.4 9.2 %copy-start.32 = (f32[2,192]{1,0:T(2,128)S(1)}, f32[2,192]{1,0:T(2,128)}, u32[]{:S(2)}) copy-start(f32[2,192]{1,0:T(2,128)} %param.31) | copy-start | bytes 4612
  22.3 21.8 %all-to-all-start = ((bf16[8,2,192,64]{2,3,1,0:T(8,128)(2,1)}), bf16[8,2,192,64]{2,3,1,0:T(8,128)(2,1)S(1)}, u32[]{:S(2)}, u32[]{:S(2)}) async-start(bf16[8,2,192,64]{2,3,1,0:T(8,128)(2,1)} %copy.162), calls=%async_computation | async-start | bytes 1048576 | tf_op jit(solution)/shard_map/all_to_all | solution.py:863
  44.2 6.7 %copy-start.29 = (f32[2,768]{1,0:T(2,128)S(1)}, f32[2,768]{1,0:T(2,128)}, u32[]{:S(2)}) copy-start(f32[2,768]{1,0:T(2,128)} %param.29) | copy-start | bytes 18436
  49.3 11.0 %copy-start = (bf16[192,512]{1,0:T(8,128)(2,1)S(1)}, bf16[192,512]{1,0:T(8,128)(2,1)}, u32[]{:S(2)}) copy-start(bf16[192,512]{1,0:T(8,128)(2,1)} %tall_mixed.1.own.mixed_ref) | copy-start | bytes 589828
  49.3 11.3 %collective-permute-start.1 = (bf16[192,512]{1,0:T(8,128)(2,1)}, bf16[192,512]{1,0:T(8,128)(2,1)S(1)}, u32[]{:S(2)}, u32[]{:S(2)}) collective-permute-start(bf16[192,512]{1,0:T(8,128)(2,1)} %tall_mixed.1.own.mixed_ref), channel_id=1, source_target_pairs={{0,2},{1,3},{2,0},{3,1},{4,6},{5,7},{6,4},{7,5},{8,10},{9,11},{10,... | collective-permute-start | bytes 589832 | tf_op jit(solution)/shard_map/ppermute | solution.py:843
  60.3 1.5 collective-permute-start
  60.6 1.4 collective-permute-start.2
  69.5 1.7 collective-permute-start.4
  69.9 8.7 %collective-permute-start.3 = (bf16[192,512]{1,0:T(8,128)(2,1)}, bf16[192,512]{1,0:T(8,128)(2,1)S(1)}, u32[]{:S(2)}, u32[]{:S(2)}) collective-permute-start(bf16[192,512]{1,0:T(8,128)(2,1)} %get-tuple-element.68), channel_id=1, source_target_pairs={{0,1},{1,0},{2,3},{3,2},{4,5},{5,4},{6,7},{7,6},{8,9},{9,8},{10,11... | collective-permute-start | bytes 589832 | tf_op jit(solution)/shard_map/ppermute | solution.py:851
  72.2 7.1 %collective-permute-start.5 = (bf16[192,512]{1,0:T(8,128)(2,1)S(1)}, bf16[192,512]{1,0:T(8,128)(2,1)S(1)}, u32[]{:S(2)}, u32[]{:S(2)}) collective-permute-start(bf16[192,512]{1,0:T(8,128)(2,1)S(1)} %add_convert_fusion.3), channel_id=1, source_target_pairs={{0,2},{1,3},{2,0},{3,1},{4,6},{5,7},{6,4},{7,5},{8,10},{9,11},{10,... | collective-permute-start | bytes 589832 | tf_op jit(solution)/shard_map/ppermute | solution.py:853
  86.0 5.9 %copy-start.2 = (bf16[2,2,128,192]{2,3,1,0:T(8,128)(2,1)S(1)}, bf16[2,2,128,192]{2,3,1,0:T(8,128)(2,1)}, u32[]{:S(2)}) copy-start(bf16[2,2,128,192]{2,3,1,0:T(8,128)(2,1)} %param.33) | copy-start | bytes 589828
  86.9 19.1 %all-to-all-start.1 = ((bf16[8,2,192,64]{2,3,1,0:T(8,128)(2,1)}), bf16[8,2,192,64]{2,3,1,0:T(8,128)(2,1)S(1)}, u32[]{:S(2)}, u32[]{:S(2)}) async-start(bf16[8,2,192,64]{2,3,1,0:T(8,128)(2,1)} %copy.177), calls=%async_computation.1 | async-start | bytes 1048576 | tf_op jit(solution)/shard_map/all_to_all | solution.py:874
  92.3 21.8 %copy-start.17 = (bf16[192,512]{1,0:T(8,128)(2,1)}, bf16[192,512]{1,0:T(8,128)(2,1)S(1)}, u32[]{:S(2)}) copy-start(bf16[192,512]{1,0:T(8,128)(2,1)S(1)} %reshape.135.grad_own) | copy-start | bytes 589828
  92.3 21.8 %collective-permute-start.10 = (bf16[192,512]{1,0:T(8,128)(2,1)S(1)}, bf16[192,512]{1,0:T(8,128)(2,1)S(1)}, u32[]{:S(2)}, u32[]{:S(2)}) collective-permute-start(bf16[192,512]{1,0:T(8,128)(2,1)S(1)} %reshape.135.grad_own), channel_id=1, source_target_pairs={{0,2},{1,3},{2,0},{3,1},{4,6},{5,7},{6,4},{7,5},{8,10},{9,11},{10,... | collective-permute-start | bytes 589832 | tf_op jit(solution)/shard_map/ppermute | solution.py:843
  112.6 5.9 %collective-permute-start.7 = (bf16[192,512]{1,0:T(8,128)(2,1)}, bf16[192,512]{1,0:T(8,128)(2,1)S(1)}, u32[]{:S(2)}, u32[]{:S(2)}) collective-permute-start(bf16[192,512]{1,0:T(8,128)(2,1)} %wide_mixed.1.own.mixed_ref), channel_id=1, source_target_pairs={{0,2},{1,3},{2,0},{3,1},{4,6},{5,7},{6,4},{7,5},{8,10},{9,11},{10,... | collective-permute-start | bytes 589832 | tf_op jit(solution)/shard_map/ppermute | solution.py:843
  114.1 5.3 %collective-permute-start.9 = (bf16[192,512]{1,0:T(8,128)(2,1)S(1)}, bf16[192,512]{1,0:T(8,128)(2,1)S(1)}, u32[]{:S(2)}, u32[]{:S(2)}) collective-permute-start(bf16[192,512]{1,0:T(8,128)(2,1)S(1)} %reshape.135.grad_own), channel_id=1, source_target_pairs={{0,1},{1,0},{2,3},{3,2},{4,5},{5,4},{6,7},{7,6},{8,9},{9,8},{10,11... | collective-permute-start | bytes 589832 | tf_op jit(solution)/shard_map/ppermute | solution.py:844
  114.1 5.8 %copy-start.36 = (bf16[192,512]{1,0:T(8,128)(2,1)}, bf16[192,512]{1,0:T(8,128)(2,1)S(1)}, u32[]{:S(2)}) copy-start(bf16[192,512]{1,0:T(8,128)(2,1)S(1)} %collective-permute-done.10.grad_far) | copy-start | bytes 589828
  114.1 5.3 %collective-permute-start.11 = (bf16[192,512]{1,0:T(8,128)(2,1)S(1)}, bf16[192,512]{1,0:T(8,128)(2,1)S(1)}, u32[]{:S(2)}, u32[]{:S(2)}) collective-permute-start(bf16[192,512]{1,0:T(8,128)(2,1)S(1)} %collective-permute-done.10.grad_far), channel_id=1, source_target_pairs={{0,1},{1,0},{2,3},{3,2},{4,5},{5,4},{6,7},{7,6},{8,9},{9,8},{10,11... | collective-permute-start | bytes 589832 | tf_op jit(solution)/shard_map/ppermute | solution.py:845
  114.6 4.8 collective-permute-start.6
  118.5 1.4 collective-permute-start.8
  131.9 3.3 collective-permute-start.16
  134.8 3.5 collective-permute-start.15
  136.2 7.4 %collective-permute-start.17 = (bf16[208,512]{1,0:T(8,128)(2,1)S(1)}, bf16[208,512]{1,0:T(8,128)(2,1)S(1)}, u32[]{:S(2)}, u32[]{:S(2)}) collective-permute-start(bf16[208,512]{1,0:T(8,128)(2,1)S(1)} %add_convert_fusion.1), channel_id=1, source_target_pairs={{0,2},{1,3},{2,0},{3,1},{4,6},{5,7},{6,4},{7,5},{8,10},{9,11},{10,... | collective-permute-start | bytes 638984 | tf_op jit(solution)/shard_map/ppermute | solution.py:853
  138.3 6.1 %copy-start.15 = (bf16[208,512]{1,0:T(8,128)(2,1)}, bf16[208,512]{1,0:T(8,128)(2,1)S(1)}, u32[]{:S(2)}) copy-start(bf16[208,512]{1,0:T(8,128)(2,1)S(1)} %collective-permute-done.15.near_ref) | copy-start | bytes 638980
  153.2 18.8 %all-to-all-start.2 = ((bf16[8,2,192,64]{2,3,1,0:T(8,128)(2,1)}), bf16[8,2,192,64]{2,3,1,0:T(8,128)(2,1)S(1)}, u32[]{:S(2)}, u32[]{:S(2)}) async-start(bf16[8,2,192,64]{2,3,1,0:T(8,128)(2,1)} %copy.193), calls=%async_computation.2 | async-start | bytes 1048576 | tf_op jit(solution)/shard_map/all_to_all | solution.py:863
  177.6 5.9 %collective-permute-start.19 = (bf16[192,512]{1,0:T(8,128)(2,1)}, bf16[192,512]{1,0:T(8,128)(2,1)S(1)}, u32[]{:S(2)}, u32[]{:S(2)}) collective-permute-start(bf16[192,512]{1,0:T(8,128)(2,1)} %get-tuple-element.87.grad_own), channel_id=1, source_target_pairs={{0,2},{1,3},{2,0},{3,1},{4,6},{5,7},{6,4},{7,5},{8,10},{9,11},{10,... | collective-permute-start | bytes 589832 | tf_op jit(solution)/shard_map/ppermute | solution.py:843
  179.1 4.4 collective-permute-start.18
  183.5 1.4 collective-permute-start.20
  195.5 1.7 collective-permute-start.22
  195.7 4.1 collective-permute-start.21
  198.2 7.4 %collective-permute-start.23 = (bf16[208,512]{1,0:T(8,128)(2,1)S(1)}, bf16[208,512]{1,0:T(8,128)(2,1)S(1)}, u32[]{:S(2)}, u32[]{:S(2)}) collective-permute-start(bf16[208,512]{1,0:T(8,128)(2,1)S(1)} %add_convert_fusion), channel_id=1, source_target_pairs={{0,2},{1,3},{2,0},{3,1},{4,6},{5,7},{6,4},{7,5},{8,10},{9,11},{10,... | collective-permute-start | bytes 638984 | tf_op jit(solution)/shard_map/ppermute | solution.py:853
  213.5 19.5 %all-to-all-start.3 = ((bf16[8,2,192,64]{2,3,1,0:T(8,128)(2,1)}), bf16[8,2,192,64]{2,3,1,0:T(8,128)(2,1)S(1)}, u32[]{:S(2)}, u32[]{:S(2)}) async-start(bf16[8,2,192,64]{2,3,1,0:T(8,128)(2,1)} %copy.205), calls=%async_computation.3 | async-start | bytes 1048576 | tf_op jit(solution)/shard_map/all_to_all | solution.py:874
  217.9 95.6 %all-reduce.8.cloned.1.call-start = ((), (), s32[]{:S(2)}) async-start(), calls=%async_computation.4 | async-start | bytes 786432 | tf_op jit(solution)/shard_map/psum | solution.py:1000
  231.3 7.6 %copy-start.12 = (f32[192,128]{1,0:T(8,128)S(1)}, f32[192,128]{1,0:T(8,128)}, u32[]{:S(2)}) copy-start(f32[192,128]{1,0:T(8,128)} %wide_kernel_grad.3) | copy-start | bytes 294916
  240.5 247.9 %all-reduce.10.cloned.1.call-start = ((), (), s32[]{:S(2)}) async-start(), calls=%async_computation.5 | async-start | bytes 9437184 | tf_op jit(solution)/shard_map/psum | solution.py:960
  240.6 9.4 %copy-start.18 = (bf16[192,512]{1,0:T(8,128)(2,1)S(1)}, bf16[192,512]{1,0:T(8,128)(2,1)}, u32[]{:S(2)}) copy-start(bf16[192,512]{1,0:T(8,128)(2,1)} %get-tuple-element.75) | copy-start | bytes 589828
  241.3 9.1 %copy-start.1 = (bf16[2,2,192,128]{3,2,1,0:T(8,128)(2,1)S(1)}, bf16[2,2,192,128]{3,2,1,0:T(8,128)(2,1)}, u32[]{:S(2)}) copy-start(bf16[2,2,192,128]{3,2,1,0:T(8,128)(2,1)} %copy.179.stream_ref) | copy-start | bytes 589828
  241.3 9.1 %copy-start.3 = (bf16[2,2,128,192]{2,3,1,0:T(8,128)(2,1)S(1)}, bf16[2,2,128,192]{2,3,1,0:T(8,128)(2,1)}, u32[]{:S(2)}) copy-start(bf16[2,2,128,192]{2,3,1,0:T(8,128)(2,1)} %param.33) | copy-start | bytes 589828
  241.5 1.4 collective-permute-start.13
  241.6 3.2 collective-permute-start.12
  243.0 7.0 %collective-permute-start.14 = (bf16[192,512]{1,0:T(8,128)(2,1)S(1)}, bf16[192,512]{1,0:T(8,128)(2,1)S(1)}, u32[]{:S(2)}, u32[]{:S(2)}) collective-permute-start(bf16[192,512]{1,0:T(8,128)(2,1)S(1)} %add_convert_fusion.2), channel_id=1, source_target_pairs={{0,2},{1,3},{2,0},{3,1},{4,6},{5,7},{6,4},{7,5},{8,10},{9,11},{10,... | collective-permute-start | bytes 589832 | tf_op jit(solution)/shard_map/ppermute | solution.py:853
  244.6 6.7 %copy-start.25 = (f32[192,128]{1,0:T(8,128)S(1)}, f32[192,128]{1,0:T(8,128)}, u32[]{:S(2)}) copy-start(f32[192,128]{1,0:T(8,128)} %get-tuple-element.108) | copy-start | bytes 294916
  244.6 6.8 %copy-start.11 = (f32[192,128]{1,0:T(8,128)S(1)}, f32[192,128]{1,0:T(8,128)}, u32[]{:S(2)}) copy-start(f32[192,128]{1,0:T(8,128)} %get-tuple-element.107) | copy-start | bytes 294916
  (24 other events, 39.6 us)
Sparse Core Ops, SparseCore 0:
  240.7 72.8 all-reduce.7
  318.6 169.7 all-reduce.9

commit v2 on v1

v2 whole, which is shorter than its diff:
```python
from functools import partial

import jax
import jax.numpy as jnp
from jax import lax
from jax.experimental import pallas as pl
from jax.experimental.pallas import tpu as pltpu
from jax.sharding import PartitionSpec as P


epsilon = 1e-06
bf16 = jnp.bfloat16
f32 = jnp.float32
vmem_bytes = 56 * 1024 * 1024
ahead = 8
band = 16
lane = 128


def dot(a, b, ca, cb):
    return lax.dot_general(a, b, (((ca,), (cb,)), ((), ())), preferred_element_type=f32)


def vmem_spec():
    return pl.BlockSpec(memory_space=pltpu.VMEM)


def smem_spec():
    return pl.BlockSpec(memory_space=pltpu.SMEM)


def any_spec():
    return pl.BlockSpec(memory_space=pl.ANY)


def struct(shape, dtype):
    return jax.ShapeDtypeStruct(shape, dtype)


def params(flops=0, moved=0):
    return dict(
        compiler_params=pltpu.CompilerParams(vmem_limit_bytes=vmem_bytes),
        cost_estimate=pl.CostEstimate(flops=flops, bytes_accessed=moved, transcendentals=0),
    )


def launch(body, name, ins, outs, scratch=(), scalars=(), after=()):
    given = len(scalars) + len(ins)

    def run(*refs):
        body(*refs[:given], *refs[given + len(after):])

    return pl.pallas_call(
        run,
        in_specs=[smem_spec()] * len(scalars) + [vmem_spec()] * len(ins) + [any_spec()] * len(after),
        out_specs=[vmem_spec()] * len(outs),
        out_shape=list(outs),
        scratch_shapes=list(scratch),
        name=name,
        **params(10_000_000, 1_000_000),
    )(*scalars, *ins, *after)


def swap(parts, number, chunk):
    width = 16 << chunk
    lanes = lax.broadcasted_iota(jnp.int32, parts[0].shape, 1)
    low = (lanes // width) % 2 == 0
    parts = list(parts)
    for i in range(8):
        j = i | (1 << number)
        if i != j:
            a, b = parts[i], parts[j]
            parts[i] = jnp.where(low, a, pltpu.roll(b, width, 1))
            parts[j] = jnp.where(low, pltpu.roll(a, lane - width, 1), b)
    return parts


half_rows = 96
strip = 32


def pieces_from_rows(get, out_ref, kind):
    for at in range(0, half_rows, strip):
        parts = [get((i >> 1) & 1, i & 1, slice((i >> 2) * half_rows + at, (i >> 2) * half_rows + at + strip)) for i in range(8)]
        for bit in range(3):
            parts = swap(parts, bit, bit)
        for target in range(8):
            out_ref[target, kind, at:at + strip, :] = parts[target].astype(bf16)


def rows_from_pieces(in_ref, kind, put):
    for at in range(0, half_rows, strip):
        parts = [in_ref[source, kind, at:at + strip, :].astype(f32) for source in range(8)]
        for bit in range(3):
            parts = swap(parts, bit, bit)
        for i in range(8):
            put((i >> 1) & 1, i & 1, slice((i >> 2) * half_rows + at, (i >> 2) * half_rows + at + strip), parts[i])


def pieces_from_cols(get, out_ref, kind):
    for at in range(0, half_rows, strip):
        parts = []
        for i in range(8):
            upper, half, canvas = i >> 2, (i >> 1) & 1, i & 1
            first = (canvas * 2 + upper) * lane
            parts.append(get(slice(half * half_rows + at, half * half_rows + at + strip), slice(first, first + lane)))
        parts = swap(swap(parts, 1, 2), 0, 1)
        for target in range(8):
            out_ref[target, kind, at:at + strip, :] = parts[target].astype(bf16)


def cols_from_pieces(in_ref, kind, out_ref):
    for at in range(0, half_rows, strip):
        parts = [in_ref[source, kind, at:at + strip, :].astype(f32) for source in range(8)]
        parts = swap(swap(parts, 1, 2), 0, 1)
        for i in range(8):
            upper, half, canvas = i >> 2, (i >> 1) & 1, i & 1
            first = (canvas * 2 + upper) * lane
            out_ref[half * half_rows + at:half * half_rows + at + strip, first:first + lane] = parts[i].astype(out_ref.dtype)


def piece_shape(kinds):
    return struct((8, kinds, half_rows, lane), bf16)


def state_powers(step, decay, frequency):
    size = jnp.exp(-step * decay)
    turn = step * frequency
    z = (size * jnp.cos(turn), size * jnp.sin(turn))

    def times(p, q):
        return (p[0] * q[0] - p[1] * q[1], p[0] * q[1] + p[1] * q[0])

    z2 = times(z, z)
    z3 = times(z2, z)
    z4 = times(z2, z2)
    return [None, z, z2, z3, z4, times(z4, z), times(z4, z2), times(z4, z3)], times(z4, z4), times


def pack_lanes(value):
    half = value.shape[0] // 2
    return jnp.concatenate([value[:half], value[half:]], axis=1)


def unpack_lanes(value):
    half = value.shape[1] // 2
    return jnp.concatenate([value[:, :half], value[:, half:]], axis=0)


def s4_section(direction, length, section, step_ref, decay_ref, freq_ref, real_ref, imag_ref, q_ref, flat_ref):
    channels = step_ref.shape[2]
    step = jnp.exp(step_ref[section, direction:direction + 1, :])
    step = jnp.concatenate([step, step], axis=1)
    decay = jnp.exp(pack_lanes(decay_ref[section, direction]))
    powers, z8, times = state_powers(step, decay, pack_lanes(freq_ref[section, direction]))
    for a in range(1, ahead):
        q_ref[2 * a] = powers[a][0]
        q_ref[2 * a + 1] = powers[a][1]
    q_ref[0] = z8[0]
    q_ref[1] = z8[1]

    def block(b, carry):
        pr, pi = carry
        rows = [jnp.sum(pr, axis=0, keepdims=True)]
        for a in range(1, ahead):
            rows.append(jnp.sum(pr * q_ref[2 * a] - pi * q_ref[2 * a + 1], axis=0, keepdims=True))
        flat_ref[pl.ds(pl.multiple_of(b * ahead, ahead), ahead), :] = step * jnp.concatenate(rows, axis=0)
        zr, zi = q_ref[0], q_ref[1]
        return (pr * zr - pi * zi, pr * zi + pi * zr)

    start = (pack_lanes(real_ref[section, direction]), pack_lanes(imag_ref[section, direction]))
    lax.fori_loop(0, length // ahead, block, start)
    flat = jnp.transpose(flat_ref[...])
    return (flat[:channels] + flat[channels:]).astype(bf16).astype(f32)


def s4_scratch(states, channels):
    return [pltpu.VMEM((2 * ahead, states // 2, 2 * channels), f32), pltpu.VMEM((lane, 2 * channels), f32)]


def s4_wide_body(length, section, copies, step_ref, decay_ref, freq_ref, real_ref, imag_ref, out_ref, q_ref, flat_ref):
    kernel = s4_section(1, length, section, step_ref, decay_ref, freq_ref, real_ref, imag_ref, q_ref, flat_ref)
    out_ref[...] = jnp.transpose(jnp.concatenate([kernel] * copies, axis=0))


def s4_wide(section, length, copies, log_step, *states):
    channels = states[0].shape[3]
    return launch(
        partial(s4_wide_body, length, section, copies), "s4_wide", [log_step, *states],
        [struct((lane, copies * channels), f32)], s4_scratch(states[0].shape[2], channels),
    )[0]


def s4_rest_body(lengths, copies, step_ref, decay_ref, freq_ref, real_ref, imag_ref, upstream_ref, pack_ref,
                 tall_low, tall_top, wide_top, scaled_ref, sums_ref, q_ref, flat_ref):
    refs = (step_ref, decay_ref, freq_ref, real_ref, imag_ref, q_ref, flat_ref)
    tall_low[...] = s4_section(0, lengths[0], 0, *refs)
    tall_top[...] = s4_section(0, lengths[0], 1, *refs)
    wide_top[...] = jnp.transpose(jnp.concatenate([s4_section(1, lengths[1], 1, *refs)] * copies, axis=0))
    scale = pack_ref[:, 4:5]
    total = jnp.zeros(scale.shape, f32)
    rows = upstream_ref.shape[1]
    for canvas in range(upstream_ref.shape[0]):
        for row in range(rows):
            scaled = upstream_ref[canvas, row].astype(f32) * scale
            at = (canvas * rows + row) * lane
            scaled_ref[:, at:at + lane] = scaled.astype(bf16)
            total += jnp.sum(scaled, axis=1, keepdims=True)
    put_columns(sums_ref, [total])


def s4_rest(lengths, copies, log_step, states, upstream, pack, after):
    channels = states[0].shape[3]
    pixels = upstream.shape[0] * upstream.shape[1] * lane
    column = struct((channels, lane), f32)
    return launch(
        partial(s4_rest_body, lengths, copies), "s4_rest", [log_step, *states, upstream, pack],
        [column, column, struct((lane, copies * channels), f32), struct((channels, pixels), bf16), column],
        s4_scratch(states[0].shape[2], channels), after=after,
    )


def pull_body(section, lengths, count, *refs):
    grads_ref, step_ref, decay_ref, freq_ref, real_ref, imag_ref = refs[:6]
    dstep_ref, ddecay_ref, dfreq_ref, dreal_ref, dimag_ref, vectors_ref, turn_ref, spread_ref, q_ref, s_ref = refs[6 + count:]
    channels = step_ref.shape[2]
    states = decay_ref.shape[2]
    tiles = 2 * channels // lane
    for direction, length in enumerate(lengths):
        step = jnp.exp(step_ref[0, direction:direction + 1, :])
        decay = jnp.exp(decay_ref[0, direction])
        freq = freq_ref[0, direction]
        wide_step = jnp.concatenate([step, step], axis=1)
        powers, z8, times = state_powers(wide_step, pack_lanes(decay), pack_lanes(freq))
        for a in range(ahead):
            for part in range(2):
                value = (z8 if a == 0 else powers[a])[part]
                for t in range(tiles):
                    q_ref[2 * a + part, t] = value[:, t * lane:(t + 1) * lane]
        first = (1 - direction) * lane
        turn_ref[0:channels, :] = grads_ref[:, first:first + lane]
        turn_ref[channels:2 * channels, :] = grads_ref[:, first:first + lane]
        flat = jnp.transpose(turn_ref[...])
        if direction == 0:
            vectors_ref[...] = flat[length:length + 16, 0:channels] if length + 16 <= lane else jnp.zeros((16, channels), f32)
        for place in range(length):
            for t in range(tiles):
                spread_ref[t, place] = jnp.broadcast_to(flat[place:place + 1, t * lane:(t + 1) * lane], (8, lane))
        turns = length // ahead
        groups = states // 16

        def group(index, carry):
            t = index // groups
            part = pl.ds(pl.multiple_of(lax.rem(index, groups) * 8, 8), 8)
            q = [(q_ref[2 * a, t, part, :], q_ref[2 * a + 1, t, part, :]) for a in range(ahead)]
            zr, zi = q[0]

            def block(turn, sums):
                s0r, s0i, s1r, s1i = sums
                b = turns - 1 - turn
                t0r = t0i = t1r = t1i = None
                for a in range(ahead - 1, 0, -1):
                    g = spread_ref[t, b * ahead + a]
                    x, y = g * q[a][0], g * q[a][1]
                    t0r, t0i = (x, y) if t0r is None else (t0r + x, t0i + y)
                    t1r, t1i = (t0r, t0i) if t1r is None else (t1r + t0r, t1i + t0i)
                t0r = t0r + spread_ref[t, b * ahead]
                base = (b * ahead).astype(f32)
                v1r, v1i = t1r + base * t0r, t1i + base * t0i
                return (
                    s0r * zr - s0i * zi + t0r,
                    s0r * zi + s0i * zr + t0i,
                    s1r * zr - s1i * zi + v1r,
                    s1r * zi + s1i * zr + v1i,
                )

            zero = jnp.zeros((8, lane), f32)
            sums = lax.fori_loop(0, turns, block, (zero, zero, zero, zero))
            for k in range(4):
                s_ref[k, t, part, :] = sums[k]
            return carry

        lax.fori_loop(0, tiles * groups, group, 0)
        s0r, s0i, s1r, s1i = [
            unpack_lanes(jnp.concatenate([s_ref[k, t] for t in range(tiles)], axis=1)) for k in range(4)
        ]
        real, imag = real_ref[0, direction], imag_ref[0, direction]
        dreal = step * s0r
        dimag = -step * s0i
        ddecay = -step * step * decay * (real * s1r - imag * s1i)
        dfreq = -step * step * (real * s1i + imag * s1r)
        dreal_ref[0, direction] = dreal
        dimag_ref[0, direction] = dimag
        ddecay_ref[0, direction] = ddecay
        dfreq_ref[0, direction] = dfreq
        dstep_ref[0, direction:direction + 1, :] = jnp.sum(
            real * dreal + imag * dimag + ddecay + freq * dfreq, axis=0, keepdims=True
        )


def s4_pullback(section, lengths, grads, log_step, log_decay, frequency, coef_real, coef_imag, earlier, after=()):
    states, channels = log_decay.shape[2], log_decay.shape[3]
    whole = pl.BlockSpec((1, 2, states, channels), lambda i: (section, 0, 0, 0))
    row = pl.BlockSpec((1, 2, channels), lambda i: (section, 0, 0))
    tiles = 2 * channels // lane
    held = [*earlier, *after]
    return pl.pallas_call(
        partial(pull_body, section, lengths, len(held)),
        grid=(1,),
        in_specs=[pl.BlockSpec((channels, 2 * lane), lambda i: (0, 0)), row, whole, whole, whole, whole] + [any_spec()] * len(held),
        out_specs=[row, whole, whole, whole, whole, pl.BlockSpec((16, channels), lambda i: (0, 0))],
        out_shape=[struct(log_step.shape, f32)] + [struct(log_decay.shape, f32)] * 4 + [struct((16, channels), f32)],
        scratch_shapes=[
            pltpu.VMEM((2 * channels, lane), f32),
            pltpu.VMEM((tiles, lane, 8, lane), f32),
            pltpu.VMEM((2 * ahead, tiles, states // 2, lane), f32),
            pltpu.VMEM((4, tiles, states // 2, lane), f32),
        ],
        input_output_aliases={6 + k: k for k in range(len(earlier))},
        name="s4_pullback",
        **params(50_000_000, 1_000_000),
    )(grads, log_step, log_decay, frequency, coef_real, coef_imag, *held)


pad = 8


def lane_tiles(value):
    return [value[:, at:at + lane] for at in range(0, value.shape[1], lane)]


def load_tiles(value, ref, first):
    for index, part in enumerate(lane_tiles(value)):
        ref[index, first:first + part.shape[0], :] = part


def width_conv(canvas, sign, signal_ref, kernel_ref, age_ref, reach_ref, out_ref):
    tiles, width = out_ref.shape[0], out_ref.shape[1]
    per = band // 8
    for index in range(width // band):
        ages = [age_ref[canvas, pl.ds((index * per + k) * 8, 8), :] for k in range(per)]

        def body(q, sums):
            sums = list(sums)
            places = [
                pl.multiple_of(jnp.clip(index * per + k - sign * q, 0, width // 8 - 1) * 8, 8) for k in range(per)
            ]
            for s in range(ahead):
                lag = q * ahead + s
                seen = [ages[k] >= lag for k in range(per)]
                for t in range(tiles):
                    value = jnp.broadcast_to(kernel_ref[t, pl.ds(lag, 1), :], (8, lane))
                    for k in range(per):
                        x = signal_ref[t, pl.ds(places[k] + (pad - sign * s), 8), :]
                        sums[k * tiles + t] += value * jnp.where(seen[k], x, 0.0)
            return tuple(sums)

        zero = jnp.zeros((8, lane), f32)
        sums = lax.fori_loop(0, reach_ref[canvas, index], body, (zero,) * (per * tiles))
        for k in range(per):
            for t in range(tiles):
                out_ref[t, pl.ds((index * per + k) * 8, 8), :] = sums[k * tiles + t]


def width_products(canvas, signal_ref, grad_ref, age_ref, reach_ref, total_ref):
    tiles, width = grad_ref.shape[0], grad_ref.shape[1]
    per = band // 8
    for index in range(width // band):
        ages = [age_ref[canvas, pl.ds((index * per + k) * 8, 8), :] for k in range(per)]
        grads = [[grad_ref[t, pl.ds((index * per + k) * 8, 8), :] for t in range(tiles)] for k in range(per)]

        def body(q, carry):
            places = [
                pl.multiple_of(jnp.clip(index * per + k - q, 0, width // 8 - 1) * 8, 8) for k in range(per)
            ]
            for s in range(ahead):
                lag = q * ahead + s
                seen = [ages[k] >= lag for k in range(per)]
                for t in range(tiles):
                    total = total_ref[t, lag]
                    for k in range(per):
                        x = signal_ref[t, pl.ds(places[k] + (pad - s), 8), :]
                        total += grads[k][t] * jnp.where(seen[k], x, 0.0)
                    total_ref[t, lag] = total
            return carry

        lax.fori_loop(0, reach_ref[canvas, index], body, 0)


def stacked_rows(ref, canvas):
    picture = ref[canvas].astype(f32)
    return jnp.transpose(picture.reshape(-1, picture.shape[2]))


def unstacked(ref, rows):
    flat = jnp.concatenate([jnp.transpose(ref[t]) for t in range(ref.shape[0])], axis=0)
    return flat.reshape(rows, flat.shape[0] // rows, flat.shape[1])


def width_scratch(rows, channels):
    tiles = rows * channels // lane
    return [
        pltpu.VMEM((tiles, lane + 2 * pad, lane), f32),
        pltpu.VMEM((tiles, lane, lane), f32),
        pltpu.VMEM((tiles, lane, lane), f32),
    ]


def convolve_canvas(canvas, sign, picture_ref, age_ref, reach_ref, signal_ref, kernel_ref, sum_ref):
    load_tiles(stacked_rows(picture_ref, canvas), signal_ref, pad)
    width_conv(canvas, sign, signal_ref, kernel_ref, age_ref, reach_ref, sum_ref)
    return unstacked(sum_ref, picture_ref.shape[1])


def wide_forward_body(packed, reach_ref, picture_ref, wide_ref, age_ref, out_ref, signal_ref, kernel_ref, sum_ref, *held):
    load_tiles(wide_ref[...], kernel_ref, 0)
    across_ref = held[0] if packed else out_ref
    for canvas in range(picture_ref.shape[0]):
        across_ref[canvas] = convolve_canvas(
            canvas, 1, picture_ref, age_ref, reach_ref, signal_ref, kernel_ref, sum_ref
        ).astype(across_ref.dtype)
    if packed:
        pieces_from_rows(lambda b, r, c: across_ref[b, r, c, :], out_ref, 0)
        pieces_from_rows(lambda b, r, c: picture_ref[b, r, c, :].astype(f32), out_ref, 1)


def wide_forward(packed, picture, wide, age, reach):
    out = piece_shape(2) if packed else struct(picture.shape, bf16)
    scratch = width_scratch(picture.shape[1], picture.shape[2])
    return launch(
        partial(wide_forward_body, packed), "wide_forward", [picture, wide, age], [out],
        scratch + [pltpu.VMEM(picture.shape, f32)] * packed, scalars=[reach],
    )[0]


def split_refs(packed, refs, held):
    return (refs[0], refs[1:]) if packed else (refs[:held], refs[held:])


def wide_mixed_body(packed, reach_ref, *refs):
    if packed:
        pieces, wide_ref, age_ref, pack_ref, out_ref, tall_ref, stream_ref, signal_ref, kernel_ref, sum_ref = refs
        for kind, ref in enumerate((tall_ref, stream_ref)):
            def put(b, r, c, value, ref=ref):
                ref[b, r, c, :] = value.astype(bf16)
            rows_from_pieces(pieces, kind, put)
    else:
        tall_ref, stream_ref, wide_ref, age_ref, pack_ref, out_ref, signal_ref, kernel_ref, sum_ref = refs
    rows = tall_ref.shape[1]
    skip = pack_ref[:, 0:1]
    load_tiles(wide_ref[...], kernel_ref, 0)
    for canvas in range(tall_ref.shape[0]):
        mixer = convolve_canvas(canvas, 1, tall_ref, age_ref, reach_ref, signal_ref, kernel_ref, sum_ref)
        for row in range(rows):
            at = (canvas * rows + row) * lane
            out_ref[:, at:at + lane] = (
                mixer[row] + skip * stream_ref[canvas, row].astype(f32)
            ).astype(bf16)


def wide_mixed(packed, moved, picture, wide, age, reach, pack):
    canvases, rows, channels, width = picture
    outs = [struct((channels, canvases * rows * lane), bf16)] + [struct(picture, bf16)] * (2 * packed)
    got = launch(
        partial(wide_mixed_body, packed), "wide_mixed", [*moved, wide, age, pack], outs,
        width_scratch(rows, channels), scalars=[reach],
    )
    return tuple(got) if packed else (got[0], *moved)


def norm_backward(grads, mixed_ref, stats_ref, pack_ref, channels_all):
    channels = mixed_ref.shape[0]
    keep, near, far = grads
    total = keep[...].astype(f32) + near[...].astype(f32) + far[...].astype(f32)
    normed_grad = total[0:channels]
    scaled_mean = total[channels:channels + 1] / channels_all
    paired_mean = total[channels + 1:channels + 2] / channels_all
    average, inverse = stats_ref[0:1, :], stats_ref[1:2, :]
    centred = (mixed_ref[...].astype(f32) - average) * inverse
    gain = pack_ref[:, 1:2]
    mixed_grad = inverse * (normed_grad * gain - scaled_mean - centred * paired_mean)
    return (
        mixed_grad,
        jnp.sum(normed_grad * centred, axis=1, keepdims=True),
        jnp.sum(normed_grad, axis=1, keepdims=True),
    )


def put_columns(ref, columns):
    places = lax.broadcasted_iota(jnp.int32, ref.shape, 1)
    value = jnp.zeros(ref.shape, f32)
    for index, column in enumerate(columns):
        value = jnp.where(places == index, column, value)
    ref[...] = value


def wide_norm_back_body(packed, channels_all, reach_ref, keep_ref, near_ref, far_ref, mixed_ref, stats_ref, pack_ref,
                        stream_ref, cotangent_ref, wide_ref, fore_ref, *refs):
    if packed:
        out_ref, grad_ref, sums_ref, signal_ref, kernel_ref, sum_ref, conv_ref, rest_ref = refs
    else:
        conv_ref, rest_ref, grad_ref, sums_ref, signal_ref, kernel_ref, sum_ref = refs
    canvases, rows = conv_ref.shape[0], conv_ref.shape[1]
    mixed_grad, gain_grad, shift_grad = norm_backward(
        (keep_ref, near_ref, far_ref), mixed_ref, stats_ref, pack_ref, channels_all
    )
    skip = pack_ref[:, 0:1]
    skip_grad = jnp.zeros_like(gain_grad)
    load_tiles(wide_ref[...], kernel_ref, 0)
    for canvas in range(canvases):
        for row in range(rows):
            at = (canvas * rows + row) * lane
            part = mixed_grad[:, at:at + lane]
            grad_ref[canvas, row] = part.astype(bf16)
            skip_grad += jnp.sum(part * stream_ref[canvas, row].astype(f32), axis=1, keepdims=True)
            rest_ref[canvas, row] = (cotangent_ref[canvas, row].astype(f32) + skip * part).astype(rest_ref.dtype)
        conv_ref[canvas] = convolve_canvas(
            canvas, -1, grad_ref, fore_ref, reach_ref, signal_ref, kernel_ref, sum_ref
        ).astype(conv_ref.dtype)
    put_columns(sums_ref, [skip_grad, gain_grad, shift_grad])
    if packed:
        pieces_from_rows(lambda b, r, c: conv_ref[b, r, c, :], out_ref, 0)
        pieces_from_rows(lambda b, r, c: rest_ref[b, r, c, :], out_ref, 1)


def wide_norm_back(packed, channels_all, grads, mixed, stats, pack, stream, cotangent, wide, fore, reach, after):
    plain = struct(stream.shape, bf16)
    sums = struct((stream.shape[2], lane), f32)
    got = launch(
        partial(wide_norm_back_body, packed, channels_all), "wide_norm_back",
        [*grads, mixed, stats, pack, stream, cotangent, wide, fore],
        [piece_shape(2), plain, sums] if packed else [plain, plain, plain, sums],
        width_scratch(stream.shape[1], stream.shape[2]) + [pltpu.VMEM(stream.shape, f32)] * (2 * packed),
        scalars=[reach], after=after,
    )
    return got[:-2], got[-2], got[-1]


def wide_back_body(packed, reach_ref, *refs):
    if packed:
        pieces, wide_ref, fore_ref, out_ref, grad_ref, signal_ref, kernel_ref, sum_ref, rest_ref = refs

        def put_grad(b, r, c, value):
            grad_ref[b, r, c, :] = value.astype(bf16)

        def put_rest(b, r, c, value):
            rest_ref[b, r, c, :] = value

        rows_from_pieces(pieces, 0, put_grad)
        rows_from_pieces(pieces, 1, put_rest)
    else:
        grad_ref, rest_ref, wide_ref, fore_ref, out_ref, signal_ref, kernel_ref, sum_ref = refs
    load_tiles(wide_ref[...], kernel_ref, 0)
    for canvas in range(grad_ref.shape[0]):
        value = convolve_canvas(canvas, -1, grad_ref, fore_ref, reach_ref, signal_ref, kernel_ref, sum_ref)
        out_ref[canvas] = (value + rest_ref[canvas].astype(f32)).astype(bf16)


def wide_back(packed, moved, picture, wide, fore, reach, after):
    plain = struct(picture, bf16)
    got = launch(
        partial(wide_back_body, packed), "wide_back", [*moved, wide, fore], [plain] * (1 + packed),
        width_scratch(picture[1], picture[2]) + [pltpu.VMEM(picture, f32)] * packed, scalars=[reach], after=after,
    )
    return (got[0], got[1] if packed else moved[0])


def wide_kernel_grad_body(reach_ref, grad_ref, input_ref, age_ref, out_ref, signal_ref, flat_ref, sum_ref, total_ref):
    channels = grad_ref.shape[2]
    rows = grad_ref.shape[1]
    total_ref[...] = jnp.zeros(total_ref.shape, f32)
    for canvas in range(grad_ref.shape[0]):
        load_tiles(stacked_rows(input_ref, canvas), signal_ref, pad)
        load_tiles(stacked_rows(grad_ref, canvas), flat_ref, 0)
        width_products(canvas, signal_ref, flat_ref, age_ref, reach_ref, total_ref)

    def reduce(index, carry):
        at = pl.multiple_of(index * 8, 8)
        for t in range(sum_ref.shape[0]):
            sum_ref[t, pl.ds(at, 8), :] = jnp.sum(total_ref[t, pl.ds(at, 8)], axis=1)
        return carry

    lax.fori_loop(0, lane // 8, reduce, 0)
    picture = unstacked(sum_ref, rows)
    out_ref[...] = sum(picture[row] for row in range(rows))


def wide_kernel_grad(grad, inputs, age, reach, after=()):
    channels = grad.shape[2]
    return launch(
        wide_kernel_grad_body, "wide_kernel_grad", [grad, inputs, age], [struct((channels, lane), f32)],
        width_scratch(grad.shape[1], channels) + [pltpu.VMEM((grad.shape[1] * channels // lane, lane, 8, lane), f32)],
        scalars=[reach], after=after,
    )[0]


def height_loop(count, body, carry):
    if count <= 16:
        for lag in range(count):
            carry = body(lag, carry)
        return carry
    return lax.fori_loop(0, count, body, carry)


def tap(kernel, lag):
    if isinstance(lag, int):
        return kernel[:, lag:lag + 1]
    places = lax.broadcasted_iota(jnp.int32, kernel.shape, 1)
    return jnp.sum(jnp.where(places == lag, kernel, 0.0), axis=1, keepdims=True)


def moved_by(value, shift):
    size = value.shape[1]
    if not isinstance(shift, int):
        return pltpu.roll(value, lax.rem(shift + size, size), 1)
    shift %= size
    return pltpu.roll(value, shift, 1) if shift else value


def height_conv(get, put, channels, kernel_ref, age_ref, sign, height):
    for at in range(0, channels, strip):
        rows = slice(at, at + strip)
        kernel = kernel_ref[rows, :]
        for canvas in range(age_ref.shape[0]):
            value, age = get(rows, canvas), age_ref[canvas]
            columns = value.shape[1] // height

            def body(lag, total):
                return total + tap(kernel, lag) * jnp.where(age >= lag, moved_by(value, sign * lag * columns), 0.0)

            put(rows, canvas, height_loop(height, body, jnp.zeros_like(value)))


def height_products(grads, values, ages, height):
    columns = values[0].shape[1] // height
    channels = values[0].shape[0]
    places = lax.broadcasted_iota(jnp.int32, (channels, lane), 1)

    def body(lag, total):
        part = None
        for grad, value, age in zip(grads, values, ages, strict=True):
            product = grad * jnp.where(age >= lag, moved_by(value, lag * columns), 0.0)
            for piece in lane_tiles(product):
                part = piece if part is None else part + piece
        return total + jnp.where(places == lag, jnp.sum(part, axis=1, keepdims=True), 0.0)

    return height_loop(height, body, jnp.zeros((channels, lane), f32))


def canvas_cut(ref, canvas, canvases):
    each = ref.shape[1] // canvases
    return slice(canvas * each, (canvas + 1) * each)


def tall_mixed_body(packed, height, *refs):
    if packed:
        pieces, kernel_ref, age_ref, pack_ref, out_ref, across_ref, stream_ref = refs
        cols_from_pieces(pieces, 0, across_ref)
        cols_from_pieces(pieces, 1, stream_ref)
    else:
        across_ref, stream_ref, kernel_ref, age_ref, pack_ref, out_ref = refs
    canvases = age_ref.shape[0]

    def get(rows, canvas):
        return across_ref[rows, canvas_cut(across_ref, canvas, canvases)].astype(f32)

    def put(rows, canvas, mixer):
        cut = canvas_cut(across_ref, canvas, canvases)
        out_ref[rows, cut] = (mixer + pack_ref[rows, 0:1] * stream_ref[rows, cut].astype(f32)).astype(bf16)

    height_conv(get, put, out_ref.shape[0], kernel_ref, age_ref, 1, height)


def tall_mixed(packed, height, moved, cols, kernel, age, pack):
    got = launch(
        partial(tall_mixed_body, packed, height), "tall_mixed", [*moved, kernel, age, pack],
        [struct(cols, bf16)] * (1 + 2 * packed),
    )
    return tuple(got) if packed else (got[0], *moved)


def tall_next_body(packed, height, keep_ref, near_ref, far_ref, stream_ref, pack_ref, kernel_ref, age_ref,
                   next_ref, branch_ref, out_ref, *held):
    canvases = age_ref.shape[0]
    conv_ref = held[0] if packed else out_ref

    def get(rows, canvas):
        cut = canvas_cut(stream_ref, canvas, canvases)
        branch = (
            keep_ref[rows, cut].astype(f32) + near_ref[rows, cut].astype(f32) + far_ref[rows, cut].astype(f32)
            + pack_ref[rows, 3:4]
        )
        branch_ref[rows, cut] = branch
        low = (stream_ref[rows, cut].astype(f32) + pack_ref[rows, 4:5] * branch).astype(bf16)
        next_ref[rows, cut] = low
        return low.astype(f32)

    def put(rows, canvas, value):
        conv_ref[rows, canvas_cut(stream_ref, canvas, canvases)] = value.astype(conv_ref.dtype)

    height_conv(get, put, stream_ref.shape[0], kernel_ref, age_ref, 1, height)
    if packed:
        pieces_from_cols(lambda rows, cut: conv_ref[rows, cut], out_ref, 0)
        pieces_from_cols(lambda rows, cut: next_ref[rows, cut].astype(f32), out_ref, 1)


def tall_next(packed, height, branches, stream, pack, kernel, age):
    got = launch(
        partial(tall_next_body, packed, height), "tall_next", [*branches, stream, pack, kernel, age],
        [struct(stream.shape, bf16), struct(stream.shape, f32), piece_shape(2) if packed else struct(stream.shape, bf16)],
        [pltpu.VMEM(stream.shape, f32)] * packed,
    )
    return got[0], got[1], [got[2]] if packed else [got[2], got[0]]


def tall_back_body(packed, height, *refs):
    if packed:
        pieces, kernel_ref, fore_ref, pack_ref, branch_ref, grad_ref, low_ref, sums_ref, conv_ref, rest_ref = refs
        cols_from_pieces(pieces, 0, conv_ref)
        cols_from_pieces(pieces, 1, rest_ref)
    else:
        conv_ref, rest_ref, kernel_ref, fore_ref, pack_ref, branch_ref, grad_ref, low_ref, sums_ref = refs
    canvases = fore_ref.shape[0]

    def get(rows, canvas):
        return conv_ref[rows, canvas_cut(conv_ref, canvas, canvases)].astype(f32)

    def put(rows, canvas, value):
        cut = canvas_cut(conv_ref, canvas, canvases)
        grad = rest_ref[rows, cut].astype(f32) + value
        grad_ref[rows, cut] = grad
        low_ref[rows, cut] = (grad * pack_ref[rows, 4:5]).astype(bf16)

    height_conv(get, put, conv_ref.shape[0], kernel_ref, fore_ref, -1, height)
    sums_ref[...] = jnp.zeros(sums_ref.shape, f32)


def tall_back(packed, height, moved, cols, kernel, fore, pack, branch, after):
    got = launch(
        partial(tall_back_body, packed, height), "tall_back", [*moved, kernel, fore, pack, branch],
        [struct(cols, f32), struct(cols, bf16), struct((cols[0], lane), f32)] + [struct(cols, bf16)] * packed,
        [pltpu.VMEM(cols, f32)] * packed, after=after,
    )
    return got[0], got[1], got[3] if packed else moved[0]


def branch_sums_body(grad_ref, branch_ref, pack_ref, bias_ref, scale_ref):
    grad = grad_ref[...]
    put_columns(bias_ref, [jnp.sum(grad * pack_ref[:, 4:5], axis=1, keepdims=True)])
    put_columns(scale_ref, [jnp.sum(grad * branch_ref[...], axis=1, keepdims=True)])


def branch_sums(grad, branch, pack, after):
    return launch(branch_sums_body, "branch_sums", [grad, branch, pack], [struct((grad.shape[0], lane), f32)] * 2, after=after)


def tall_norm_back_body(packed, height, channels_all, keep_ref, near_ref, far_ref, mixed_ref, stats_ref, pack_ref, stream_ref,
                        grad_ref, kernel_ref, fore_ref, *refs):
    if packed:
        out_ref, low_ref, sums_ref, conv_ref, rest_ref = refs
    else:
        conv_ref, rest_ref, low_ref, sums_ref = refs
    canvases = fore_ref.shape[0]
    mixed_grad, gain_grad, shift_grad = norm_backward(
        (keep_ref, near_ref, far_ref), mixed_ref, stats_ref, pack_ref, channels_all
    )
    low_ref[...] = mixed_grad.astype(bf16)
    rest_ref[...] = (grad_ref[...] + pack_ref[:, 0:1] * mixed_grad).astype(rest_ref.dtype)
    skip_grad = jnp.sum(mixed_grad * stream_ref[...].astype(f32), axis=1, keepdims=True)

    def get(rows, canvas):
        return low_ref[rows, canvas_cut(low_ref, canvas, canvases)].astype(f32)

    def put(rows, canvas, value):
        conv_ref[rows, canvas_cut(low_ref, canvas, canvases)] = value.astype(conv_ref.dtype)

    height_conv(get, put, low_ref.shape[0], kernel_ref, fore_ref, -1, height)
    put_columns(sums_ref, [skip_grad, gain_grad, shift_grad])
    if packed:
        pieces_from_cols(lambda rows, cut: conv_ref[rows, cut], out_ref, 0)
        pieces_from_cols(lambda rows, cut: rest_ref[rows, cut], out_ref, 1)


def tall_norm_back(packed, height, channels_all, grads, mixed, stats, pack, stream, grad, kernel, fore, after):
    plain, sums = struct(mixed.shape, bf16), struct((mixed.shape[0], lane), f32)
    got = launch(
        partial(tall_norm_back_body, packed, height, channels_all), "tall_norm_back",
        [*grads, mixed, stats, pack, stream, grad, kernel, fore],
        [piece_shape(2), plain, sums] if packed else [plain, plain, plain, sums],
        [pltpu.VMEM(mixed.shape, f32)] * (2 * packed), after=after,
    )
    return got[:-2], got[-2], got[-1]


def tall_kernel_grad_body(height, grad_ref, input_ref, age_ref, out_ref):
    canvases = age_ref.shape[0]
    for at in range(0, out_ref.shape[0], strip):
        rows = slice(at, at + strip)
        cuts = [canvas_cut(grad_ref, canvas, canvases) for canvas in range(canvases)]
        out_ref[rows, :] = height_products(
            [grad_ref[rows, cut].astype(f32) for cut in cuts], [input_ref[rows, cut].astype(f32) for cut in cuts],
            [age_ref[canvas] for canvas in range(canvases)], height,
        )


def tall_kernel_grad(height, grad, inputs, age, after=()):
    return launch(
        partial(tall_kernel_grad_body, height), "tall_kernel_grad", [grad, inputs, age],
        [struct((grad.shape[0], lane), f32)], after=after,
    )[0]


root = 0.7978845608028654
cubic = 0.044715


def gather_into(me_ref, parts, whole_ref):
    me = me_ref[0]
    for flip, part in enumerate(parts):
        whole_ref[me ^ flip] = part[...]


def scatter_out(me_ref, whole_ref, outs):
    me = me_ref[0]
    for flip, out in zip((3, 1, 2, 0), outs, strict=True):
        out[...] = whole_ref[me ^ flip]


def gather_shape(me_ref, parts, section, shape_ref):
    gather_into(me_ref, parts, shape_ref)
    every = shape_ref[...].reshape(-1, shape_ref.shape[2])
    return every[:, 2 * section:2 * section + 1], every[:, 2 * section + 1:2 * section + 2]


def mlp_forward(me_ref, parts, full_ref, shape, weight_in_ref, bias_ref, normed_ref, hidden_ref, slope_ref, stats_ref):
    gather_into(me_ref, parts, full_ref)
    mixed = full_ref[...].astype(f32).reshape(-1, full_ref.shape[2])
    average = jnp.mean(mixed, axis=0, keepdims=True)
    moved = mixed - average
    inverse = lax.rsqrt(jnp.mean(moved * moved, axis=0, keepdims=True) + epsilon)
    centred = moved * inverse
    stats_ref[0:1, :] = average
    stats_ref[1:2, :] = inverse
    normed = (centred * shape[0] + shape[1]).astype(bf16)
    normed_ref[...] = normed
    before = dot(weight_in_ref[0], normed, 0, 0) + bias_ref[...]
    square = before * before
    bend = jnp.tanh(root * before * (1.0 + cubic * square))
    half = 0.5 * (1.0 + bend)
    hidden_ref[...] = (before * half).astype(bf16)
    slope_ref[...] = (half + 0.5 * before * (1.0 - bend * bend) * root * (1.0 + 3.0 * cubic * square)).astype(slope_ref.dtype)
    return centred


def mlp_first_body(section, me_ref, own, near, far, cross, shape_own, shape_near, shape_far, shape_cross, weight_in_ref,
                   bias_ref, weight_out_ref,
                   send_far, send_own, keep_far, keep_own, normed_ref, hidden_ref, slope_ref, stats_ref, full_ref, sum_ref,
                   shape_ref):
    shape = gather_shape(me_ref, (shape_own, shape_near, shape_far, shape_cross), section, shape_ref)
    mlp_forward(me_ref, (own, near, far, cross), full_ref, shape, weight_in_ref, bias_ref,
                normed_ref, hidden_ref, slope_ref, stats_ref)
    partial_out = dot(weight_out_ref[0], hidden_ref[...], 0, 0)
    sum_ref[...] = partial_out.astype(bf16).reshape(sum_ref.shape)
    scatter_out(me_ref, sum_ref, (send_far, send_own, keep_far, keep_own))


def mlp_backward(me_ref, parts, full_ref, weight_out_ref, weight_in_ref, slope, gain, centred, sum_ref, outs, before_grad_ref):
    gather_into(me_ref, parts, full_ref)
    grad = full_ref[...].reshape(-1, full_ref.shape[2])
    before_grad = (dot(weight_out_ref[0], grad, 1, 0) * slope).astype(bf16)
    before_grad_ref[...] = before_grad
    normed_part = dot(weight_in_ref[0], before_grad, 1, 0)
    channels = sum_ref.shape[1] - 16
    scaled = normed_part * gain
    scaled_sum = jnp.sum(scaled, axis=0, keepdims=True)
    paired_sum = jnp.sum(scaled * centred, axis=0, keepdims=True)
    places = lax.broadcasted_iota(jnp.int32, (16, grad.shape[1]), 0)
    tail = jnp.where(places == 0, scaled_sum, jnp.where(places == 1, paired_sum, 0.0)).astype(bf16)
    for index in range(sum_ref.shape[0]):
        sum_ref[index, 0:channels, :] = normed_part[index * channels:(index + 1) * channels].astype(bf16)
        sum_ref[index, channels:, :] = tail
    scatter_out(me_ref, sum_ref, outs)


def mlp_top_body(section, me_ref, own, near, far, cross, grad_own, grad_near, grad_far, grad_cross,
                 shape_own, shape_near, shape_far, shape_cross, weight_in_ref, bias_ref, weight_out_ref,
                 back_sf, back_so, back_kf, back_ko, stats_ref, normed_ref, hidden_ref, before_grad_ref,
                 full_ref, back_ref, slope_ref, shape_ref):
    shape = gather_shape(me_ref, (shape_own, shape_near, shape_far, shape_cross), section, shape_ref)
    centred = mlp_forward(me_ref, (own, near, far, cross), full_ref, shape, weight_in_ref, bias_ref,
                          normed_ref, hidden_ref, slope_ref, stats_ref)
    mlp_backward(me_ref, (grad_own, grad_near, grad_far, grad_cross), full_ref, weight_out_ref, weight_in_ref,
                 slope_ref[...], shape[0], centred, back_ref, (back_sf, back_so, back_kf, back_ko), before_grad_ref)


def mlp_back_body(section, me_ref, own, near, far, cross, grad_own, grad_near, grad_far, grad_cross,
                  shape_own, shape_near, shape_far, shape_cross, weight_in_ref, weight_out_ref, slope_ref, stats_ref,
                  back_sf, back_so, back_kf, back_ko, before_grad_ref, full_ref, back_ref, shape_ref):
    shape = gather_shape(me_ref, (shape_own, shape_near, shape_far, shape_cross), section, shape_ref)
    gather_into(me_ref, (own, near, far, cross), full_ref)
    centred = (full_ref[...].astype(f32).reshape(-1, full_ref.shape[2]) - stats_ref[0:1, :]) * stats_ref[1:2, :]
    mlp_backward(me_ref, (grad_own, grad_near, grad_far, grad_cross), full_ref, weight_out_ref, weight_in_ref,
                 slope_ref[...].astype(f32), shape[0], centred, back_ref, (back_sf, back_so, back_kf, back_ko), before_grad_ref)


tile = 256


def pixel_block(rows):
    return pl.BlockSpec((rows, tile), lambda i: (0, i))


def fixed_block(shape):
    return pl.BlockSpec(shape, lambda i: (0,) * len(shape))


def section_block(section, shape):
    return pl.BlockSpec((1,) + shape, lambda i: (section, 0, 0))


def mlp_first(section, me, parts, shaping, weight_in, bias, weight_out):
    own = parts[0]
    channels, pixels = own.shape
    wide, units = weight_in.shape[1], weight_in.shape[2]
    piece = pixel_block(channels)
    return pl.pallas_call(
        partial(mlp_first_body, section),
        grid=(pixels // tile,),
        in_specs=[smem_spec()] + [piece] * 4 + [
            *[fixed_block(shaping[0].shape)] * 4, section_block(section, (wide, units)), fixed_block(bias.shape),
            section_block(section, (units, wide)),
        ],
        out_specs=[piece] * 4 + [pixel_block(wide), pixel_block(units), pixel_block(units), pixel_block(8)],
        out_shape=[struct(own.shape, bf16)] * 4 + [
            struct((wide, pixels), bf16), struct((units, pixels), bf16), struct((units, pixels), bf16), struct((8, pixels), f32),
        ],
        scratch_shapes=[
            pltpu.VMEM((4, channels, tile), bf16), pltpu.VMEM((4, channels, tile), bf16), pltpu.VMEM((4,) + shaping[0].shape, f32),
        ],
        name="mlp_first",
        **params(10_000_000, 1_000_000),
    )(me, *parts, *shaping, weight_in, bias, weight_out)


def mlp_top(section, me, parts, grads, shaping, weight_in, bias, weight_out):
    own = parts[0]
    channels, pixels = own.shape
    wide, units = weight_in.shape[1], weight_in.shape[2]
    piece, back = pixel_block(channels), pixel_block(channels + 16)
    return pl.pallas_call(
        partial(mlp_top_body, section),
        grid=(pixels // tile,),
        in_specs=[smem_spec()] + [piece] * 8 + [
            *[fixed_block(shaping[0].shape)] * 4, section_block(section, (wide, units)), fixed_block(bias.shape),
            section_block(section, (units, wide)),
        ],
        out_specs=[back] * 4 + [pixel_block(8), pixel_block(wide), pixel_block(units), pixel_block(units)],
        out_shape=[struct((channels + 16, pixels), bf16)] * 4 + [
            struct((8, pixels), f32), struct((wide, pixels), bf16), struct((units, pixels), bf16), struct((units, pixels), bf16),
        ],
        scratch_shapes=[
            pltpu.VMEM((4, channels, tile), bf16), pltpu.VMEM((4, channels + 16, tile), bf16),
            pltpu.VMEM((units, tile), f32), pltpu.VMEM((4,) + shaping[0].shape, f32),
        ],
        name="mlp_top",
        **params(10_000_000, 1_000_000),
    )(me, *parts, *grads, *shaping, weight_in, bias, weight_out)


def mlp_back(section, me, parts, grads, shaping, weight_in, weight_out, slope, stats):
    own = parts[0]
    channels, pixels = own.shape
    wide, units = weight_in.shape[1], weight_in.shape[2]
    piece, back = pixel_block(channels), pixel_block(channels + 16)
    return pl.pallas_call(
        partial(mlp_back_body, section),
        grid=(pixels // tile,),
        in_specs=[smem_spec()] + [piece] * 8 + [
            *[fixed_block(shaping[0].shape)] * 4, section_block(section, (wide, units)), section_block(section, (units, wide)),
            pixel_block(units), pixel_block(8),
        ],
        out_specs=[back] * 4 + [pixel_block(units)],
        out_shape=[struct((channels + 16, pixels), bf16)] * 4 + [struct((units, pixels), bf16)],
        scratch_shapes=[
            pltpu.VMEM((4, channels, tile), bf16), pltpu.VMEM((4, channels + 16, tile), bf16),
            pltpu.VMEM((4,) + shaping[0].shape, f32),
        ],
        name="mlp_back",
        **params(10_000_000, 1_000_000),
    )(me, *parts, *grads, *shaping, weight_in, weight_out, slope, stats)


def mlp_out_body(me_ref, hidden_ref, weight_out_ref, send_far, send_own, keep_far, keep_own, sum_ref):
    sum_ref[...] = dot(weight_out_ref[0], hidden_ref[...], 0, 0).astype(bf16).reshape(sum_ref.shape)
    scatter_out(me_ref, sum_ref, (send_far, send_own, keep_far, keep_own))


def mlp_out(section, me, hidden, weight_out, after):
    units, wide = weight_out.shape[1:]
    pixels = hidden.shape[1]
    channels = wide // 4
    piece = pixel_block(channels)

    def body(me_ref, hidden_ref, weight_out_ref, *refs):
        mlp_out_body(me_ref, hidden_ref, weight_out_ref, *refs[len(after):])

    return pl.pallas_call(
        body,
        grid=(pixels // tile,),
        in_specs=[smem_spec(), pixel_block(units), section_block(section, (units, wide))] + [any_spec()] * len(after),
        out_specs=[piece] * 4,
        out_shape=[struct((channels, pixels), bf16)] * 4,
        scratch_shapes=[pltpu.VMEM((4, channels, tile), bf16)],
        name="mlp_out",
        **params(10_000_000, 1_000_000),
    )(me, hidden, weight_out, *after)


def put_halves(me_ref, total, outs):
    if len(outs) == 1:
        outs[0][...] = total[...].astype(bf16)
        return
    part = outs[0].shape[0]
    mine = lax.rem(me_ref[1], 2)

    @pl.when(mine == 0)
    def _():
        outs[0][...] = total[:part].astype(bf16)
        outs[1][...] = total[part:].astype(bf16)

    @pl.when(mine == 1)
    def _():
        outs[0][...] = total[part:].astype(bf16)
        outs[1][...] = total[:part].astype(bf16)


def out_grad_body(me_ref, hidden_ref, grad_own, grad_near, grad_far, grad_cross, *refs):
    *outs, full_ref, total_ref = refs
    gather_into(me_ref, (grad_own, grad_near, grad_far, grad_cross), full_ref)
    total_ref[...] = dot(hidden_ref[...], full_ref[...].reshape(-1, full_ref.shape[2]), 1, 1)
    put_halves(me_ref, total_ref, outs)


def halves_of(rows, columns, halves):
    return [struct((rows // 2, columns), bf16)] * 2 if halves else [struct((rows, columns), bf16)]


def out_grad(halves, me, hidden, grads, after=()):
    units = hidden.shape[0]
    wide = 4 * grads[0].shape[0]
    return launch(
        out_grad_body, "out_grad", [hidden, *grads], halves_of(units, wide, halves),
        [pltpu.VMEM((4,) + grads[0].shape, bf16), pltpu.VMEM((units, wide), f32)], scalars=[me], after=after,
    )


def in_grad_body(me_ref, normed_ref, before_grad_ref, *refs):
    *outs, bias_ref, total_ref = refs
    before_grad = before_grad_ref[...]
    total_ref[...] = dot(normed_ref[...], before_grad, 1, 1)
    put_halves(me_ref, total_ref, outs)
    bias_ref[...] = jnp.broadcast_to(jnp.sum(before_grad.astype(f32), axis=1, keepdims=True), bias_ref.shape)


def in_grad(halves, me, normed, before_grad, after=()):
    wide, units = normed.shape[0], before_grad.shape[0]
    return launch(
        in_grad_body, "in_grad", [normed, before_grad], halves_of(wide, units, halves) + [struct((units, lane), f32)],
        [pltpu.VMEM((wide, units), f32)], scalars=[me], after=after,
    )


def top_output_body(keep_ref, near_ref, far_ref, stream_ref, cotangent_ref, pack_ref, out_ref, sums_ref):
    bias, scale = pack_ref[:, 3:4], pack_ref[:, 4:5]
    total = jnp.zeros(scale.shape, f32)
    rows = stream_ref.shape[1]
    for canvas in range(stream_ref.shape[0]):
        for row in range(rows):
            at = (canvas * rows + row) * lane
            cut = slice(at, at + lane)
            branch = keep_ref[:, cut].astype(f32) + near_ref[:, cut].astype(f32) + far_ref[:, cut].astype(f32) + bias
            out_ref[canvas, row] = (stream_ref[canvas, row].astype(f32) + scale * branch).astype(bf16)
            total += jnp.sum(cotangent_ref[canvas, row].astype(f32) * branch, axis=1, keepdims=True)
    put_columns(sums_ref, [total])


def top_output(branches, stream, cotangent, pack, after):
    return launch(
        top_output_body, "top_output", [*branches, stream, cotangent, pack],
        [struct(stream.shape, bf16), struct((stream.shape[2], lane), f32)], after=after,
    )


core_pairs = [(i, i ^ 1) for i in range(4)]
chip_pairs = [(i, i ^ 2) for i in range(4)]


def gather_channels(own):
    far = lax.ppermute(own, "ch", chip_pairs)
    near = lax.ppermute(own, "ch", core_pairs)
    cross = lax.ppermute(far, "ch", core_pairs)
    return (own, near, far, cross)


def scatter_channels(send_far, send_own, keep_far, keep_own):
    near_far = lax.ppermute(send_far, "ch", core_pairs)
    near_own = lax.ppermute(send_own, "ch", core_pairs)
    onward = (keep_far.astype(f32) + near_far.astype(f32)).astype(bf16)
    far = lax.ppermute(onward, "ch", chip_pairs)
    return (keep_own, near_own, far)


def across_rows(value, flip):
    return lax.ppermute(value, "rows", [(i, i ^ flip) for i in range(8)])


def rows_sum(value):
    for flip in (1, 2, 4):
        value = value + across_rows(value, flip)
    return value


def collect_body(height, tall_ref, wide_ref, norm_ref, bias_ref, scale_ref, units_ref, out_ref):
    channels = tall_ref.shape[0]
    places = lax.broadcasted_iota(jnp.int32, tall_ref.shape, 1)
    held = jnp.where(places < height, tall_ref[...], 0.0)
    columns = [norm_ref[:, k:k + 1] for k in range(3)] + [bias_ref[:, 0:1], scale_ref[:, 0:1]]
    columns += [units_ref[at:at + channels, 0:1] for at in range(0, units_ref.shape[0], channels)]
    for index, column in enumerate(columns):
        held = jnp.where(places == height + index, column, held)
    out_ref[:, 0:lane] = wide_ref[...]
    out_ref[:, lane:] = held


def collect(height, *parts):
    return launch(partial(collect_body, height), "collect", parts, [struct((parts[0].shape[0], 2 * lane), f32)])[0]


def quarter_body(me_ref, keep_ref, near_ref, *outs):
    mine = me_ref[1] // 2
    part = outs[0].shape[0]
    for flip, out in enumerate(outs):
        cut = pl.ds(pl.multiple_of((mine ^ flip) * part, part), part)
        out[...] = (keep_ref[cut, :].astype(f32) + near_ref[cut, :].astype(f32)).astype(bf16)


def quarters(me, keep, near, after=()):
    shape = struct((keep.shape[0] // 4, keep.shape[1]), bf16)
    return launch(quarter_body, "quarters", [keep, near], [shape] * 4, scalars=[me], after=after)


def rows_sum_matrix(me, keep, near, after=()):
    own, *others = quarters(me, keep, near, after)
    total = own.astype(f32)
    for index, other in enumerate(others):
        total = total + across_rows(other, 2 * (index + 1)).astype(f32)
    total = total.astype(bf16)
    half = jnp.concatenate([total] + [across_rows(total, 2 * flip) for flip in (1, 2, 3)], axis=0)
    return half, across_rows(half, 1)


def assemble_body(me_ref, half_ref, other_ref, top_ref, out_ref):
    mine, group = lax.rem(me_ref[1], 2), me_ref[1] // 2
    size = half_ref.shape[0]
    part = size // 4
    for flip in range(4):
        for side, ref in ((mine, half_ref), (1 - mine, other_ref)):
            at = pl.multiple_of(side * size + (group ^ flip) * part, part)
            out_ref[0, pl.ds(at, part), :] = ref[flip * part:(flip + 1) * part, :].astype(f32)
    out_ref[1] = top_ref[...].astype(f32)


def assemble(me, half, other, top):
    return pl.pallas_call(
        assemble_body,
        in_specs=[smem_spec()] + [vmem_spec()] * 3,
        out_specs=vmem_spec(),
        out_shape=struct((2,) + top.shape, f32),
        name="assemble",
        **params(1_000_000, 7_000_000),
    )(me, half, other, top)


def exchange(pieces):
    return lax.all_to_all(pieces, "rows", split_axis=0, concat_axis=0, tiled=True)


def rows_to_cols(packed, moving, count, picture):
    if packed:
        return [exchange(moving[0])]
    canvases, rows, channels, width = picture
    pieces = []
    for part in moving:
        cut = part.reshape(canvases, rows, channels, count, width // count)
        pieces.append(cut.transpose(3, 2, 0, 1, 4).reshape(count, channels, -1))
    moved = exchange(jnp.stack(pieces, axis=1))
    moved = moved.reshape(count, len(moving), channels, canvases, rows, width // count)
    return [moved[:, k].transpose(1, 2, 0, 3, 4).reshape(channels, -1) for k in range(len(moving))]


def cols_to_rows(packed, moving, count, picture):
    if packed:
        return [exchange(moving[0])]
    canvases, rows, channels, width = picture
    pieces = []
    for part in moving:
        cut = part.reshape(channels, canvases, count, rows, width // count)
        pieces.append(cut.transpose(2, 0, 1, 3, 4).reshape(count, channels, -1))
    moved = exchange(jnp.stack(pieces, axis=1))
    moved = moved.reshape(count, len(moving), channels, canvases, rows, width // count)
    return [moved[:, k].transpose(2, 3, 1, 0, 4).reshape(picture) for k in range(len(moving))]


def crop_reach(starts):
    count = starts.shape[1]
    places = jnp.arange(count, dtype=jnp.int32)
    here, there = places[None, :, None], places[None, None, :]
    begins = starts[:, None, :] > 0
    first = jnp.max(jnp.where(begins & (there <= here), there, 0), axis=2)
    following = jnp.min(jnp.where(begins & (there > here), there, count), axis=2)
    return places[None, :] - first, following - 1 - places[None, :]


def band_turns(age):
    return jnp.max(age.reshape(age.shape[0], -1, band), axis=2) // ahead + 1


def on_device(
    count,
    pixels,
    row_starts,
    col_starts,
    log_step,
    log_decay,
    frequency,
    coef_real,
    coef_imag,
    skip_gain,
    norm_gain,
    norm_shift,
    weight_in,
    bias_in,
    weight_out,
    bias_out,
    layer_scale,
    cotangent,
):
    canvases, rows, width, channels = pixels.shape
    height = row_starts.shape[1]
    channels_all = weight_in.shape[1]
    lengths = (height, width)
    picture = (canvases, rows, channels, width)
    cols = (channels, canvases * height * (width // count))
    me = jnp.stack([lax.axis_index("ch"), lax.axis_index("rows")]).astype(jnp.int32)
    eight = count == 8
    packed = eight and picture == (2, 2, 2 * half_rows, lane)

    stream = jnp.swapaxes(pixels, 2, 3)
    upstream = jnp.swapaxes(cotangent, 2, 3)
    states = [jnp.swapaxes(value, 2, 3) for value in (log_decay, frequency, coef_real, coef_imag)]

    age, fore = crop_reach(col_starts)
    age_reach, fore_reach = band_turns(age), band_turns(fore)
    age = jnp.broadcast_to(age[:, :, None], (canvases, width, lane))
    fore = jnp.broadcast_to(fore[:, :, None], (canvases, width, lane))
    row_age, row_fore = crop_reach(row_starts)
    row_age = jnp.repeat(row_age, width // count, axis=1)[:, None, :]
    row_fore = jnp.repeat(row_fore, width // count, axis=1)[:, None, :]

    packs = [
        jnp.stack([skip_gain[k], norm_gain[k], norm_shift[k], bias_out[k], layer_scale[k]], axis=1) for k in range(2)
    ]
    shaping = gather_channels(jnp.stack([norm_gain[0], norm_shift[0], norm_gain[1], norm_shift[1]], axis=1))
    bias_columns = [bias_in[k][:, None] for k in range(2)]

    wide_low = s4_wide(0, width, rows, log_step, *states)
    across = wide_forward(packed, stream, wide_low, age, age_reach)
    tall_low, tall_top, wide_top, top_scaled, top_bias_sums = s4_rest(
        lengths, rows, log_step, states, upstream, packs[1], [across]
    )
    moved = rows_to_cols(packed, [across] if packed else [across, stream], count, picture)
    mixed_low, across_cols, stream_cols = tall_mixed(packed, height, moved, cols, tall_low, row_age, packs[0])
    low_parts = gather_channels(mixed_low)
    first = mlp_first(0, me, low_parts, shaping, weight_in, bias_columns[0], weight_out)
    normed_low, hidden_low, slope_low, stats_low = first[4:]
    branches = scatter_channels(*first[:4])
    top_parts = gather_channels(top_scaled)

    next_cols, branch_cols, moving = tall_next(packed, height, branches, stream_cols, packs[0], tall_top, row_age)
    moved = cols_to_rows(packed, moving, count, picture)
    mixed_top, tall_rows, next_rows = wide_mixed(packed, moved, picture, wide_top, age, age_reach, packs[1])
    top_mixed_parts = gather_channels(mixed_top)
    top = mlp_top(1, me, top_mixed_parts, top_parts, shaping, weight_in, bias_columns[1], weight_out)
    stats_top, normed_top, hidden_top, before_grad_top = top[4:]
    top_grads = scatter_channels(*top[:4])
    top_out = out_grad(False, me, hidden_top, top_parts)[0]
    top_in, top_units = in_grad(False, me, normed_top, before_grad_top)
    top_weights = lax.psum((top_in, top_out), "rows")

    moving, grad_rows, top_sums = wide_norm_back(
        packed, channels_all, top_grads, mixed_top, stats_top, packs[1], next_rows, upstream, wide_top, fore, fore_reach,
        [top_in, top_out],
    )
    top_partials = mlp_out(1, me, hidden_top, weight_out, moving[:1])
    moved = rows_to_cols(packed, moving, count, picture)
    grad_cols, grad_low, conv_cols = tall_back(packed, height, moved, cols, tall_top, row_fore, packs[0], branch_cols, top_partials[:1])

    grad_parts = gather_channels(grad_low)
    *back, before_grad_low = mlp_back(0, me, low_parts, grad_parts, shaping, weight_in, weight_out, slope_low, stats_low)
    low_grads = scatter_channels(*back)
    low_out = out_grad(eight, me, hidden_low, grad_parts, [before_grad_low])
    if eight:
        near_out = across_rows(low_out[1], 1)
        *low_in, low_units = in_grad(True, me, normed_low, before_grad_low, [near_out])
        near_in = across_rows(low_in[1], 1)
    else:
        *low_in, low_units = in_grad(False, me, normed_low, before_grad_low)
    moving, low_grad_cols, low_sums = tall_norm_back(
        packed, height, channels_all, low_grads, mixed_low, stats_low, packs[0], stream_cols, grad_cols, tall_low, row_fore,
        low_out[1:],
    )
    moved = cols_to_rows(packed, moving, count, picture)
    pixels_grad, low_conv_rows = wide_back(packed, moved, picture, wide_low, fore, fore_reach, top_weights[:1])
    if eight:
        in_grads = assemble(me, *rows_sum_matrix(me, low_in[0], near_in), top_weights[0])
        out_grads = assemble(me, *rows_sum_matrix(me, low_out[0], near_out), top_weights[1])
    else:
        low_weights = lax.psum((low_in[0], low_out[0]), "rows")
        in_grads = jnp.stack([low_weights[0], top_weights[0]]).astype(f32)
        out_grads = jnp.stack([low_weights[1], top_weights[1]]).astype(f32)

    top_branches = scatter_channels(*top_partials)
    activations, top_scale_sums = top_output(top_branches, next_rows, upstream, packs[1], moving[:1])
    low_branch = branch_sums(grad_cols, branch_cols, packs[0], moving[:1])
    top_tall = tall_kernel_grad(height, conv_cols, next_cols, row_age, moving[:1])
    top_wide = wide_kernel_grad(grad_rows, tall_rows, age, age_reach, moving[:1])
    low_tall = tall_kernel_grad(height, low_grad_cols, across_cols, row_age, moving[:1])
    low_wide = wide_kernel_grad(low_conv_rows, stream, age, age_reach)
    small = [
        [low_tall, low_wide, low_sums, *low_branch, low_units],
        [top_tall, top_wide, top_sums, top_bias_sums, top_scale_sums, top_units],
    ]
    if eight:
        sums = [rows_sum(collect(height, *parts)) for parts in small]
    else:
        small = lax.psum(small, "rows")
        sums = [jnp.concatenate([parts[1], parts[0]], axis=1) for parts in small]
    state_grads = []
    vectors = [None, None]
    for section in (1, 0):
        *state_grads, vectors[section] = s4_pullback(section, lengths, sums[section], log_step, *states, state_grads)
    if not eight:
        vectors = [
            jnp.concatenate([parts[2][:, :3].T, parts[3][:, :1].T, parts[4][:, :1].T, parts[5][:, 0].reshape(-1, channels)], axis=0)
            for parts in small
        ]
    step_grad, decay_grad, freq_grad, real_grad, imag_grad = state_grads
    vectors = jnp.stack([value[:5 + weight_in.shape[2] // channels] for value in vectors])
    return (
        jnp.swapaxes(activations, 2, 3),
        jnp.swapaxes(pixels_grad, 2, 3),
        step_grad,
        jnp.swapaxes(decay_grad, 2, 3),
        jnp.swapaxes(freq_grad, 2, 3),
        jnp.swapaxes(real_grad, 2, 3),
        jnp.swapaxes(imag_grad, 2, 3),
        vectors[:, 0],
        vectors[:, 1],
        vectors[:, 2],
        in_grads,
        vectors[:, 5:].reshape(2, -1),
        out_grads,
        vectors[:, 3],
        vectors[:, 4],
    )


def solution(mesh):
    picture = P(None, "rows", None, "ch")
    state = P(None, None, "ch", None)
    step = P(None, None, "ch")
    vector = P(None, "ch")
    into = P(None, None, "ch")
    out = P(None, "ch", None)
    in_specs = (
        picture, P(), P(), step, state, state, state, state, vector, vector, vector, into, vector, out, vector, vector, picture,
    )
    out_specs = (
        picture, picture, step, state, state, state, state, vector, vector, vector, into, vector, out, vector, vector,
    )
    return jax.shard_map(
        partial(on_device, mesh.shape["rows"]), mesh=mesh, in_specs=in_specs, out_specs=out_specs, check_vma=False
    )
```

time: 512 us -> 366 us (0.71)
  waiting for transfers between devices: 249 us -> 90.8 us
  blocking collectives: 46.2 us -> 0 us
  Pallas kernels: 102 us -> 145 us
  starting transfers between devices: 37 us -> 77.8 us
  other arithmetic: 19.8 us -> 8.71 us
  local copies, waits for them, and re-layouts: 32.5 us -> 22.7 us
    psum x2 -> x1, waiting for transfers between devices: 181 us -> 0.02 us  [on_device(): top_weights = lax.psum((top_in, top_out), 'rows')]
    pallas_call x18 -> x32, Pallas kernels: 102 us -> 145 us  [the longest x24 100 us: launch(): pl.pallas_call(run, in_specs=[smem_spec()] * len(scalars) + [vmem_spec()]...]
    ppermute x0 -> x22, starting transfers between devices: none -> 40.6 us  [across_rows(): return lax.ppermute(value, 'rows', [(i, i ^ flip) for i in range(8)])]
    ppermute x0 -> x22, waiting for transfers between devices: none -> 39.8 us  [across_rows(): return lax.ppermute(value, 'rows', [(i, i ^ flip) for i in range(8)])]
    psum x1 -> x0, blocking collectives: 38.1 us -> none  [on_device(): lax.psum((tall_grads, wide_grads, columns, bias_grads), 'rows')]
    all_to_all x4, waiting for transfers between devices: 37.1 us -> 21.3 us  [exchange(): lax.all_to_all(pieces, 'rows', split_axis=0, concat_axis=0, tiled=True)]
    unnamed x84 -> x103, local copies, waits for them, and re-layouts: 3.84 us -> 14.5 us
    all_gather x1 -> x0, blocking collectives: 8.11 us -> none  [on_device(): lax.all_gather(jnp.stack([norm_gain, norm_shift], axis=2), 'ch', axis=1,...]
  transfers between devices with their start and end apart: 30 -> 54, of which waited for: 17 -> 19; matrix products, arithmetic and copies ran while one was open for 4% -> 5% of each run, Pallas kernels for 8% -> 28%
where the time goes in v2:
time: 366 us; the launch traced here: 360 us
  Pallas kernels  145 us (40%)
  waiting for transfers between devices  90.8 us (25%)
  starting transfers between devices  77.8 us (21%)
  local copies, waits for them, and re-layouts  22.7 us (6%)
  between operations  15.1 us (4%)
  other arithmetic  8.71 us (2%)
    pallas_call x24, Pallas kernels, launch(): pl.pallas_call(run, in_specs=[smem_spec()] * len(scalars) + [vmem_spec()]...  100 us
    ppermute x22, starting transfers between devices, across_rows(): return lax.ppermute(value, 'rows', [(i, i ^ flip) for i in range(8)])  40.6 us
    ppermute x22, waiting for transfers between devices, across_rows(): return lax.ppermute(value, 'rows', [(i, i ^ flip) for i in range(8)])  39.8 us
    all_to_all x4, starting transfers between devices, exchange(): lax.all_to_all(pieces, 'rows', split_axis=0, concat_axis=0, tiled=True)  22.4 us
    all_to_all x4, waiting for transfers between devices, exchange(): lax.all_to_all(pieces, 'rows', split_axis=0, concat_axis=0, tiled=True)  21.3 us
    unnamed x103, local copies, waits for them, and re-layouts  14.5 us
    ppermute x5, waiting for transfers between devices, gather_channels(): far = lax.ppermute(own, 'ch', chip_pairs)  13.3 us
    pallas_call x2, Pallas kernels, s4_pullback(): pl.pallas_call(partial(pull_body, section, lengths, len(held)), grid=(1,)...  12.6 us
  transfers between devices with their start and end apart: 54, of which 19 were waited for; matrix products, arithmetic and copies ran while one was open for 5% of the time, Pallas kernels for 28%

profile of v2, /device:TPU:0, one launch (start us, length us, event | category | flops | bytes accessed | tf_op | source)
XLA Modules:
  0.0 360.3 jit_solution(9904737762601455728)
XLA Ops:
  9.0 3.7 %s4_wide.1.refs_2_ = f32[128,384]{1,0:T(8,128)} custom-call(f32[2,2,192]{2,1,0:T(2,128)} %refs_1_.3, f32[2,2,64,192]{3,2,1,0:T(8,128)} %bitcast.57, f32[2,2,64,192]{3,2,1,0:T(8,128)} %bitcast.61, f32[2,2,64,192]{3,2,1,0:T(8,128)} %bitcast.65, f32[2,2,64,192]{3,2,1,0:T(8,128)} %bitcast.69), custom_call_target="tpu_custom_call" | custom-call | flops 10000000 | bytes 1000000 | tf_op jit(solution)/shard_map/s4_wide/pallas_call | solution.py:53
  13.4 6.1 %wide_forward.1.refs_7_ = bf16[8,2,96,128]{3,2,1,0:T(8,128)(2,1)} custom-call(s32[2,8]{1,0:T(2,128)} %fusion.1.refs_0_, bf16[2,2,192,128]{3,2,1,0:T(8,128)(2,1)} %bitcast.76, f32[128,384]{1,0:T(8,128)} %s4_wide.1.refs_2_, s32[2,128,128]{2,1,0:T(8,128)} %broadcast_in_dim.70.refs_3_), custom_call_target="tpu_custom_call" | custom-call | flops 10000000 | bytes 1000000 | tf_op jit(solution)/shard_map/wide_forward/pallas_call | solution.py:53
  19.5 7.3 %all-to-all-start = ((bf16[8,2,96,128]{3,2,1,0:T(8,128)(2,1)}), bf16[8,2,96,128]{3,2,1,0:T(8,128)(2,1)S(1)}, u32[]{:S(2)}, u32[]{:S(2)}) async-start(bf16[8,2,96,128]{3,2,1,0:T(8,128)(2,1)} %wide_forward.1.refs_7_), calls=%async_computation | async-start | bytes 786432 | tf_op jit(solution)/shard_map/all_to_all | solution.py:1185
  29.4 4.8 %s4_rest.1 = (f32[192,128]{1,0:T(8,128)}, f32[192,128]{1,0:T(8,128)}, f32[128,384]{1,0:T(8,128)}, bf16[192,512]{1,0:T(8,128)(2,1)}, f32[192,128]{1,0:T(8,128)}) custom-call(f32[2,2,192]{2,1,0:T(2,128)} %refs_1_.3, f32[2,2,64,192]{3,2,1,0:T(8,128)} %bitcast.58, f32[2,2,64,192]{3,2,1,0:T(8,128)} %bitcast.62, f32[2,2,64,192]{3,2,1,0:T(8,128)} %bitcast.66, ...), custom_call_target="tpu_custom_call" | custom-call | flops 10000000 | bytes 1000000 | tf_op jit(solution)/shard_map/s4_rest/pallas_call | solution.py:53
  34.2 4.3 %all-to-all-done.refs_0_ = bf16[8,2,96,128]{3,2,1,0:T(8,128)(2,1)S(1)} async-done(((bf16[8,2,96,128]{3,2,1,0:T(8,128)(2,1)}), bf16[8,2,96,128]{3,2,1,0:T(8,128)(2,1)S(1)}, u32[]{:S(2)}, u32[]{:S(2)}) %all-to-all-start) | async-done | bytes 393248 | tf_op jit(solution)/shard_map/all_to_all | solution.py:1185
  39.3 3.7 %tall_mixed.1 = (bf16[192,512]{1,0:T(8,128)(2,1)}, bf16[192,512]{1,0:T(8,128)(2,1)}, bf16[192,512]{1,0:T(8,128)(2,1)}) custom-call(bf16[8,2,96,128]{3,2,1,0:T(8,128)(2,1)} %copy-done.4, f32[192,128]{1,0:T(8,128)} %get-tuple-element.96.refs_1_.refs_8_, s32[2,1,256]{2,1,0:T(1,128)} %broadcast_in_dim_reshape.6.refs_2_.refs_6_, ...), custom_call_target="tpu_custom_call" | custom-call | flops 10000000 | bytes 1000000 | tf_op jit(solution)/shard_map/tall_mixed/pallas_call | solution.py:53
  45.7 3.1 collective-permute-done.1.far
  52.9 7.0 %mlp_first.1 = (bf16[192,512]{1,0:T(8,128)(2,1)}, bf16[192,512]{1,0:T(8,128)(2,1)}, bf16[192,512]{1,0:T(8,128)(2,1)}, bf16[192,512]{1,0:T(8,128)(2,1)}, bf16[768...) custom-call(s32[2]{0:T(128)} %pad_add_fusion.me_ref.refs_0_, ...), custom_call_target="tpu_custom_call" | custom-call | flops 10000000 | bytes 1000000 | tf_op jit(solution)/shard_map/mlp_first/pallas_call | solution.py:926
  64.3 5.7 %collective-permute-done.8.refs_2_ = bf16[192,512]{1,0:T(8,128)(2,1)S(1)} collective-permute-done((bf16[192,512]{1,0:T(8,128)(2,1)S(1)}, bf16[192,512]{1,0:T(8,128)(2,1)S(1)}, u32[]{:S(2)}, u32[]{:S(2)}) %collective-permute-start.8) | collective-permute-done | bytes 196640 | tf_op jit(solution)/shard_map/ppermute | solution.py:1109
  70.7 4.9 %tall_next.1 = (bf16[192,512]{1,0:T(8,128)(2,1)}, f32[192,512]{1,0:T(8,128)}, bf16[8,2,96,128]{3,2,1,0:T(8,128)(2,1)}) custom-call(bf16[192,512]{1,0:T(8,128)(2,1)} %get-tuple-element.98.refs_0_, bf16[192,512]{1,0:T(8,128)(2,1)} %copy-done.37, bf16[192,512]{1,0:T(8,128)(2,1)} %copy-done.38, bf16[192,512]{1,0:T(8,128)(2,1)} %get-tuple-element.102.refs_3_.refs_6_, ...), custom_call_target="tpu_custom_call" | custom-call | flops 10000000 | bytes 1000000 | tf_op jit(solution)/shard_map/tall_next/pallas_call | solution.py:53
  75.6 5.7 %all-to-all-start.1 = ((bf16[8,2,96,128]{3,2,1,0:T(8,128)(2,1)}), bf16[8,2,96,128]{3,2,1,0:T(8,128)(2,1)S(1)}, u32[]{:S(2)}, u32[]{:S(2)}) async-start(bf16[8,2,96,128]{3,2,1,0:T(8,128)(2,1)} %get-tuple-element.104), calls=%async_computation.1 | async-start | bytes 786432 | tf_op jit(solution)/shard_map/all_to_all | solution.py:1185
  82.9 9.8 %all-to-all-done.1.refs_1_ = bf16[8,2,96,128]{3,2,1,0:T(8,128)(2,1)S(1)} async-done(((bf16[8,2,96,128]{3,2,1,0:T(8,128)(2,1)}), bf16[8,2,96,128]{3,2,1,0:T(8,128)(2,1)S(1)}, u32[]{:S(2)}, u32[]{:S(2)}) %all-to-all-start.1) | async-done | bytes 393248 | tf_op jit(solution)/shard_map/all_to_all | solution.py:1185
  93.4 6.0 %wide_mixed.1 = (bf16[192,512]{1,0:T(8,128)(2,1)}, bf16[2,2,192,128]{3,2,1,0:T(8,128)(2,1)}, bf16[2,2,192,128]{3,2,1,0:T(8,128)(2,1)}) custom-call(s32[2,8]{1,0:T(2,128)} %fusion.1.refs_0_, bf16[8,2,96,128]{3,2,1,0:T(8,128)(2,1)} %copy-done.5, f32[128,384]{1,0:T(8,128)} %get-tuple-element.105.refs_2_.refs_9_, s32[2,128,128]{2,1,0:T(8,128)} %broadcast_in_dim.70.refs_3_, ...), custom_call_target="tpu_custom_call" | custom-call | flops 10000000 | bytes 1000000 | tf_op jit(solution)/shard_map/wide_mixed/pallas_call | solution.py:53
  101.6 3.8 %collective-permute-done.10.far = bf16[192,512]{1,0:T(8,128)(2,1)S(1)} collective-permute-done((bf16[192,512]{1,0:T(8,128)(2,1)}, bf16[192,512]{1,0:T(8,128)(2,1)S(1)}, u32[]{:S(2)}, u32[]{:S(2)}) %collective-permute-start.10) | collective-permute-done | bytes 196640 | tf_op jit(solution)/shard_map/ppermute | solution.py:1099
  107.8 7.4 %mlp_top.1 = (bf16[208,512]{1,0:T(8,128)(2,1)}, bf16[208,512]{1,0:T(8,128)(2,1)}, bf16[208,512]{1,0:T(8,128)(2,1)}, bf16[208,512]{1,0:T(8,128)(2,1)}, f32[8,512]...) custom-call(s32[2]{0:T(128)} %pad_add_fusion.me_ref.refs_0_, ...), custom_call_target="tpu_custom_call" | custom-call | flops 10000000 | bytes 1000000 | tf_op jit(solution)/shard_map/mlp_top/pallas_call | solution.py:950
  120.2 3.3 in_grad.2
  123.5 3.3 out_grad.2.refs_12_
  127.6 7.0 %wide_norm_back.1 = (bf16[8,2,96,128]{3,2,1,0:T(8,128)(2,1)}, bf16[2,2,192,128]{3,2,1,0:T(8,128)(2,1)}, f32[192,128]{1,0:T(8,128)}) custom-call(s32[2,8]{1,0:T(2,128)} %fusion.refs_0_, bf16[208,512]{1,0:T(8,128)(2,1)} %get-tuple-element.109.refs_1_, bf16[208,512]{1,0:T(8,128)(2,1)} %copy-done.28, bf16[208,512]{1,0:T(8,128)(2,1)} %copy-done.29, ...), custom_call_target="tpu_custom_call" | custom-call | flops 10000000 | bytes 1000000 | tf_op jit(solution)/shard_map/wide_norm_back/pallas_call | solution.py:53
  134.6 4.0 %all-to-all-start.2 = ((bf16[8,2,96,128]{3,2,1,0:T(8,128)(2,1)}), bf16[8,2,96,128]{3,2,1,0:T(8,128)(2,1)S(1)}, u32[]{:S(2)}, u32[]{:S(2)}) async-start(bf16[8,2,96,128]{3,2,1,0:T(8,128)(2,1)} %get-tuple-element.118.refs_0_), calls=%async_computation.2 | async-start | bytes 786432 | tf_op jit(solution)/shard_map/all_to_all | solution.py:1185
  140.1 3.3 mlp_out.1
  143.4 7.2 %all-to-all-done.2.refs_0_ = bf16[8,2,96,128]{3,2,1,0:T(8,128)(2,1)S(1)} async-done(((bf16[8,2,96,128]{3,2,1,0:T(8,128)(2,1)}), bf16[8,2,96,128]{3,2,1,0:T(8,128)(2,1)S(1)}, u32[]{:S(2)}, u32[]{:S(2)}) %all-to-all-start.2) | async-done | bytes 393248 | tf_op jit(solution)/shard_map/all_to_all | solution.py:1185
  151.3 4.0 %tall_back.1 = (f32[192,512]{1,0:T(8,128)}, bf16[192,512]{1,0:T(8,128)(2,1)}, f32[192,128]{1,0:T(8,128)}, bf16[192,512]{1,0:T(8,128)(2,1)}) custom-call(bf16[8,2,96,128]{3,2,1,0:T(8,128)(2,1)} %copy-done.7, f32[192,128]{1,0:T(8,128)} %get-tuple-element.103.refs_5_.refs_1_, s32[2,1,256]{2,1,0:T(1,128)} %broadcast_in_dim_reshape.7.refs_2_.refs_9_, ...), custom_call_target="tpu_custom_call" | custom-call | flops 10000000 | bytes 1000000 | tf_op jit(solution)/shard_map/tall_back/pallas_call | solution.py:53
  155.9 5.3 %collective-permute-done.22.grad_far.refs_4_ = bf16[192,512]{1,0:T(8,128)(2,1)S(1)} collective-permute-done((bf16[192,512]{1,0:T(8,128)(2,1)}, bf16[192,512]{1,0:T(8,128)(2,1)S(1)}, u32[]{:S(2)}, u32[]{:S(2)}) %collective-permute-start.22) | collective-permute-done | bytes 196640 | tf_op jit(solution)/shard_map/ppermute | solution.py:1099
  163.3 6.4 %mlp_back.1 = (bf16[208,512]{1,0:T(8,128)(2,1)}, bf16[208,512]{1,0:T(8,128)(2,1)}, bf16[208,512]{1,0:T(8,128)(2,1)}, bf16[208,512]{1,0:T(8,128)(2,1)}, bf16[768,512]{1,0:T(8,128)(2,1)}) custom-call(s32[2]{0:T(128)} %pad_add_fusion.me_ref.refs_0_, bf16[192,512]{1,0:T(8,128)(2,1)} %get-tuple-element.97.own.refs_3_, bf16[192,512]{1,0:T(8,128)(2,1)} %copy-done.16, ...), custom_call_target="tpu_custom_call" | custom-call | flops 10000000 | bytes 1000000 | tf_op jit(solution)/shard_map/mlp_back/pallas_call | solution.py:975
  170.8 3.4 out_grad.3
  178.3 6.0 %collective-permute-done.26.refs_2_ = bf16[208,512]{1,0:T(8,128)(2,1)S(1)} collective-permute-done((bf16[208,512]{1,0:T(8,128)(2,1)S(1)}, bf16[208,512]{1,0:T(8,128)(2,1)S(1)}, u32[]{:S(2)}, u32[]{:S(2)}) %collective-permute-start.26) | collective-permute-done | bytes 213024 | tf_op jit(solution)/shard_map/ppermute | solution.py:1109
  185.0 4.5 %tall_norm_back.1 = (bf16[8,2,96,128]{3,2,1,0:T(8,128)(2,1)}, bf16[192,512]{1,0:T(8,128)(2,1)}, f32[192,128]{1,0:T(8,128)}) custom-call(bf16[208,512]{1,0:T(8,128)(2,1)} %get-tuple-element.127.refs_0_, bf16[208,512]{1,0:T(8,128)(2,1)} %copy-done.25, bf16[208,512]{1,0:T(8,128)(2,1)} %copy-done.26, bf16[192,512]{1,0:T(8,128)(2,1)} %get-tuple-element.97.own.refs_3_, ...), custom_call_target="tpu_custom_call" | custom-call | flops 10000000 | bytes 1000000 | tf_op jit(solution)/shard_map/tall_norm_back/pallas_call | solution.py:53
  189.5 4.6 %collective-permute-done.27.refs_3_.refs_2_ = bf16[384,768]{1,0:T(8,128)(2,1)S(1)} collective-permute-done((bf16[384,768]{1,0:T(8,128)(2,1)}, bf16[384,768]{1,0:T(8,128)(2,1)S(1)}, u32[]{:S(2)}, u32[]{:S(2)}) %collective-permute-start.27) | collective-permute-done | bytes 589856 | tf_op jit(solution)/shard_map/ppermute | solution.py:1114
  194.9 3.6 in_grad.3
  200.2 5.8 %wide_kernel_grad.3.refs_1_ = f32[192,128]{1,0:T(8,128)} custom-call(s32[2,8]{1,0:T(2,128)} %fusion.1.refs_0_, bf16[2,2,192,128]{3,2,1,0:T(8,128)(2,1)} %get-tuple-element.148.refs_1_, bf16[2,2,192,128]{3,2,1,0:T(8,128)(2,1)} %get-tuple-element.149.refs_2_, s32[2,128,128]{2,1,0:T(8,128)} %broadcast_in_dim.70.refs_3_, ...), custom_call_target="tpu_custom_call" | custom-call | flops 10000000 | bytes 1000000 | tf_op jit(solution)/shard_map/wide_kernel_grad/pallas_call | solution.py:53
  206.0 5.7 %tall_kernel_grad.3.refs_0_ = f32[192,128]{1,0:T(8,128)} custom-call(bf16[192,512]{1,0:T(8,128)(2,1)} %get-tuple-element.146.refs_0_, bf16[192,512]{1,0:T(8,128)(2,1)} %get-tuple-element.147.refs_1_, s32[2,1,256]{2,1,0:T(1,128)} %broadcast_in_dim_reshape.6.refs_2_.refs_6_, bf16[8,2,96,128]{3,2,1,0:T(8,128)(2,1)} %get-tuple-element.135.refs_6_.refs_3_.refs_4_), custom_call_target="tpu_custom_call" | custom-call | flops 10000000 | bytes 1000000 | tf_op jit(solution)/shard_map/tall_kernel_grad/pallas_call | solution.py:53
  212.5 2.2 top_output.1
  217.2 5.4 %all-to-all-start.3 = ((bf16[8,2,96,128]{3,2,1,0:T(8,128)(2,1)}), bf16[8,2,96,128]{3,2,1,0:T(8,128)(2,1)S(1)}, u32[]{:S(2)}, u32[]{:S(2)}) async-start(bf16[8,2,96,128]{3,2,1,0:T(8,128)(2,1)} %get-tuple-element.135.refs_6_.refs_3_.refs_4_), calls=%async_computation.3 | async-start | bytes 786432 | tf_op jit(solution)/shard_map/all_to_all | solution.py:1185
  226.7 2.4 collective-permute-start.43
  230.3 13.1 %collective-permute-done.42 = bf16[96,768]{1,0:T(8,128)(2,1)S(1)} collective-permute-done((bf16[96,768]{1,0:T(8,128)(2,1)}, bf16[96,768]{1,0:T(8,128)(2,1)S(1)}, u32[]{:S(2)}, u32[]{:S(2)}) %collective-permute-start.42) | collective-permute-done | bytes 147488 | tf_op jit(solution)/shard_map/ppermute | solution.py:1114
  243.4 12.0 %collective-permute-done.43 = bf16[96,768]{1,0:T(8,128)(2,1)S(1)} collective-permute-done((bf16[96,768]{1,0:T(8,128)(2,1)}, bf16[96,768]{1,0:T(8,128)(2,1)S(1)}, u32[]{:S(2)}, u32[]{:S(2)}) %collective-permute-start.43) | collective-permute-done | bytes 147488 | tf_op jit(solution)/shard_map/ppermute | solution.py:1114
  257.1 14.5 %collective-permute-start.46 = (bf16[96,768]{1,0:T(8,128)(2,1)S(1)}, bf16[96,768]{1,0:T(8,128)(2,1)S(1)}, u32[]{:S(2)}, u32[]{:S(2)}) collective-permute-start(bf16[96,768]{1,0:T(8,128)(2,1)S(1)} %add_convert_fusion.4), channel_id=1, source_target_pairs={{0,16},{4,20},{8,24},{12,28},{16,0},{20,4},{24,8},{28,12},{1,17},{... | collective-permute-start | bytes 442376 | tf_op jit(solution)/shard_map/ppermute | solution.py:1114
  276.6 2.4 collective-permute-start.37
  281.0 5.7 %tall_kernel_grad.2.refs_0_ = f32[192,128]{1,0:T(8,128)} custom-call(bf16[192,512]{1,0:T(8,128)(2,1)} %get-tuple-element.138.refs_0_, bf16[192,512]{1,0:T(8,128)(2,1)} %get-tuple-element.139.refs_1_, s32[2,1,256]{2,1,0:T(1,128)} %broadcast_in_dim_reshape.6.refs_2_.refs_6_, bf16[8,2,96,128]{3,2,1,0:T(8,128)(2,1)} %get-tuple-element.135.refs_6_.refs_3_.refs_4_), custom_call_target="tpu_custom_call" | custom-call | flops 10000000 | bytes 1000000 | tf_op jit(solution)/shard_map/tall_kernel_grad/pallas_call | solution.py:53
  286.8 7.3 %collective-permute-done.46 = bf16[96,768]{1,0:T(8,128)(2,1)S(1)} collective-permute-done((bf16[96,768]{1,0:T(8,128)(2,1)S(1)}, bf16[96,768]{1,0:T(8,128)(2,1)S(1)}, u32[]{:S(2)}, u32[]{:S(2)}) %collective-permute-start.46) | collective-permute-done | bytes 147488 | tf_op jit(solution)/shard_map/ppermute | solution.py:1114
  295.5 6.0 %wide_back.1 = (bf16[2,2,192,128]{3,2,1,0:T(8,128)(2,1)}, bf16[2,2,192,128]{3,2,1,0:T(8,128)(2,1)}) custom-call(s32[2,8]{1,0:T(2,128)} %fusion.refs_0_, bf16[8,2,96,128]{3,2,1,0:T(8,128)(2,1)} %copy-done.6, f32[128,384]{1,0:T(8,128)} %s4_wide.1.refs_2_, s32[2,128,128]{2,1,0:T(8,128)} %broadcast_in_dim.76.refs_10_.refs_3_, ...), custom_call_target="tpu_custom_call" | custom-call | flops 10000000 | bytes 1000000 | tf_op jit(solution)/shard_map/wide_back/pallas_call | solution.py:53
  301.4 5.8 %wide_kernel_grad.2.refs_1_ = f32[192,128]{1,0:T(8,128)} custom-call(s32[2,8]{1,0:T(2,128)} %fusion.1.refs_0_, bf16[2,2,192,128]{3,2,1,0:T(8,128)(2,1)} %get-tuple-element.140.refs_1_, bf16[2,2,192,128]{3,2,1,0:T(8,128)(2,1)} %bitcast.77, s32[2,128,128]{2,1,0:T(8,128)} %broadcast_in_dim.70.refs_3_), custom_call_target="tpu_custom_call" | custom-call | flops 10000000 | bytes 1000000 | tf_op jit(solution)/shard_map/wide_kernel_grad/pallas_call | solution.py:53
  307.3 2.2 collect.2
  319.2 6.3 %s4_pullback.2 = (f32[2,2,192]{2,1,0:T(2,128)}, f32[2,2,64,192]{3,2,1,0:T(8,128)}, f32[2,2,64,192]{3,2,1,0:T(8,128)}, f32[2,2,64,192]{3,2,1,0:T(8,128)}, f32[2,2,64,192]{3,2,1,0:T(8,128)}, /*index=5*/f32[16,192]{1,0:T(8,128)}) custom-call(f32[192,256]{1,0:T(8,128)} %add.84.refs_0_, f32[2,2,192]{2,1,0:T(2,128)} %refs_1_.3, f32[2,2,64,192]{3,2,1,0:T(8,128)} %bitcast.59, ...), custom_call_target="tpu_custom_call" | custom-call | flops 50000000 | bytes 1000000 | tf_op jit(solution)/shard_map/s4_pullback/pallas_call | solution.py:307
  327.5 2.6 collective-permute-start.30
  331.0 4.1 %assemble.3 = f32[2,768,768]{2,1,0:T(8,128)} custom-call(s32[2]{0:T(128)} %pad_add_fusion.me_ref.refs_0_, bf16[384,768]{1,0:T(8,128)(2,1)} %copy-done, bf16[384,768]{1,0:T(8,128)(2,1)} %copy-done.22, bf16[768,768]{1,0:T(8,128)(2,1)} %get-tuple-element.184.top_ref), custom_call_target="tpu_custom_call" | custom-call | flops 1000000 | bytes 7000000 | tf_op jit(solution)/shard_map/assemble/pallas_call | solution.py:1174
  337.4 6.3 %s4_pullback.3 = (f32[2,2,192]{2,1,0:T(2,128)}, f32[2,2,64,192]{3,2,1,0:T(8,128)}, f32[2,2,64,192]{3,2,1,0:T(8,128)}, f32[2,2,64,192]{3,2,1,0:T(8,128)}, f32[2,2,64,192]{3,2,1,0:T(8,128)}, /*index=5*/f32[16,192]{1,0:T(8,128)}) custom-call(f32[192,256]{1,0:T(8,128)} %add.81.refs_0_, ...), custom_call_target="tpu_custom_call", output_to_operand_aliasing={{0}: (6, {}), {1}: (7, {}), {2}: (8, {}), {3}: (9, {}), {4}... | custom-call | flops 50000000 | bytes 1000000 | tf_op jit(solution)/shard_map/s4_pullback/pallas_call | solution.py:307
  348.9 4.1 %assemble.2 = f32[2,768,768]{2,1,0:T(8,128)} custom-call(s32[2]{0:T(128)} %pad_add_fusion.me_ref.refs_0_, bf16[384,768]{1,0:T(8,128)(2,1)} %copy-done.1, bf16[384,768]{1,0:T(8,128)(2,1)} %copy-done.23, bf16[768,768]{1,0:T(8,128)(2,1)} %get-tuple-element.183.refs_4_.top_ref), custom_call_target="tpu_custom_call" | custom-call | flops 1000000 | bytes 7000000 | tf_op jit(solution)/shard_map/assemble/pallas_call | solution.py:1174
  (250 shorter events, 81.9 us)
Async XLA Ops:
  19.5 19.0 %all-to-all-start = ((bf16[8,2,96,128]{3,2,1,0:T(8,128)(2,1)}), bf16[8,2,96,128]{3,2,1,0:T(8,128)(2,1)S(1)}, u32[]{:S(2)}, u32[]{:S(2)}) async-start(bf16[8,2,96,128]{3,2,1,0:T(8,128)(2,1)} %wide_forward.1.refs_7_), calls=%async_computation | async-start | bytes 786432 | tf_op jit(solution)/shard_map/all_to_all | solution.py:1185
  43.0 5.9 %collective-permute-start.1 = (bf16[192,512]{1,0:T(8,128)(2,1)}, bf16[192,512]{1,0:T(8,128)(2,1)S(1)}, u32[]{:S(2)}, u32[]{:S(2)}) collective-permute-start(bf16[192,512]{1,0:T(8,128)(2,1)} %get-tuple-element.97.own.refs_3_), channel_id=1, source_target_pairs={{0,2},{1,3},{2,0},{3,1},{4,6},{5,7},{6,4},{7,5},{8,10},{9,11},{10,... | collective-permute-start | bytes 589832 | tf_op jit(solution)/shard_map/ppermute | solution.py:1099
  44.6 5.3 %collective-permute-start.4 = (f32[192,4]{1,0:T(8,128)S(1)}, f32[192,4]{1,0:T(8,128)S(1)}, u32[]{:S(2)}, u32[]{:S(2)}) collective-permute-start(f32[192,4]{1,0:T(8,128)S(1)} %copy.73.shape_own), channel_id=1, source_target_pairs={{0,2},{1,3},{2,0},{3,1},{4,6},{5,7},{6,4},{7,5},{8,10},{9,11},{10,... | collective-permute-start | bytes 9224 | tf_op jit(solution)/shard_map/ppermute | solution.py:1099
  45.2 6.3 %collective-permute-start.3 = (f32[192,4]{1,0:T(8,128)S(1)}, f32[192,4]{1,0:T(8,128)S(1)}, u32[]{:S(2)}, u32[]{:S(2)}) collective-permute-start(f32[192,4]{1,0:T(8,128)S(1)} %copy.73.shape_own), channel_id=1, source_target_pairs={{0,1},{1,0},{2,3},{3,2},{4,5},{5,4},{6,7},{7,6},{8,9},{9,8},{10,11... | collective-permute-start | bytes 9224 | tf_op jit(solution)/shard_map/ppermute | solution.py:1100
  45.2 6.3 %collective-permute-start = (bf16[192,512]{1,0:T(8,128)(2,1)}, bf16[192,512]{1,0:T(8,128)(2,1)S(1)}, u32[]{:S(2)}, u32[]{:S(2)}) collective-permute-start(bf16[192,512]{1,0:T(8,128)(2,1)} %get-tuple-element.97.own.refs_3_), channel_id=1, source_target_pairs={{0,1},{1,0},{2,3},{3,2},{4,5},{5,4},{6,7},{7,6},{8,9},{9,8},{10,11... | collective-permute-start | bytes 589832 | tf_op jit(solution)/shard_map/ppermute | solution.py:1100
  60.4 3.9 %collective-permute-start.6 = (bf16[192,512]{1,0:T(8,128)(2,1)}, bf16[192,512]{1,0:T(8,128)(2,1)S(1)}, u32[]{:S(2)}, u32[]{:S(2)}) collective-permute-start(bf16[192,512]{1,0:T(8,128)(2,1)} %get-tuple-element.99), channel_id=1, source_target_pairs={{0,1},{1,0},{2,3},{3,2},{4,5},{5,4},{6,7},{7,6},{8,9},{9,8},{10,11... | collective-permute-start | bytes 589832 | tf_op jit(solution)/shard_map/ppermute | solution.py:1107
  62.8 7.2 %collective-permute-start.8 = (bf16[192,512]{1,0:T(8,128)(2,1)S(1)}, bf16[192,512]{1,0:T(8,128)(2,1)S(1)}, u32[]{:S(2)}, u32[]{:S(2)}) collective-permute-start(bf16[192,512]{1,0:T(8,128)(2,1)S(1)} %add_convert_fusion.3), channel_id=1, source_target_pairs={{0,2},{1,3},{2,0},{3,1},{4,6},{5,7},{6,4},{7,5},{8,10},{9,11},{10,... | collective-permute-start | bytes 589832 | tf_op jit(solution)/shard_map/ppermute | solution.py:1109
  75.6 17.1 %all-to-all-start.1 = ((bf16[8,2,96,128]{3,2,1,0:T(8,128)(2,1)}), bf16[8,2,96,128]{3,2,1,0:T(8,128)(2,1)S(1)}, u32[]{:S(2)}, u32[]{:S(2)}) async-start(bf16[8,2,96,128]{3,2,1,0:T(8,128)(2,1)} %get-tuple-element.104), calls=%async_computation.1 | async-start | bytes 786432 | tf_op jit(solution)/shard_map/all_to_all | solution.py:1185
  81.3 19.7 %collective-permute-start.13 = (bf16[192,512]{1,0:T(8,128)(2,1)S(1)}, bf16[192,512]{1,0:T(8,128)(2,1)S(1)}, u32[]{:S(2)}, u32[]{:S(2)}) collective-permute-start(bf16[192,512]{1,0:T(8,128)(2,1)S(1)} %copy-done.11), channel_id=1, source_target_pairs={{0,2},{1,3},{2,0},{3,1},{4,6},{5,7},{6,4},{7,5},{8,10},{9,11},{10,... | collective-permute-start | bytes 589832 | tf_op jit(solution)/shard_map/ppermute | solution.py:1099
  99.5 5.9 %collective-permute-start.10 = (bf16[192,512]{1,0:T(8,128)(2,1)}, bf16[192,512]{1,0:T(8,128)(2,1)S(1)}, u32[]{:S(2)}, u32[]{:S(2)}) collective-permute-start(bf16[192,512]{1,0:T(8,128)(2,1)} %get-tuple-element.106.own.refs_4_), channel_id=1, source_target_pairs={{0,2},{1,3},{2,0},{3,1},{4,6},{5,7},{6,4},{7,5},{8,10},{9,11},{10,... | collective-permute-start | bytes 589832 | tf_op jit(solution)/shard_map/ppermute | solution.py:1099
  101.0 5.3 %collective-permute-start.12 = (bf16[192,512]{1,0:T(8,128)(2,1)S(1)}, bf16[192,512]{1,0:T(8,128)(2,1)S(1)}, u32[]{:S(2)}, u32[]{:S(2)}) collective-permute-start(bf16[192,512]{1,0:T(8,128)(2,1)S(1)} %copy-done.11), channel_id=1, source_target_pairs={{0,1},{1,0},{2,3},{3,2},{4,5},{5,4},{6,7},{7,6},{8,9},{9,8},{10,11... | collective-permute-start | bytes 589832 | tf_op jit(solution)/shard_map/ppermute | solution.py:1100
  101.0 5.3 %collective-permute-start.14 = (bf16[192,512]{1,0:T(8,128)(2,1)S(1)}, bf16[192,512]{1,0:T(8,128)(2,1)S(1)}, u32[]{:S(2)}, u32[]{:S(2)}) collective-permute-start(bf16[192,512]{1,0:T(8,128)(2,1)S(1)} %collective-permute-done.13.grad_far.refs_4_), channel_id=1, source_target_pairs={{0,1},{1,0},{2,3},{3,2},{4,5},{5,4},{6,7},{7,6},{8,9},{9,8},{10,11... | collective-permute-start | bytes 589832 | tf_op jit(solution)/shard_map/ppermute | solution.py:1101
  101.5 4.8 %collective-permute-start.9 = (bf16[192,512]{1,0:T(8,128)(2,1)}, bf16[192,512]{1,0:T(8,128)(2,1)S(1)}, u32[]{:S(2)}, u32[]{:S(2)}) collective-permute-start(bf16[192,512]{1,0:T(8,128)(2,1)} %get-tuple-element.106.own.refs_4_), channel_id=1, source_target_pairs={{0,1},{1,0},{2,3},{3,2},{4,5},{5,4},{6,7},{7,6},{8,9},{9,8},{10,11... | collective-permute-start | bytes 589832 | tf_op jit(solution)/shard_map/ppermute | solution.py:1100
  115.8 11.0 %collective-permute-start.15 = (bf16[208,512]{1,0:T(8,128)(2,1)}, bf16[208,512]{1,0:T(8,128)(2,1)S(1)}, u32[]{:S(2)}, u32[]{:S(2)}) collective-permute-start(bf16[208,512]{1,0:T(8,128)(2,1)} %get-tuple-element.110), channel_id=1, source_target_pairs={{0,1},{1,0},{2,3},{3,2},{4,5},{5,4},{6,7},{7,6},{8,9},{9,8},{10,11... | collective-permute-start | bytes 638984 | tf_op jit(solution)/shard_map/ppermute | solution.py:1107
  118.1 8.8 %collective-permute-start.17 = (bf16[208,512]{1,0:T(8,128)(2,1)S(1)}, bf16[208,512]{1,0:T(8,128)(2,1)S(1)}, u32[]{:S(2)}, u32[]{:S(2)}) collective-permute-start(bf16[208,512]{1,0:T(8,128)(2,1)S(1)} %add_convert_fusion.1), channel_id=1, source_target_pairs={{0,2},{1,3},{2,0},{3,1},{4,6},{5,7},{6,4},{7,5},{8,10},{9,11},{10,... | collective-permute-start | bytes 638984 | tf_op jit(solution)/shard_map/ppermute | solution.py:1109
  134.6 16.0 %all-to-all-start.2 = ((bf16[8,2,96,128]{3,2,1,0:T(8,128)(2,1)}), bf16[8,2,96,128]{3,2,1,0:T(8,128)(2,1)S(1)}, u32[]{:S(2)}, u32[]{:S(2)}) async-start(bf16[8,2,96,128]{3,2,1,0:T(8,128)(2,1)} %get-tuple-element.118.refs_0_), calls=%async_computation.2 | async-start | bytes 786432 | tf_op jit(solution)/shard_map/all_to_all | solution.py:1185
  138.7 156.0 %all-reduce.3.cloned.1.call-start = ((), (), s32[]{:S(2)}) async-start(), calls=%async_computation.4 | async-start | bytes 4718592 | tf_op jit(solution)/shard_map/psum | solution.py:1298
  155.3 5.9 %collective-permute-start.22 = (bf16[192,512]{1,0:T(8,128)(2,1)}, bf16[192,512]{1,0:T(8,128)(2,1)S(1)}, u32[]{:S(2)}, u32[]{:S(2)}) collective-permute-start(bf16[192,512]{1,0:T(8,128)(2,1)} %get-tuple-element.124.grad_own.refs_2_), channel_id=1, source_target_pairs={{0,2},{1,3},{2,0},{3,1},{4,6},{5,7},{6,4},{7,5},{8,10},{9,11},{10,... | collective-permute-start | bytes 589832 | tf_op jit(solution)/shard_map/ppermute | solution.py:1099
  155.9 5.3 %collective-permute-start.21 = (bf16[192,512]{1,0:T(8,128)(2,1)}, bf16[192,512]{1,0:T(8,128)(2,1)S(1)}, u32[]{:S(2)}, u32[]{:S(2)}) collective-permute-start(bf16[192,512]{1,0:T(8,128)(2,1)} %get-tuple-element.124.grad_own.refs_2_), channel_id=1, source_target_pairs={{0,1},{1,0},{2,3},{3,2},{4,5},{5,4},{6,7},{7,6},{8,9},{9,8},{10,11... | collective-permute-start | bytes 589832 | tf_op jit(solution)/shard_map/ppermute | solution.py:1100
  169.7 6.3 %collective-permute-start.25 = (bf16[208,512]{1,0:T(8,128)(2,1)}, bf16[208,512]{1,0:T(8,128)(2,1)S(1)}, u32[]{:S(2)}, u32[]{:S(2)}) collective-permute-start(bf16[208,512]{1,0:T(8,128)(2,1)} %get-tuple-element.130), channel_id=1, source_target_pairs={{0,1},{1,0},{2,3},{3,2},{4,5},{5,4},{6,7},{7,6},{8,9},{9,8},{10,11... | collective-permute-start | bytes 638984 | tf_op jit(solution)/shard_map/ppermute | solution.py:1106
  169.9 7.1 %collective-permute-start.19 = (bf16[192,512]{1,0:T(8,128)(2,1)S(1)}, bf16[192,512]{1,0:T(8,128)(2,1)S(1)}, u32[]{:S(2)}, u32[]{:S(2)}) collective-permute-start(bf16[192,512]{1,0:T(8,128)(2,1)S(1)} %copy-done.33), channel_id=1, source_target_pairs={{0,1},{1,0},{2,3},{3,2},{4,5},{5,4},{6,7},{7,6},{8,9},{9,8},{10,11... | collective-permute-start | bytes 589832 | tf_op jit(solution)/shard_map/ppermute | solution.py:1106
  170.3 41.4 %collective-permute-start.18 = (bf16[192,512]{1,0:T(8,128)(2,1)S(1)}, bf16[192,512]{1,0:T(8,128)(2,1)S(1)}, u32[]{:S(2)}, u32[]{:S(2)}) collective-permute-start(bf16[192,512]{1,0:T(8,128)(2,1)S(1)} %copy-done.47), channel_id=1, source_target_pairs={{0,1},{1,0},{2,3},{3,2},{4,5},{5,4},{6,7},{7,6},{8,9},{9,8},{10,11... | collective-permute-start | bytes 589832 | tf_op jit(solution)/shard_map/ppermute | solution.py:1107
  170.4 7.9 %collective-permute-start.24 = (bf16[208,512]{1,0:T(8,128)(2,1)}, bf16[208,512]{1,0:T(8,128)(2,1)S(1)}, u32[]{:S(2)}, u32[]{:S(2)}) collective-permute-start(bf16[208,512]{1,0:T(8,128)(2,1)} %get-tuple-element.128), channel_id=1, source_target_pairs={{0,1},{1,0},{2,3},{3,2},{4,5},{5,4},{6,7},{7,6},{8,9},{9,8},{10,11... | collective-permute-start | bytes 638984 | tf_op jit(solution)/shard_map/ppermute | solution.py:1107
  174.3 19.8 %collective-permute-start.27 = (bf16[384,768]{1,0:T(8,128)(2,1)}, bf16[384,768]{1,0:T(8,128)(2,1)S(1)}, u32[]{:S(2)}, u32[]{:S(2)}) collective-permute-start(bf16[384,768]{1,0:T(8,128)(2,1)} %get-tuple-element.134.refs_10_), channel_id=1, source_target_pairs={{0,4},{4,0},{8,12},{12,8},{16,20},{20,16},{24,28},{28,24},{1,5},{5... | collective-permute-start | bytes 1769480 | tf_op jit(solution)/shard_map/ppermute | solution.py:1114
  176.1 8.2 %collective-permute-start.26 = (bf16[208,512]{1,0:T(8,128)(2,1)S(1)}, bf16[208,512]{1,0:T(8,128)(2,1)S(1)}, u32[]{:S(2)}, u32[]{:S(2)}) collective-permute-start(bf16[208,512]{1,0:T(8,128)(2,1)S(1)} %add_convert_fusion), channel_id=1, source_target_pairs={{0,2},{1,3},{2,0},{3,1},{4,6},{5,7},{6,4},{7,5},{8,10},{9,11},{10,... | collective-permute-start | bytes 638984 | tf_op jit(solution)/shard_map/ppermute | solution.py:1109
  177.1 34.7 %collective-permute-start.20 = (bf16[192,512]{1,0:T(8,128)(2,1)S(1)}, bf16[192,512]{1,0:T(8,128)(2,1)S(1)}, u32[]{:S(2)}, u32[]{:S(2)}) collective-permute-start(bf16[192,512]{1,0:T(8,128)(2,1)S(1)} %add_convert_fusion.2), channel_id=1, source_target_pairs={{0,2},{1,3},{2,0},{3,1},{4,6},{5,7},{6,4},{7,5},{8,10},{9,11},{10,... | collective-permute-start | bytes 589832 | tf_op jit(solution)/shard_map/ppermute | solution.py:1109
  198.5 73.1 %collective-permute-start.34 = (bf16[384,768]{1,0:T(8,128)(2,1)}, bf16[384,768]{1,0:T(8,128)(2,1)S(1)}, u32[]{:S(2)}, u32[]{:S(2)}) collective-permute-start(bf16[384,768]{1,0:T(8,128)(2,1)} %get-tuple-element.167), channel_id=1, source_target_pairs={{0,4},{4,0},{8,12},{12,8},{16,20},{20,16},{24,28},{28,24},{1,5},{5... | collective-permute-start | bytes 1769480 | tf_op jit(solution)/shard_map/ppermute | solution.py:1114
  216.9 12.2 %collective-permute-start.31 = (f32[192,256]{1,0:T(8,128)}, f32[192,256]{1,0:T(8,128)S(1)}, u32[]{:S(2)}, u32[]{:S(2)}) collective-permute-start(f32[192,256]{1,0:T(8,128)} %collect.3), channel_id=1, source_target_pairs={{0,4},{4,0},{8,12},{12,8},{16,20},{20,16},{24,28},{28,24},{1,5},{5... | collective-permute-start | bytes 589832 | tf_op jit(solution)/shard_map/ppermute | solution.py:1114
  217.2 77.4 %all-to-all-start.3 = ((bf16[8,2,96,128]{3,2,1,0:T(8,128)(2,1)}), bf16[8,2,96,128]{3,2,1,0:T(8,128)(2,1)S(1)}, u32[]{:S(2)}, u32[]{:S(2)}) async-start(bf16[8,2,96,128]{3,2,1,0:T(8,128)(2,1)} %get-tuple-element.135.refs_6_.refs_3_.refs_4_), calls=%async_computation.3 | async-start | bytes 786432 | tf_op jit(solution)/shard_map/all_to_all | solution.py:1185
  224.7 18.7 %collective-permute-start.42 = (bf16[96,768]{1,0:T(8,128)(2,1)}, bf16[96,768]{1,0:T(8,128)(2,1)S(1)}, u32[]{:S(2)}, u32[]{:S(2)}) collective-permute-start(bf16[96,768]{1,0:T(8,128)(2,1)} %get-tuple-element.174), channel_id=1, source_target_pairs={{0,8},{4,12},{8,0},{12,4},{16,24},{20,28},{24,16},{28,20},{1,9},{5... | collective-permute-start | bytes 442376 | tf_op jit(solution)/shard_map/ppermute | solution.py:1114
  226.7 28.7 %collective-permute-start.43 = (bf16[96,768]{1,0:T(8,128)(2,1)}, bf16[96,768]{1,0:T(8,128)(2,1)S(1)}, u32[]{:S(2)}, u32[]{:S(2)}) collective-permute-start(bf16[96,768]{1,0:T(8,128)(2,1)} %get-tuple-element.175), channel_id=1, source_target_pairs={{0,16},{4,20},{8,24},{12,28},{16,0},{20,4},{24,8},{28,12},{1,17},{... | collective-permute-start | bytes 442376 | tf_op jit(solution)/shard_map/ppermute | solution.py:1114
  229.1 26.3 %collective-permute-start.44 = (bf16[96,768]{1,0:T(8,128)(2,1)}, bf16[96,768]{1,0:T(8,128)(2,1)S(1)}, u32[]{:S(2)}, u32[]{:S(2)}) collective-permute-start(bf16[96,768]{1,0:T(8,128)(2,1)} %get-tuple-element.176), channel_id=1, source_target_pairs={{0,24},{4,28},{8,16},{12,20},{16,8},{20,12},{24,0},{28,4},{1,25},{... | collective-permute-start | bytes 442376 | tf_op jit(solution)/shard_map/ppermute | solution.py:1114
  229.2 47.4 %collective-permute-start.32 = (f32[192,256]{1,0:T(8,128)S(1)}, f32[192,256]{1,0:T(8,128)S(1)}, u32[]{:S(2)}, u32[]{:S(2)}) collective-permute-start(f32[192,256]{1,0:T(8,128)S(1)} %add.82), channel_id=1, source_target_pairs={{0,8},{4,12},{8,0},{12,4},{16,24},{20,28},{24,16},{28,20},{1,9},{5... | collective-permute-start | bytes 589832 | tf_op jit(solution)/shard_map/ppermute | solution.py:1114
  256.4 20.2 %collective-permute-start.47 = (bf16[96,768]{1,0:T(8,128)(2,1)S(1)}, bf16[96,768]{1,0:T(8,128)(2,1)S(1)}, u32[]{:S(2)}, u32[]{:S(2)}) collective-permute-start(bf16[96,768]{1,0:T(8,128)(2,1)S(1)} %add_convert_fusion.4), channel_id=1, source_target_pairs={{0,24},{4,28},{8,16},{12,20},{16,8},{20,12},{24,0},{28,4},{1,25},{... | collective-permute-start | bytes 442376 | tf_op jit(solution)/shard_map/ppermute | solution.py:1114
  257.1 37.0 %collective-permute-start.46 = (bf16[96,768]{1,0:T(8,128)(2,1)S(1)}, bf16[96,768]{1,0:T(8,128)(2,1)S(1)}, u32[]{:S(2)}, u32[]{:S(2)}) collective-permute-start(bf16[96,768]{1,0:T(8,128)(2,1)S(1)} %add_convert_fusion.4), channel_id=1, source_target_pairs={{0,16},{4,20},{8,24},{12,28},{16,0},{20,4},{24,8},{28,12},{1,17},{... | collective-permute-start | bytes 442376 | tf_op jit(solution)/shard_map/ppermute | solution.py:1114
  271.6 22.8 %collective-permute-start.45 = (bf16[96,768]{1,0:T(8,128)(2,1)S(1)}, bf16[96,768]{1,0:T(8,128)(2,1)S(1)}, u32[]{:S(2)}, u32[]{:S(2)}) collective-permute-start(bf16[96,768]{1,0:T(8,128)(2,1)S(1)} %add_convert_fusion.4), channel_id=1, source_target_pairs={{0,8},{4,12},{8,0},{12,4},{16,24},{20,28},{24,16},{28,20},{1,9},{5... | collective-permute-start | bytes 442376 | tf_op jit(solution)/shard_map/ppermute | solution.py:1114
  274.6 34.9 %collective-permute-start.35 = (bf16[96,768]{1,0:T(8,128)(2,1)}, bf16[96,768]{1,0:T(8,128)(2,1)S(1)}, u32[]{:S(2)}, u32[]{:S(2)}) collective-permute-start(bf16[96,768]{1,0:T(8,128)(2,1)} %get-tuple-element.169), channel_id=1, source_target_pairs={{0,8},{4,12},{8,0},{12,4},{16,24},{20,28},{24,16},{28,20},{1,9},{5... | collective-permute-start | bytes 442376 | tf_op jit(solution)/shard_map/ppermute | solution.py:1114
  276.6 34.8 %collective-permute-start.36 = (bf16[96,768]{1,0:T(8,128)(2,1)}, bf16[96,768]{1,0:T(8,128)(2,1)S(1)}, u32[]{:S(2)}, u32[]{:S(2)}) collective-permute-start(bf16[96,768]{1,0:T(8,128)(2,1)} %get-tuple-element.170), channel_id=1, source_target_pairs={{0,16},{4,20},{8,24},{12,28},{16,0},{20,4},{24,8},{28,12},{1,17},{... | collective-permute-start | bytes 442376 | tf_op jit(solution)/shard_map/ppermute | solution.py:1114
  276.6 34.8 %collective-permute-start.37 = (bf16[96,768]{1,0:T(8,128)(2,1)}, bf16[96,768]{1,0:T(8,128)(2,1)S(1)}, u32[]{:S(2)}, u32[]{:S(2)}) collective-permute-start(bf16[96,768]{1,0:T(8,128)(2,1)} %get-tuple-element.171), channel_id=1, source_target_pairs={{0,24},{4,28},{8,16},{12,20},{16,8},{20,12},{24,0},{28,4},{1,25},{... | collective-permute-start | bytes 442376 | tf_op jit(solution)/shard_map/ppermute | solution.py:1114
  294.1 24.4 %collective-permute-start.33 = (f32[192,256]{1,0:T(8,128)S(1)}, f32[192,256]{1,0:T(8,128)S(1)}, u32[]{:S(2)}, u32[]{:S(2)}) collective-permute-start(f32[192,256]{1,0:T(8,128)S(1)} %add.83), channel_id=1, source_target_pairs={{0,16},{4,20},{8,24},{12,28},{16,0},{20,4},{24,8},{28,12},{1,17},{... | collective-permute-start | bytes 589832 | tf_op jit(solution)/shard_map/ppermute | solution.py:1114
  294.5 35.7 %collective-permute-start.48 = (bf16[384,768]{1,0:T(8,128)(2,1)S(1)}, bf16[384,768]{1,0:T(8,128)(2,1)S(1)}, u32[]{:S(2)}, u32[]{:S(2)}) collective-permute-start(bf16[384,768]{1,0:T(8,128)(2,1)S(1)} %pad_maximum_fusion.1.half_ref), channel_id=1, source_target_pairs={{0,4},{4,0},{8,12},{12,8},{16,20},{20,16},{24,28},{28,24},{1,5},{5... | collective-permute-start | bytes 1769480 | tf_op jit(solution)/shard_map/ppermute | solution.py:1114
  309.5 5.9 %collective-permute-start.28 = (f32[192,256]{1,0:T(8,128)}, f32[192,256]{1,0:T(8,128)S(1)}, u32[]{:S(2)}, u32[]{:S(2)}) collective-permute-start(f32[192,256]{1,0:T(8,128)} %collect.2), channel_id=1, source_target_pairs={{0,4},{4,0},{8,12},{12,8},{16,20},{20,16},{24,28},{28,24},{1,5},{5... | collective-permute-start | bytes 589832 | tf_op jit(solution)/shard_map/ppermute | solution.py:1114
  311.5 14.1 %collective-permute-start.40 = (bf16[96,768]{1,0:T(8,128)(2,1)S(1)}, bf16[96,768]{1,0:T(8,128)(2,1)S(1)}, u32[]{:S(2)}, u32[]{:S(2)}) collective-permute-start(bf16[96,768]{1,0:T(8,128)(2,1)S(1)} %add_convert_fusion.5), channel_id=1, source_target_pairs={{0,24},{4,28},{8,16},{12,20},{16,8},{20,12},{24,0},{28,4},{1,25},{... | collective-permute-start | bytes 442376 | tf_op jit(solution)/shard_map/ppermute | solution.py:1114
  313.3 12.2 %collective-permute-start.39 = (bf16[96,768]{1,0:T(8,128)(2,1)S(1)}, bf16[96,768]{1,0:T(8,128)(2,1)S(1)}, u32[]{:S(2)}, u32[]{:S(2)}) collective-permute-start(bf16[96,768]{1,0:T(8,128)(2,1)S(1)} %add_convert_fusion.5), channel_id=1, source_target_pairs={{0,16},{4,20},{8,24},{12,28},{16,0},{20,4},{24,8},{28,12},{1,17},{... | collective-permute-start | bytes 442376 | tf_op jit(solution)/shard_map/ppermute | solution.py:1114
  315.4 10.2 %collective-permute-start.38 = (bf16[96,768]{1,0:T(8,128)(2,1)S(1)}, bf16[96,768]{1,0:T(8,128)(2,1)S(1)}, u32[]{:S(2)}, u32[]{:S(2)}) collective-permute-start(bf16[96,768]{1,0:T(8,128)(2,1)S(1)} %add_convert_fusion.5), channel_id=1, source_target_pairs={{0,8},{4,12},{8,0},{12,4},{16,24},{20,28},{24,16},{28,20},{1,9},{5... | collective-permute-start | bytes 442376 | tf_op jit(solution)/shard_map/ppermute | solution.py:1114
  318.4 9.1 %collective-permute-start.29 = (f32[192,256]{1,0:T(8,128)S(1)}, f32[192,256]{1,0:T(8,128)S(1)}, u32[]{:S(2)}, u32[]{:S(2)}) collective-permute-start(f32[192,256]{1,0:T(8,128)S(1)} %add.79), channel_id=1, source_target_pairs={{0,8},{4,12},{8,0},{12,4},{16,24},{20,28},{24,16},{28,20},{1,9},{5... | collective-permute-start | bytes 589832 | tf_op jit(solution)/shard_map/ppermute | solution.py:1114
  325.6 22.4 %collective-permute-start.41 = (bf16[384,768]{1,0:T(8,128)(2,1)S(1)}, bf16[384,768]{1,0:T(8,128)(2,1)S(1)}, u32[]{:S(2)}, u32[]{:S(2)}) collective-permute-start(bf16[384,768]{1,0:T(8,128)(2,1)S(1)} %pad_maximum_fusion.half_ref), channel_id=1, source_target_pairs={{0,4},{4,0},{8,12},{12,8},{16,20},{20,16},{24,28},{28,24},{1,5},{5... | collective-permute-start | bytes 1769480 | tf_op jit(solution)/shard_map/ppermute | solution.py:1114
  327.5 9.1 %collective-permute-start.30 = (f32[192,256]{1,0:T(8,128)S(1)}, f32[192,256]{1,0:T(8,128)S(1)}, u32[]{:S(2)}, u32[]{:S(2)}) collective-permute-start(f32[192,256]{1,0:T(8,128)S(1)} %add.80), channel_id=1, source_target_pairs={{0,16},{4,20},{8,24},{12,28},{16,0},{20,4},{24,8},{28,12},{1,17},{... | collective-permute-start | bytes 589832 | tf_op jit(solution)/shard_map/ppermute | solution.py:1114
  (55 other events, 263.9 us)
Sparse Core Ops, SparseCore 0:
  143.7 140.3 all-reduce.2
